TPU v7x, 128 devices: a whole 4x4x4 slice. The times are simulated.
128 devices in a mesh: row: 32 (over z, y, core), col: 4 (over x).
Axes of the slice: x: 4, y: 4, z: 4, core: 2. Of those that a mesh axis runs over, the one named last changes fastest.
Arguments:
- blocks: bfloat16 [4, 32, 128, 32, 4, 128], P(None, 'row', None, None, 'col'), may hold values from -5 to 5, as said below
- scales: float32 [4, 32, 32, 4], P(None, 'row', None, 'col'), may hold values from 0 to 3, as said below
Outputs:
- factored: bfloat16 [4, 32, 128, 32, 4, 128], P(None, 'row', None, None, 'col')
- block_scales: float32 [4, 32, 32, 4], P(None, 'row', None, 'col')
Inputs may be any that keep to these rules, and one draw needn't show every extreme that they name: blocks times scales form a symmetric positive definite matrix; scales of block (I, J) and (J, I) are equal, and so are the blocks up to transposition. `scales`: positive.
All inputs are finite; a program needn't handle non-finite values. Where the computation divides by a largest or mean magnitude, that divisor is 1e-20 or more.
Results may differ from a plain program's by a relative error of at most 0.0044.
Values may be sent and summed in bfloat16 or wider, within the bound.
No kernel may reach another device: no remote copies, remote signals or barrier semaphores. Data moves between devices by JAX's collectives and lax.ppermute only.
A program may use at most 128 MiB of HBM per device.

v0:
```python
import jax
import jax.numpy as jnp
from jax import lax
from jax.sharding import PartitionSpec as P


def from_root(array, axis, root):
    mine = lax.axis_index(axis) == root
    return lax.psum(jnp.where(mine, array, jnp.zeros_like(array)), axis)


def on_device(blocks, scales):
    row_count = lax.axis_size("row")
    col_count = lax.axis_size("col")
    row_index = lax.axis_index("row")
    col_index = lax.axis_index("col")
    block_rows = blocks.shape[0]
    block_size = blocks.shape[2]
    block_cols = blocks.shape[3]
    matrix = (blocks.astype(jnp.float32) * scales[:, :, None, :, :, None]).reshape(
        block_rows, block_size, block_cols, block_size
    )
    global_rows = jnp.arange(block_rows) * row_count + row_index
    global_cols = jnp.arange(block_cols) * col_count + col_index

    def factor_panel(current, panel):
        diag_here = current[0, :, 0, :]
        diag_block = from_root(diag_here, "row", panel)
        factor = jnp.linalg.cholesky(diag_block)
        column = current[:, :, 0, :].reshape(block_rows * block_size, block_size)
        solved = lax.linalg.triangular_solve(
            factor, column, left_side=False, lower=True, transpose_a=True
        )
        solved = solved.reshape(block_rows, block_size, block_size)
        below_mask = (global_rows > panel)[:, None, None]
        strip = jnp.where(below_mask, solved, 0.0).astype(jnp.bfloat16)
        row_strip = from_root(strip, "col", panel)
        return (factor, row_strip)

    def columns_of(row_strip):
        width = row_strip.shape[2]
        whole = lax.all_gather(row_strip[:, None], "row", axis=1, tiled=True)
        whole = whole.reshape(block_cols, col_count, block_size, width)
        return lax.dynamic_index_in_dim(whole, col_index, 1, keepdims=False)

    def update(current, row_strip, col_strip):
        width = row_strip.shape[2]
        product = jnp.einsum(
            "ik,jk->ij",
            row_strip.reshape(block_rows * block_size, width),
            col_strip.reshape(block_cols * block_size, width),
            preferred_element_type=jnp.float32,
        )
        return current - product.reshape(block_rows, block_size, block_cols, block_size)

    factor_zero, rows_zero = factor_panel(matrix, 0)
    cols_zero = columns_of(rows_zero)
    matrix = update(matrix, rows_zero, cols_zero)
    factor_one, rows_one = factor_panel(matrix, 1)
    cols_one = columns_of(rows_one)
    matrix = update(matrix, rows_one, cols_one)
    for panel, factor, row_strip, col_strip in (
        (0, factor_zero, rows_zero, cols_zero),
        (1, factor_one, rows_one, cols_one),
    ):
        lower_part = (global_rows > panel)[:, None, None, None] & (global_cols == panel)[
            None, None, :, None
        ]
        matrix = jnp.where(lower_part, row_strip.astype(jnp.float32)[:, :, None, :], matrix)
        diag_part = (global_rows == panel)[:, None, None, None] & (global_cols == panel)[
            None, None, :, None
        ]
        matrix = jnp.where(diag_part, factor[None, :, None, :], matrix)
        upper_part = (global_rows == panel)[:, None, None, None] & (global_cols > panel)[
            None, None, :, None
        ]
        matrix = jnp.where(
            upper_part, jnp.transpose(col_strip, (2, 0, 1)).astype(jnp.float32)[None], matrix
        )
    largest = jnp.max(jnp.abs(matrix), axis=(1, 3)) + 1e-06
    factored = (matrix / largest[:, None, :, None]).astype(jnp.bfloat16)
    factored = factored.reshape(block_rows, 1, block_size, block_cols, 1, block_size)
    return (factored, largest.reshape(block_rows, 1, block_cols, 1))


def solution(mesh):
    in_specs = (P(None, "row", None, None, "col", None), P(None, "row", None, "col"))
    out_specs = (P(None, "row", None, None, "col", None), P(None, "row", None, "col"))
    return jax.shard_map(
        on_device, mesh=mesh, in_specs=in_specs, out_specs=out_specs, check_vma=False
    )
```

profile of v0, /device:TPU:1, one launch (start us, length us, event | category | flops | bytes accessed | tf_op | source)
XLA Modules:
  0.0 480.1 jit_solution(17630116137620809229)
XLA Ops:
  7.2 7.8 %copy.18 = bf16[4,1,128,32,1,128]{2,5,3,0,4,1:T(8,128)(2,1)} copy(bf16[4,1,128,32,1,128]{5,3,4,2,1,0:T(8,128)(2,1)} %param.5) | data formatting | bytes 8388608 | tf_op args[0]
  15.1 2.8 multiply_bitcast_fusion
  17.9 3.2 copy-done.1
  21.8 1.0 slice.23
  22.9 97.9 %all-reduce.5.cloned.1.call-done = f32[128,128]{0,1:T(8,128)} async-done(((f32[128,128]{0,1:T(8,128)}), f32[128,128]{0,1:T(8,128)}) %all-reduce.5.cloned.1.call-update) | async-done | bytes 65552 | tf_op jit(solution)/shard_map/psum | solution.py:9
  120.8 0.9 copy.19
  121.8 0.9 fusion.14
  122.6 11.7 %cholesky.44 = f32[128,128]{1,0:T(8,128)S(1)} custom-call(f32[128,128]{1,0:T(8,128)S(1)} %fusion.14), custom_call_target="Cholesky" | custom-call | tf_op jit(solution)/shard_map/jit(cholesky)/cholesky | solution.py:29
  134.4 0.6 compare_reduce_fusion.1
  135.0 0.7 fusion.18
  135.7 9.8 %custom-call.6 = f32[1,128,128]{1,2,0:T(8,128)S(1)} custom-call(f32[1,128,128]{2,1,0:T(8,128)S(1)} %get-tuple-element.10), custom_call_target="InvertDiagBlocksLowerTriangular" | custom-call | tf_op jit(solution)/shard_map/triangular_solve/custom-call.0 | solution.py:31
  146.0 0.8 fusion.5
  146.9 37.6 %all-reduce.7.cloned.1.call-done = bf16[4,128,128]{2,1,0:T(8,128)(2,1)} async-done(((bf16[4,128,128]{2,1,0:T(8,128)(2,1)}), bf16[4,128,128]{2,1,0:T(8,128)(2,1)}) %all-reduce.7.cloned.1.call-update) | async-done | bytes 131088 | tf_op jit(solution)/shard_map/psum | solution.py:9
  184.5 51.6 %all-gather.5.cloned.1.call-done = bf16[4,4096,128]{2,1,0:T(8,128)(2,1)} async-done(((bf16[4,128,128]{2,1,0:T(8,128)(2,1)}), bf16[4,4096,128]{2,1,0:T(8,128)(2,1)}) %all-gather.5.cloned.1.call-update) | async-done | bytes 4194320 | tf_op jit(solution)/shard_map/all_gather | solution.py:42
  236.2 3.9 convolution_subtract_fusion
  240.1 3.2 copy-done
  244.2 1.0 slice.25
  245.3 93.3 %all-reduce.9.cloned.1.call-done = f32[128,128]{0,1:T(8,128)} async-done(((f32[128,128]{0,1:T(8,128)}), f32[128,128]{0,1:T(8,128)}) %all-reduce.9.cloned.1.call-update) | async-done | bytes 65552 | tf_op jit(solution)/shard_map/psum | solution.py:9
  338.6 0.9 copy.24
  339.5 0.9 fusion.12
  340.3 11.7 %cholesky.55 = f32[128,128]{1,0:T(8,128)S(1)} custom-call(f32[128,128]{1,0:T(8,128)S(1)} %fusion.12), custom_call_target="Cholesky" | custom-call | tf_op jit(solution)/shard_map/jit(cholesky)/cholesky | solution.py:29
  352.7 0.7 select_bitcast_fusion
  353.4 9.8 %custom-call.7 = f32[1,128,128]{1,2,0:T(8,128)S(1)} custom-call(f32[1,128,128]{2,1,0:T(8,128)S(1)} %get-tuple-element.8), custom_call_target="InvertDiagBlocksLowerTriangular" | custom-call | tf_op jit(solution)/shard_map/triangular_solve/custom-call.0 | solution.py:31
  363.8 0.8 fusion.6
  364.6 37.6 %all-reduce.11.cloned.1.call-done = bf16[4,128,128]{2,1,0:T(8,128)(2,1)} async-done(((bf16[4,128,128]{2,1,0:T(8,128)(2,1)}), bf16[4,128,128]{2,1,0:T(8,128)(2,1)}) %all-reduce.11.cloned.1.call-update) | async-done | bytes 131088 | tf_op jit(solution)/shard_map/psum | solution.py:9
  402.7 1.5 convert_bitcast_fusion
  404.3 1.0 copy.28
  405.3 48.5 %all-gather.7.cloned.1.call-done = bf16[4,4096,128]{2,1,0:T(8,128)(2,1)} async-done(((bf16[4,128,128]{2,1,0:T(8,128)(2,1)}), bf16[4,4096,128]{2,1,0:T(8,128)(2,1)}) %all-gather.7.cloned.1.call-update) | async-done | bytes 4194320 | tf_op jit(solution)/shard_map/all_gather | solution.py:42
  453.8 1.5 convert_bitcast_fusion.1
  455.2 6.8 %abs_reduce_fusion = (f32[4,32]{1,0:T(4,128)S(1)}, f32[4,128,32,128]{1,3,2,0:T(8,128)S(1)}) fusion(f32[4,128,32,128]{1,3,2,0:T(8,128)} %copy-done, bf16[32,4,128,128]{3,2,1,0:T(8,128)(2,1)} %bitcast.82, s32[]{:T(128)S(6)} %select_n.78, bf16[4,128,128]{2,1,0:T(8,128)(2,1)} %all-reduce.11.cloned.1.call-done, f32[4,128,128]{1,2,0:T(8,128)S(1)} %copy.30, ...), kind=kOutput, calls=%fused_computation.1 | convolution fusion | flops 555745152 | bytes 22807812 | tf_op jit(solution)/shard_map/ik,jk->ij/dot_general | solution.py:48
  462.1 3.3 fusion
  465.4 7.8 %copy.32 = bf16[4,1,128,32,1,128]{5,3,4,2,1,0:T(8,128)(2,1)} copy(bf16[4,1,128,32,1,128]{2,5,3,0,4,1:T(8,128)(2,1)} %fusion) | data formatting | bytes 8388608
  (42 shorter events, 4.3 us)
Async XLA Ops:
  7.2 7.9 %copy-start.3 = (f32[4,1,32,1]{2,3,1,0:T(1,128)S(1)}, f32[4,1,32,1]{2,3,1,0:T(1,128)}, u32[]{:S(2)}) copy-start(f32[4,1,32,1]{2,3,1,0:T(1,128)} %param.6) | copy-start | bytes 1540
  7.2 113.7 %all-reduce.5.cloned.1.call-start = ((), (), s32[]{:S(2)}) async-start(), calls=%async_computation | async-start | bytes 131072 | tf_op jit(solution)/shard_map/psum | solution.py:9
  17.9 3.2 copy-start.1
  21.7 162.7 %all-reduce.7.cloned.1.call-start = ((), (), s32[]{:S(2)}) async-start(), calls=%async_computation.1 | async-start | bytes 262144 | tf_op jit(solution)/shard_map/psum | solution.py:9
  146.8 89.4 %all-gather.5.cloned.1.call-start = ((), (), s32[]{:S(2)}) async-start(), calls=%async_computation.4 | async-start | bytes 4325376 | tf_op jit(solution)/shard_map/all_gather | solution.py:42
  184.5 154.1 %all-reduce.9.cloned.1.call-start = ((), (), s32[]{:S(2)}) async-start(), calls=%async_computation.2 | async-start | bytes 131072 | tf_op jit(solution)/shard_map/psum | solution.py:9
  236.2 166.4 %copy-start.2 = (bf16[4,128,128]{2,1,0:T(8,128)(2,1)S(1)}, bf16[4,128,128]{2,1,0:T(8,128)(2,1)}, u32[]{:S(2)}) copy-start(bf16[4,128,128]{2,1,0:T(8,128)(2,1)} %all-reduce.7.cloned.1.call-done) | copy-start | bytes 393220
  240.1 3.2 copy-start
  243.9 158.3 %all-reduce.11.cloned.1.call-start = ((), (), s32[]{:S(2)}) async-start(), calls=%async_computation.3 | async-start | bytes 262144 | tf_op jit(solution)/shard_map/psum | solution.py:9
  364.6 89.2 %all-gather.7.cloned.1.call-start = ((), (), s32[]{:S(2)}) async-start(), calls=%async_computation.5 | async-start | bytes 4325376 | tf_op jit(solution)/shard_map/all_gather | solution.py:42
  462.1 11.1 %copy-start.4 = (f32[4,32]{1,0:T(4,128)}, f32[4,32]{1,0:T(4,128)S(1)}, u32[]{:S(2)}) copy-start(f32[4,32]{1,0:T(4,128)S(1)} %broadcast_add_fusion) | copy-start | bytes 1540
Sparse Core Ops, SparseCore 0:
  21.9 98.9 all-reduce.4
  146.9 37.4 all-reduce.6
  186.8 49.3 all-gather.4
  244.1 94.4 all-reduce.8
  364.7 37.5 all-reduce.10
  404.4 49.3 all-gather.6
where the time goes:
time: 481 us; the launch traced here: 480 us
  waiting for transfers between devices  367 us (76%)
  other arithmetic  59.4 us (12%)
  local copies, waits for them, and re-layouts  27.7 us (6%)
  between operations  14.4 us (3%)
  matrix products  11.5 us (2%)
    psum x4, waiting for transfers between devices, from_root(): return lax.psum(jnp.where(mine, array, jnp.zeros_like(array)), axis)  266 us
    all_gather x2, waiting for transfers between devices, columns_of(): whole = lax.all_gather(row_strip[:, None], 'row', axis=1, tiled=True)  100 us
    another operation x6, other arithmetic, factor_panel(): factor = jnp.linalg.cholesky(diag_block)  24.8 us
    unnamed x12, local copies, waits for them, and re-layouts  22.1 us
    another operation x4, other arithmetic, factor_panel(): lax.linalg.triangular_solve(factor, column, left_side=False, lower=True,...  20.9 us
    dot_general x2, matrix products, update(): jnp.einsum('ik,jk->ij', row_strip.reshape(block_rows * block_size, width)...  10.7 us
  transfers between devices with their start and end apart: 6, of which 6 were waited for; matrix products, arithmetic and copies ran while one was open for 1% of the time, Pallas kernels for 0%

commit v1 on v0

v1 whole, which is shorter than its diff:
```python
import jax
import jax.numpy as jnp
from jax import lax
from jax.experimental import pallas as pl
from jax.experimental.pallas import tpu as pltpu
from jax.sharding import PartitionSpec as P

AXES = ("row", "col")
NX, NY, NZ, NK = 4, 4, 4, 2
BS = 128
PIECE = 4 * BS + 16
HIGH = lax.Precision.HIGHEST


def dev(z, y, k, x):
    return (((z % NZ) * NY + (y % NY)) * NK + (k % NK)) * NX + (x % NX)


PLACES = [(z, y, k, x) for z in range(NZ) for y in range(NY) for k in range(NK) for x in range(NX)]


def shift(array, dz=0, dy=0, dk=0, dx=0, where=lambda z, y, k, x: True):
    pairs = [
        (dev(z, y, k, x), dev(z + dz, y + dy, k + dk, x + dx)) for z, y, k, x in PLACES if where(z, y, k, x)
    ]
    return lax.ppermute(array, AXES, pairs)


def scale_rows(scale):
    high = lax.reduce_precision(scale, 8, 7)
    rest = scale - high
    mid = lax.reduce_precision(rest, 8, 7)
    low = lax.reduce_precision(rest - mid, 8, 7)
    rows = jnp.stack([high, mid, low], axis=1).reshape(12, 1)
    rows = jnp.concatenate([rows, jnp.zeros((4, 1), jnp.float32)], axis=0)
    return jnp.broadcast_to(rows, (16, BS)).astype(jnp.bfloat16)


def along_x(array, x, where=lambda z, y, k, x: True):
    pairs = [
        [(0, 1), (1, 0)],
        [(0, 3), (1, 2)],
        [(0, 2), (1, 3)],
    ]
    got = []
    for hop in pairs:
        table = [
            (dev(z, y, k, s), dev(z, y, k, t))
            for z, y, k, s in PLACES
            for s0, t in hop
            if s == s0 and where(z, y, k, s)
        ]
        got.append(lax.ppermute(array, AXES, table))
    u = jnp.where(x <= 1, array, got[1])
    v = jnp.where(x <= 1, got[0], got[2])
    return u, v


def leading_block(lead, z, y, k, x):
    at_root = lambda z, y, k, x: z == 0 and y == 0 and (k == 1 or x == 0)
    u, v = along_x(lead, x, at_root)
    first = (x == 0) | (x == 3)
    pair = jnp.concatenate([jnp.where(first, u, v), jnp.where(first, v, u)], axis=0)
    root = lambda z, y, k, x: z == 0 and y == 0
    up, down, over = (shift(pair, dy=d, where=root) for d in (1, -1, 2))
    pair = jnp.where(y == 0, pair, jnp.where(y == 1, up, jnp.where(y == 3, down, over)))
    root = lambda z, y, k, x: z == 0
    up, down, over = (shift(pair, dz=d, where=root) for d in (1, -1, 2))
    pair = jnp.where(z == 0, pair, jnp.where(z == 1, up, jnp.where(z == 3, down, over)))
    other = shift(pair, dk=1)
    rows = BS + 16
    core0 = jnp.where(k == 0, pair, other)
    core1 = jnp.where(k == 0, other, pair)
    blocks = [core0[:rows], core1[:rows], core1[rows:]]

    def value(b):
        s = b[BS].astype(jnp.float32) + b[BS + 1].astype(jnp.float32) + b[BS + 2].astype(jnp.float32)
        return b[:BS].astype(jnp.float32) * s[None, :]

    return [value(b) for b in blocks]


def column_pieces(piece, z, y, k, x):
    table = [
        (dev(zz, yy, kk, p), dev(zz, yy, p, 2 * (yy % 2) + kk))
        for zz in range(NZ)
        for yy in range(NY)
        for kk in range(NK)
        for p in range(2)
    ]
    mine = lax.ppermute(piece, AXES, table)
    source = lambda z, y, k, x: y % 2 == x // 2
    up, down, over = (shift(mine, dy=d, where=source) for d in (1, -1, 2))
    turn = (y - x // 2) % 4
    slot0 = jnp.where(turn == 0, mine, jnp.where(turn == 1, up, jnp.where(turn == 2, over, down)))
    slot1 = jnp.where(turn == 0, over, jnp.where(turn == 1, down, jnp.where(turn == 2, mine, up)))
    both = jnp.concatenate([slot0, slot1], axis=0)
    held = [both] + [shift(both, dz=d) for d in (1, -1, 2)]
    return held, [shift(h, dk=1) for h in held]


def factor(blocks):
    d00, d10, d11 = blocks
    eye = jnp.eye(BS, dtype=jnp.float32)
    solve = lambda l: lax.linalg.triangular_solve(l, eye, left_side=True, lower=True)
    l0 = jnp.linalg.cholesky(d00)
    w00 = solve(l0)
    l10 = jnp.dot(d10, w00.T, precision=HIGH).astype(jnp.bfloat16)
    l10f = l10.astype(jnp.float32)
    l1 = jnp.linalg.cholesky(d11 - jnp.dot(l10f, l10f.T, precision=HIGH))
    w11 = solve(l1)
    w10 = -jnp.dot(w11, jnp.dot(l10f, w00, precision=HIGH), precision=HIGH)
    wt = jnp.concatenate(
        [
            jnp.concatenate([w00.T, w10.T], axis=1),
            jnp.concatenate([jnp.zeros_like(eye), w11.T], axis=1),
        ],
        axis=0,
    )
    return l0, l10f, l1, wt


def finish_kernel(place, a_ref, sc_ref, m0, m1, m2, m3, t0, t1, t2, t3, u_ref, v_ref, wt_ref, corner_ref,
                  out_ref, big_ref, q_ref, p_ref, prod_ref, wk_ref):
    step = pl.program_id(0)
    row, col, k, z, first = place[0], place[1], place[2], place[3], place[4]

    def scale_of(ref, base, a):
        s = ref[base + 4 * BS : base + 4 * BS + 16, :].astype(jnp.float32)
        return s[3 * a : 3 * a + 1] + s[3 * a + 1 : 3 * a + 2] + s[3 * a + 2 : 3 * a + 3]

    def panel_tile(ref_m, ref_t, base, a, wm, wt):
        def part(ref, w):
            raw = ref[base + a * BS : base + (a + 1) * BS, :]
            d = jnp.dot(jnp.concatenate([raw, raw], axis=1), w, preferred_element_type=jnp.float32)
            s = scale_of(ref, base, a)
            return d * jnp.concatenate([s, s], axis=1)

        return (part(ref_m, wm) + part(ref_t, wt)).astype(jnp.bfloat16)

    @pl.when(step == 0)
    def _():
        w = wt_ref[...]
        hi = w.astype(jnp.bfloat16)
        lo = (w - hi.astype(jnp.float32)).astype(jnp.bfloat16)
        for h in range(2):
            wk_ref[h, :BS, :] = hi[h * BS : (h + 1) * BS]
            wk_ref[h, BS:, :] = lo[h * BS : (h + 1) * BS]
        w_mine = wk_ref[k]
        w_other = wk_ref[1 - k]
        for i, (mine, other) in enumerate(((m0, t0), (m1, t1), (m2, t2), (m3, t3))):
            zs = lax.rem(z + (0, 3, 1, 2)[i], 4)
            for ys in range(2):
                for a in range(4):
                    b = a * 8 + zs * 2 + ys
                    q_ref[pl.ds(pl.multiple_of(b * BS, BS), BS), :] = panel_tile(
                        mine, other, ys * PIECE, a, w_mine, w_other
                    )
        w_u = wk_ref[first]
        w_v = wk_ref[1 - first]
        for a in range(4):
            p_ref[a * BS : (a + 1) * BS, :] = panel_tile(u_ref, v_ref, 0, a, w_u, w_v)
        e = lax.broadcasted_iota(jnp.int32, (BS, 2 * BS), 0)
        f = lax.broadcasted_iota(jnp.int32, (BS, 2 * BS), 1)

        @pl.when(row < 2)
        def _():
            p_ref[0:BS, :] = jnp.where(f == e + row * BS, -1.0, 0.0).astype(jnp.bfloat16)

        @pl.when(col < 2)
        def _():
            q_ref[0:BS, :] = jnp.where(f == e + col * BS, -1.0, 0.0).astype(jnp.bfloat16)

    p = p_ref[pl.ds(pl.multiple_of(step * BS, BS), BS), :]
    for b in range(32):
        d = lax.dot_general(
            p, q_ref[b * BS : (b + 1) * BS, :], (((1,), (1,)), ((), ())), preferred_element_type=jnp.float32
        )
        prod_ref[pl.ds(b, BS, stride=32), :] = d

    @pl.when((step == 0) & (row < 2) & (col < 2))
    def _():
        prod_ref[pl.ds(0, BS, stride=32), :] = -corner_ref[...]

    sc = sc_ref[0]

    def update(e, mx):
        rows = pl.ds(pl.multiple_of(e * 32, 32), 32)
        m = a_ref[0, e].astype(jnp.float32) * sc - prod_ref[rows, :]
        prod_ref[rows, :] = m
        return jnp.maximum(mx, jnp.abs(m))

    mx = lax.fori_loop(0, BS, update, jnp.zeros((32, BS), jnp.float32), unroll=8)
    big = jnp.max(mx, axis=1, keepdims=True) + 1e-06
    big = jnp.broadcast_to(big, (32, BS))
    big_ref[0] = big
    inv = 1.0 / big

    def divide(e, carry):
        rows = pl.ds(pl.multiple_of(e * 32, 32), 32)
        out_ref[0, e] = (prod_ref[rows, :] * inv).astype(jnp.bfloat16)
        return carry

    lax.fori_loop(0, BS, divide, 0, unroll=8)


def finish(place, blocks, sc, held, others, u, v, wt, corner):
    whole = lambda shape: pl.BlockSpec(shape, lambda a, *_: (0,) * len(shape))
    spec = pltpu.PrefetchScalarGridSpec(
        num_scalar_prefetch=1,
        grid=(4,),
        in_specs=[
            pl.BlockSpec((1, BS, 32, BS), lambda a, *_: (a, 0, 0, 0)),
            pl.BlockSpec((1, 32, BS), lambda a, *_: (a, 0, 0)),
        ]
        + [whole((2 * PIECE, BS))] * 8
        + [whole((PIECE, BS))] * 2
        + [whole((2 * BS, 2 * BS)), whole((BS, BS))],
        out_specs=[
            pl.BlockSpec((1, BS, 32, BS), lambda a, *_: (a, 0, 0, 0)),
            pl.BlockSpec((1, 32, BS), lambda a, *_: (a, 0, 0)),
        ],
        scratch_shapes=[
            pltpu.VMEM((32 * BS, 2 * BS), jnp.bfloat16),
            pltpu.VMEM((4 * BS, 2 * BS), jnp.bfloat16),
            pltpu.VMEM((32 * BS, BS), jnp.float32),
            pltpu.VMEM((2, 2 * BS, 2 * BS), jnp.bfloat16),
        ],
    )
    return pl.pallas_call(
        finish_kernel,
        grid_spec=spec,
        out_shape=[
            jax.ShapeDtypeStruct((4, BS, 32, BS), jnp.bfloat16),
            jax.ShapeDtypeStruct((4, 32, BS), jnp.float32),
        ],
        compiler_params=pltpu.CompilerParams(vmem_limit_bytes=32 * 1024 * 1024),
        cost_estimate=pl.CostEstimate(flops=2 * 512 * 4096 * 512, bytes_accessed=12 * 2**20, transcendentals=0),
        name="finish",
    )(place, blocks, sc, *held, *others, u, v, wt, corner)


def on_device(blocks, scales):
    row = lax.axis_index("row")
    col = lax.axis_index("col")
    x = col
    k = row % 2
    y = (row // 2) % 4
    z = row // 8
    blocks = blocks.reshape(4, BS, 32, BS)
    scales = scales.reshape(4, 32)
    srows = scale_rows(scales[:, 0])
    strip = blocks[:, :, 0, :]
    piece = jnp.concatenate([strip.reshape(4 * BS, BS), srows], axis=0)
    lead = jnp.concatenate([strip[0], srows], axis=0)

    lead_blocks = leading_block(lead, z, y, k, x)
    held, others = column_pieces(piece, z, y, k, x)
    u, v = along_x(piece, x)
    l0, l10, l1, wt = factor(lead_blocks)
    corner = jnp.where(
        row == 0, jnp.where(col == 0, l0, l10.T), jnp.where(col == 0, l10, l1)
    )
    special = ((jnp.arange(4) == 0) & (row < 2))[:, None] | ((jnp.arange(32) == 0) & (col < 2))[None, :]
    sc = jnp.broadcast_to(jnp.where(special, 0.0, scales)[:, :, None], (4, 32, BS))
    first = jnp.where((x == 0) | (x == 3), 0, 1)
    place = jnp.stack([row, col, k, z, first]).astype(jnp.int32)
    factored, largest = finish(place, blocks, sc, held, others, u, v, wt, corner)
    return factored.reshape(4, 1, BS, 32, 1, BS), largest[:, None, :, :1]


def solution(mesh):
    in_specs = (P(None, "row", None, None, "col", None), P(None, "row", None, "col"))
    out_specs = (P(None, "row", None, None, "col", None), P(None, "row", None, "col"))
    return jax.shard_map(
        on_device, mesh=mesh, in_specs=in_specs, out_specs=out_specs, check_vma=False
    )
```

time: 481 us -> 121 us (0.25)
  waiting for transfers between devices: 367 us -> 10.3 us
  starting transfers between devices: 0.42 us -> 38.7 us
  local copies, waits for them, and re-layouts: 27.7 us -> 6.17 us
  between operations: 14.4 us -> 1.18 us
  Pallas kernels: 0 us -> 12.9 us
  other arithmetic: 59.4 us -> 48.6 us
  matrix products: 11.5 us -> 2.17 us
    psum x4 -> x0, waiting for transfers between devices: 266 us -> none  [from_root(): return lax.psum(jnp.where(mine, array, jnp.zeros_like(array)), axis)]
    all_gather x2 -> x0, waiting for transfers between devices: 100 us -> none  [columns_of(): whole = lax.all_gather(row_strip[:, None], 'row', axis=1, tiled=True)]
    ppermute x0 -> x24, starting transfers between devices: none -> 38.7 us  [the longest x17 23 us: shift(): return lax.ppermute(array, AXES, pairs)]
    unnamed x12 -> x3, local copies, waits for them, and re-layouts: 22.1 us -> 2.21 us
    pallas_call x0 -> x1, Pallas kernels: none -> 12.9 us  [finish(): pl.pallas_call(finish_kernel, grid_spec=spec, out_shape=[jax.ShapeDtypeSt...]
    ppermute x0 -> x24, waiting for transfers between devices: none -> 10.3 us  [the longest x17 10.3 us: shift(): return lax.ppermute(array, AXES, pairs)]
    dot_general x2 -> x4, matrix products: 10.7 us -> 1.62 us  [the longest x1 1 us: factor(): l10 = jnp.dot(d10, w00.T, precision=HIGH).astype(jnp.bfloat16)]
    reshape x2 -> x0, other arithmetic: 6.1 us -> none  [the longest x1 3.3 us: on_device(): factored.reshape(block_rows, 1, block_size, block_cols, 1, block_size)]
  transfers between devices with their start and end apart: 6 -> 24, of which waited for: 6 -> 5; matrix products, arithmetic and copies ran while one was open for 1% -> 43% of each run, Pallas kernels for 0% -> 0%
where the time goes in v1:
time: 121 us; the launch traced here: 120 us
  other arithmetic  48.6 us (40%)
  starting transfers between devices  38.7 us (32%)
  Pallas kernels  12.9 us (11%)
  waiting for transfers between devices  10.3 us (9%)
  local copies, waits for them, and re-layouts  6.17 us (5%)
  matrix products  2.17 us (2%)
    ppermute x17, starting transfers between devices, shift(): return lax.ppermute(array, AXES, pairs)  23 us
    another operation x3, other arithmetic, factor(): lax.linalg.triangular_solve(l, eye, left_side=True, lower=True)  20.4 us
    pallas_call x1, Pallas kernels, finish(): pl.pallas_call(finish_kernel, grid_spec=spec, out_shape=[jax.ShapeDtypeSt...  12.9 us
    another operation x3, other arithmetic, factor(): l0 = jnp.linalg.cholesky(d00)  12.5 us
    another operation x3, other arithmetic, factor(): l1 = jnp.linalg.cholesky(d11 - jnp.dot(l10f, l10f.T, precision=HIGH))  12.4 us
    ppermute x6, starting transfers between devices, along_x(): got.append(lax.ppermute(array, AXES, table))  12.2 us
    ppermute x17, waiting for transfers between devices, shift(): return lax.ppermute(array, AXES, pairs)  10.3 us
    ppermute x1, starting transfers between devices, column_pieces(): mine = lax.ppermute(piece, AXES, table)  3.46 us
  transfers between devices with their start and end apart: 24, of which 5 were waited for; matrix products, arithmetic and copies ran while one was open for 43% of the time, Pallas kernels for 0%

profile of v1, /device:TPU:1, one launch (start us, length us, event | category | flops | bytes accessed | tf_op | source)
XLA Modules:
  0.0 120.0 jit_solution(7890760625292079384)
XLA Ops:
  1.5 1.0 slice.88
  2.6 3.9 %collective-permute-start.15 = (bf16[144,128]{0,1:T(8,128)(2,1)S(1)}, bf16[144,128]{0,1:T(8,128)(2,1)S(1)}, u32[]{:S(2)}, u32[]{:S(2)}) collective-permute-start(bf16[144,128]{0,1:T(8,128)(2,1)S(1)} %pad_maximum_fusion.3), channel_id=1, source_target_pairs={{0,1},{4,5},{5,4}} | collective-permute-start | bytes 110600 | tf_op jit(solution)/shard_map/ppermute | solution.py:53
  6.6 2.2 %collective-permute-start.16 = (bf16[144,128]{0,1:T(8,128)(2,1)S(1)}, bf16[144,128]{0,1:T(8,128)(2,1)S(1)}, u32[]{:S(2)}, u32[]{:S(2)}) collective-permute-start(bf16[144,128]{0,1:T(8,128)(2,1)S(1)} %pad_maximum_fusion.3), channel_id=1, source_target_pairs={{0,2},{4,6},{5,7}} | collective-permute-start | bytes 110600 | tf_op jit(solution)/shard_map/ppermute | solution.py:53
  8.8 1.3 %collective-permute-start.14 = (bf16[144,128]{0,1:T(8,128)(2,1)S(1)}, bf16[144,128]{0,1:T(8,128)(2,1)S(1)}, u32[]{:S(2)}, u32[]{:S(2)}) collective-permute-start(bf16[144,128]{0,1:T(8,128)(2,1)S(1)} %pad_maximum_fusion.3), channel_id=1, source_target_pairs={{0,3},{4,7},{5,6}} | collective-permute-start | bytes 110600 | tf_op jit(solution)/shard_map/ppermute | solution.py:53
  10.1 1.4 %slice.87 = bf16[4,128,1,128]{3,2,1,0:T(2,128)(2,1)S(1)} slice(bf16[4,128,32,128]{3,2,1,0:T(8,128)(2,1)} %bitcast.49), slice={[0:4], [0:128], [0:1], [0:128]} | slice | bytes 262144 | tf_op jit(solution)/shard_map/slice | solution.py:253
  11.7 2.2 %collective-permute-start.12 = (bf16[528,128]{1,0:T(8,128)(2,1)S(1)}, bf16[528,128]{1,0:T(8,128)(2,1)S(1)}, u32[]{:S(2)}, u32[]{:S(2)}) collective-permute-start(bf16[528,128]{1,0:T(8,128)(2,1)S(1)} %pad_maximum_fusion.1), channel_id=1, source_target_pairs={{0,1},{1,0},{4,5},{5,4},{8,9},{9,8},{12,13},{13,12},{16,17},{17,16... | collective-permute-start | bytes 405512 | tf_op jit(solution)/shard_map/ppermute | solution.py:53
  13.9 1.3 %collective-permute-start.13 = (bf16[528,128]{1,0:T(8,128)(2,1)S(1)}, bf16[528,128]{1,0:T(8,128)(2,1)S(1)}, u32[]{:S(2)}, u32[]{:S(2)}) collective-permute-start(bf16[528,128]{1,0:T(8,128)(2,1)S(1)} %pad_maximum_fusion.1), channel_id=1, source_target_pairs={{0,2},{1,3},{4,6},{5,7},{8,10},{9,11},{12,14},{13,15},{16,18},{17,... | collective-permute-start | bytes 405512 | tf_op jit(solution)/shard_map/ppermute | solution.py:53
  15.4 2.0 %collective-permute-start.19 = (bf16[288,128]{0,1:T(8,128)(2,1)S(1)}, bf16[288,128]{0,1:T(8,128)(2,1)S(1)}, u32[]{:S(2)}, u32[]{:S(2)}) collective-permute-start(bf16[288,128]{0,1:T(8,128)(2,1)S(1)} %pad_maximum_fusion.2), channel_id=1, source_target_pairs={{0,16},{1,17},{2,18},{3,19},{4,20},{5,21},{6,22},{7,23}} | collective-permute-start | bytes 221192 | tf_op jit(solution)/shard_map/ppermute | solution.py:26
  17.4 1.3 %collective-permute-start.18 = (bf16[288,128]{0,1:T(8,128)(2,1)S(1)}, bf16[288,128]{0,1:T(8,128)(2,1)S(1)}, u32[]{:S(2)}, u32[]{:S(2)}) collective-permute-start(bf16[288,128]{0,1:T(8,128)(2,1)S(1)} %pad_maximum_fusion.2), channel_id=1, source_target_pairs={{0,24},{1,25},{2,26},{3,27},{4,28},{5,29},{6,30},{7,31}} | collective-permute-start | bytes 221192 | tf_op jit(solution)/shard_map/ppermute | solution.py:26
  18.7 1.3 %collective-permute-start.17 = (bf16[288,128]{0,1:T(8,128)(2,1)S(1)}, bf16[288,128]{0,1:T(8,128)(2,1)S(1)}, u32[]{:S(2)}, u32[]{:S(2)}) collective-permute-start(bf16[288,128]{0,1:T(8,128)(2,1)S(1)} %pad_maximum_fusion.2), channel_id=1, source_target_pairs={{0,8},{1,9},{2,10},{3,11},{4,12},{5,13},{6,14},{7,15}} | collective-permute-start | bytes 221192 | tf_op jit(solution)/shard_map/ppermute | solution.py:26
  20.9 1.3 %collective-permute-start.11 = (bf16[528,128]{1,0:T(8,128)(2,1)S(1)}, bf16[528,128]{1,0:T(8,128)(2,1)S(1)}, u32[]{:S(2)}, u32[]{:S(2)}) collective-permute-start(bf16[528,128]{1,0:T(8,128)(2,1)S(1)} %pad_maximum_fusion.1), channel_id=1, source_target_pairs={{0,3},{1,2},{4,7},{5,6},{8,11},{9,10},{12,15},{13,14},{16,19},{17,... | collective-permute-start | bytes 405512 | tf_op jit(solution)/shard_map/ppermute | solution.py:53
  22.2 3.5 %collective-permute-start = (bf16[528,128]{1,0:T(8,128)(2,1)S(1)}, bf16[528,128]{1,0:T(8,128)(2,1)S(1)}, u32[]{:S(2)}, u32[]{:S(2)}) collective-permute-start(bf16[528,128]{1,0:T(8,128)(2,1)S(1)} %pad_maximum_fusion.1), channel_id=1, source_target_pairs={{0,0},{1,4},{4,1},{5,5},{8,10},{9,14},{12,11},{13,15},{16,16},{17,... | collective-permute-start | bytes 405512 | tf_op jit(solution)/shard_map/ppermute | solution.py:91
  25.8 1.3 %collective-permute-start.22 = (bf16[288,128]{0,1:T(8,128)(2,1)S(1)}, bf16[288,128]{0,1:T(8,128)(2,1)S(1)}, u32[]{:S(2)}, u32[]{:S(2)}) collective-permute-start(bf16[288,128]{0,1:T(8,128)(2,1)S(1)} %select_select_fusion.3), channel_id=1, source_target_pairs={{0,64},{1,65},{2,66},{3,67},{4,68},{5,69},{6,70},{7,71},{8,72},{9,... | collective-permute-start | bytes 221192 | tf_op jit(solution)/shard_map/ppermute | solution.py:26
  27.1 1.3 %collective-permute-start.21 = (bf16[288,128]{0,1:T(8,128)(2,1)S(1)}, bf16[288,128]{0,1:T(8,128)(2,1)S(1)}, u32[]{:S(2)}, u32[]{:S(2)}) collective-permute-start(bf16[288,128]{0,1:T(8,128)(2,1)S(1)} %select_select_fusion.3), channel_id=1, source_target_pairs={{0,96},{1,97},{2,98},{3,99},{4,100},{5,101},{6,102},{7,103},{8,104... | collective-permute-start | bytes 221192 | tf_op jit(solution)/shard_map/ppermute | solution.py:26
  28.4 1.3 %collective-permute-start.20 = (bf16[288,128]{0,1:T(8,128)(2,1)S(1)}, bf16[288,128]{0,1:T(8,128)(2,1)S(1)}, u32[]{:S(2)}, u32[]{:S(2)}) collective-permute-start(bf16[288,128]{0,1:T(8,128)(2,1)S(1)} %select_select_fusion.3), channel_id=1, source_target_pairs={{0,32},{1,33},{2,34},{3,35},{4,36},{5,37},{6,38},{7,39},{8,40},{9,... | collective-permute-start | bytes 221192 | tf_op jit(solution)/shard_map/ppermute | solution.py:26
  29.7 2.5 %collective-permute-start.3 = (bf16[528,128]{1,0:T(8,128)(2,1)S(1)}, bf16[528,128]{1,0:T(8,128)(2,1)S(1)}, u32[]{:S(2)}, u32[]{:S(2)}) collective-permute-start(bf16[528,128]{1,0:T(8,128)(2,1)S(1)} %collective-permute-done), channel_id=1, source_target_pairs={{0,24},{1,25},{4,28},{5,29},{10,2},{11,3},{14,6},{15,7},{16,8},{17... | collective-permute-start | bytes 405512 | tf_op jit(solution)/shard_map/ppermute | solution.py:26
  32.3 3.0 %collective-permute-start.2 = (bf16[528,128]{1,0:T(8,128)(2,1)S(1)}, bf16[528,128]{1,0:T(8,128)(2,1)S(1)}, u32[]{:S(2)}, u32[]{:S(2)}) collective-permute-start(bf16[528,128]{1,0:T(8,128)(2,1)S(1)} %collective-permute-done), channel_id=1, source_target_pairs={{0,16},{1,17},{4,20},{5,21},{10,26},{11,27},{14,30},{15,31},{16,0}... | collective-permute-start | bytes 405512 | tf_op jit(solution)/shard_map/ppermute | solution.py:26
  35.4 1.3 %collective-permute-start.1 = (bf16[528,128]{1,0:T(8,128)(2,1)S(1)}, bf16[528,128]{1,0:T(8,128)(2,1)S(1)}, u32[]{:S(2)}, u32[]{:S(2)}) collective-permute-start(bf16[528,128]{1,0:T(8,128)(2,1)S(1)} %collective-permute-done), channel_id=1, source_target_pairs={{0,8},{1,9},{4,12},{5,13},{10,18},{11,19},{14,22},{15,23},{16,24},... | collective-permute-start | bytes 405512 | tf_op jit(solution)/shard_map/ppermute | solution.py:26
  38.8 11.7 %cholesky.44 = f32[128,128]{1,0:T(8,128)S(1)} custom-call(f32[128,128]{1,0:T(8,128)S(1)} %fusion.9), custom_call_target="Cholesky" | custom-call | tf_op jit(solution)/shard_map/jit(cholesky)/cholesky | solution.py:106
  52.1 9.8 %custom-call.6 = f32[1,128,128]{1,2,0:T(8,128)S(1)} custom-call(f32[1,128,128]{2,1,0:T(8,128)S(1)} %copy.36), custom_call_target="InvertDiagBlocksLowerTriangular" | custom-call | tf_op jit(solution)/shard_map/triangular_solve/custom-call.0 | solution.py:105
  62.2 1.0 fusion.4
  63.6 11.7 %cholesky.55 = f32[128,128]{1,0:T(8,128)S(1)} custom-call(f32[128,128]{1,0:T(8,128)S(1)} %fusion.7), custom_call_target="Cholesky" | custom-call | tf_op jit(solution)/shard_map/jit(cholesky)/cholesky | solution.py:110
  76.7 10.0 %custom-call.7 = f32[1,128,128]{1,2,0:T(8,128)S(1)} custom-call(f32[1,128,128]{2,1,0:T(8,128)S(1)} %get-tuple-element.23), custom_call_target="InvertDiagBlocksLowerTriangular" | custom-call | tf_op jit(solution)/shard_map/triangular_solve/custom-call.0 | solution.py:105
  86.8 0.9 collective-permute-start.6
  87.6 1.5 %collective-permute-start.4 = (bf16[1056,128]{1,0:T(8,128)(2,1)S(1)}, bf16[1056,128]{1,0:T(8,128)(2,1)S(1)}, u32[]{:S(2)}, u32[]{:S(2)}) collective-permute-start(bf16[1056,128]{1,0:T(8,128)(2,1)S(1)} %pad_maximum_fusion.m0), channel_id=1, source_target_pairs={{0,32},{1,33},{2,34},{3,35},{4,36},{5,37},{6,38},{7,39},{8,40},{9,... | collective-permute-start | bytes 811016 | tf_op jit(solution)/shard_map/ppermute | solution.py:26
  89.7 1.1 collective-permute-start.7
  90.8 5.3 %collective-permute-done.6.m3 = bf16[1056,128]{1,0:T(8,128)(2,1)S(1)} collective-permute-done((bf16[1056,128]{1,0:T(8,128)(2,1)S(1)}, bf16[1056,128]{1,0:T(8,128)(2,1)S(1)}, u32[]{:S(2)}, u32[]{:S(2)}) %collective-permute-start.6) | collective-permute-done | bytes 270368 | tf_op jit(solution)/shard_map/ppermute | solution.py:26
  96.1 2.0 %collective-permute-start.10 = (bf16[1056,128]{1,0:T(8,128)(2,1)S(1)}, bf16[1056,128]{1,0:T(8,128)(2,1)S(1)}, u32[]{:S(2)}, u32[]{:S(2)}) collective-permute-start(bf16[1056,128]{1,0:T(8,128)(2,1)S(1)} %collective-permute-done.6.m3), channel_id=1, source_target_pairs={{0,4},{1,5},{2,6},{3,7},{4,0},{5,1},{6,2},{7,3},{8,12},{9,13},{10,... | collective-permute-start | bytes 811016 | tf_op jit(solution)/shard_map/ppermute | solution.py:26
  98.4 1.2 collective-permute-start.9
  99.5 3.0 %collective-permute-done.4.m1 = bf16[1056,128]{1,0:T(8,128)(2,1)S(1)} collective-permute-done((bf16[1056,128]{1,0:T(8,128)(2,1)S(1)}, bf16[1056,128]{1,0:T(8,128)(2,1)S(1)}, u32[]{:S(2)}, u32[]{:S(2)}) %collective-permute-start.4) | collective-permute-done | bytes 270368 | tf_op jit(solution)/shard_map/ppermute | solution.py:26
  104.3 2.2 %copy-done = bf16[4,1,128,32,1,128]{5,3,4,2,1,0:T(8,128)(2,1)S(1)} copy-done((bf16[4,1,128,32,1,128]{5,3,4,2,1,0:T(8,128)(2,1)S(1)}, bf16[4,1,128,32,1,128]{5,3,4,2,1,0:T(8,128)(2,1)}, u32[]{:S(2)}) %copy-start) | copy-done | bytes 4194328
  106.5 12.9 %finish.1 = (bf16[4,128,32,128]{3,2,1,0:T(8,128)(2,1)}, f32[4,32,128]{2,1,0:T(8,128)S(1)}) custom-call(s32[5]{0:T(128)S(1)} %stack.30.place, bf16[4,128,32,128]{3,2,1,0:T(8,128)(2,1)S(1)} %bitcast.50, f32[4,32,128]{2,1,0:T(8,128)S(1)} %broadcast_in_dim.11.sc_ref, bf16[1056,128]{1,0:T(8,128)(2,1)S(1)} %pad_maximum_fusion.m0, ...), custom_call_target="tpu_custom_call" | custom-call | flops 2147483648 | bytes 12582912 | tf_op jit(solution)/shard_map/finish/pallas_call | solution.py:230
  (73 shorter events, 11.2 us)
Async XLA Ops:
  2.6 12.6 %collective-permute-start.15 = (bf16[144,128]{0,1:T(8,128)(2,1)S(1)}, bf16[144,128]{0,1:T(8,128)(2,1)S(1)}, u32[]{:S(2)}, u32[]{:S(2)}) collective-permute-start(bf16[144,128]{0,1:T(8,128)(2,1)S(1)} %pad_maximum_fusion.3), channel_id=1, source_target_pairs={{0,1},{4,5},{5,4}} | collective-permute-start | bytes 110600 | tf_op jit(solution)/shard_map/ppermute | solution.py:53
  6.6 8.7 %collective-permute-start.16 = (bf16[144,128]{0,1:T(8,128)(2,1)S(1)}, bf16[144,128]{0,1:T(8,128)(2,1)S(1)}, u32[]{:S(2)}, u32[]{:S(2)}) collective-permute-start(bf16[144,128]{0,1:T(8,128)(2,1)S(1)} %pad_maximum_fusion.3), channel_id=1, source_target_pairs={{0,2},{4,6},{5,7}} | collective-permute-start | bytes 110600 | tf_op jit(solution)/shard_map/ppermute | solution.py:53
  8.8 6.5 %collective-permute-start.14 = (bf16[144,128]{0,1:T(8,128)(2,1)S(1)}, bf16[144,128]{0,1:T(8,128)(2,1)S(1)}, u32[]{:S(2)}, u32[]{:S(2)}) collective-permute-start(bf16[144,128]{0,1:T(8,128)(2,1)S(1)} %pad_maximum_fusion.3), channel_id=1, source_target_pairs={{0,3},{4,7},{5,6}} | collective-permute-start | bytes 110600 | tf_op jit(solution)/shard_map/ppermute | solution.py:53
  11.7 15.4 %collective-permute-start.12 = (bf16[528,128]{1,0:T(8,128)(2,1)S(1)}, bf16[528,128]{1,0:T(8,128)(2,1)S(1)}, u32[]{:S(2)}, u32[]{:S(2)}) collective-permute-start(bf16[528,128]{1,0:T(8,128)(2,1)S(1)} %pad_maximum_fusion.1), channel_id=1, source_target_pairs={{0,1},{1,0},{4,5},{5,4},{8,9},{9,8},{12,13},{13,12},{16,17},{17,16... | collective-permute-start | bytes 405512 | tf_op jit(solution)/shard_map/ppermute | solution.py:53
  13.9 14.5 %collective-permute-start.13 = (bf16[528,128]{1,0:T(8,128)(2,1)S(1)}, bf16[528,128]{1,0:T(8,128)(2,1)S(1)}, u32[]{:S(2)}, u32[]{:S(2)}) collective-permute-start(bf16[528,128]{1,0:T(8,128)(2,1)S(1)} %pad_maximum_fusion.1), channel_id=1, source_target_pairs={{0,2},{1,3},{4,6},{5,7},{8,10},{9,11},{12,14},{13,15},{16,18},{17,... | collective-permute-start | bytes 405512 | tf_op jit(solution)/shard_map/ppermute | solution.py:53
  15.4 5.5 %collective-permute-start.19 = (bf16[288,128]{0,1:T(8,128)(2,1)S(1)}, bf16[288,128]{0,1:T(8,128)(2,1)S(1)}, u32[]{:S(2)}, u32[]{:S(2)}) collective-permute-start(bf16[288,128]{0,1:T(8,128)(2,1)S(1)} %pad_maximum_fusion.2), channel_id=1, source_target_pairs={{0,16},{1,17},{2,18},{3,19},{4,20},{5,21},{6,22},{7,23}} | collective-permute-start | bytes 221192 | tf_op jit(solution)/shard_map/ppermute | solution.py:26
  17.4 4.7 %collective-permute-start.18 = (bf16[288,128]{0,1:T(8,128)(2,1)S(1)}, bf16[288,128]{0,1:T(8,128)(2,1)S(1)}, u32[]{:S(2)}, u32[]{:S(2)}) collective-permute-start(bf16[288,128]{0,1:T(8,128)(2,1)S(1)} %pad_maximum_fusion.2), channel_id=1, source_target_pairs={{0,24},{1,25},{2,26},{3,27},{4,28},{5,29},{6,30},{7,31}} | collective-permute-start | bytes 221192 | tf_op jit(solution)/shard_map/ppermute | solution.py:26
  18.7 6.9 %collective-permute-start.17 = (bf16[288,128]{0,1:T(8,128)(2,1)S(1)}, bf16[288,128]{0,1:T(8,128)(2,1)S(1)}, u32[]{:S(2)}, u32[]{:S(2)}) collective-permute-start(bf16[288,128]{0,1:T(8,128)(2,1)S(1)} %pad_maximum_fusion.2), channel_id=1, source_target_pairs={{0,8},{1,9},{2,10},{3,11},{4,12},{5,13},{6,14},{7,15}} | collective-permute-start | bytes 221192 | tf_op jit(solution)/shard_map/ppermute | solution.py:26
  20.9 16.4 %collective-permute-start.11 = (bf16[528,128]{1,0:T(8,128)(2,1)S(1)}, bf16[528,128]{1,0:T(8,128)(2,1)S(1)}, u32[]{:S(2)}, u32[]{:S(2)}) collective-permute-start(bf16[528,128]{1,0:T(8,128)(2,1)S(1)} %pad_maximum_fusion.1), channel_id=1, source_target_pairs={{0,3},{1,2},{4,7},{5,6},{8,11},{9,10},{12,15},{13,14},{16,19},{17,... | collective-permute-start | bytes 405512 | tf_op jit(solution)/shard_map/ppermute | solution.py:53
  22.2 7.5 %collective-permute-start = (bf16[528,128]{1,0:T(8,128)(2,1)S(1)}, bf16[528,128]{1,0:T(8,128)(2,1)S(1)}, u32[]{:S(2)}, u32[]{:S(2)}) collective-permute-start(bf16[528,128]{1,0:T(8,128)(2,1)S(1)} %pad_maximum_fusion.1), channel_id=1, source_target_pairs={{0,0},{1,4},{4,1},{5,5},{8,10},{9,14},{12,11},{13,15},{16,16},{17,... | collective-permute-start | bytes 405512 | tf_op jit(solution)/shard_map/ppermute | solution.py:91
  25.8 6.5 %collective-permute-start.22 = (bf16[288,128]{0,1:T(8,128)(2,1)S(1)}, bf16[288,128]{0,1:T(8,128)(2,1)S(1)}, u32[]{:S(2)}, u32[]{:S(2)}) collective-permute-start(bf16[288,128]{0,1:T(8,128)(2,1)S(1)} %select_select_fusion.3), channel_id=1, source_target_pairs={{0,64},{1,65},{2,66},{3,67},{4,68},{5,69},{6,70},{7,71},{8,72},{9,... | collective-permute-start | bytes 221192 | tf_op jit(solution)/shard_map/ppermute | solution.py:26
  27.1 8.3 %collective-permute-start.21 = (bf16[288,128]{0,1:T(8,128)(2,1)S(1)}, bf16[288,128]{0,1:T(8,128)(2,1)S(1)}, u32[]{:S(2)}, u32[]{:S(2)}) collective-permute-start(bf16[288,128]{0,1:T(8,128)(2,1)S(1)} %select_select_fusion.3), channel_id=1, source_target_pairs={{0,96},{1,97},{2,98},{3,99},{4,100},{5,101},{6,102},{7,103},{8,104... | collective-permute-start | bytes 221192 | tf_op jit(solution)/shard_map/ppermute | solution.py:26
  28.4 8.3 %collective-permute-start.20 = (bf16[288,128]{0,1:T(8,128)(2,1)S(1)}, bf16[288,128]{0,1:T(8,128)(2,1)S(1)}, u32[]{:S(2)}, u32[]{:S(2)}) collective-permute-start(bf16[288,128]{0,1:T(8,128)(2,1)S(1)} %select_select_fusion.3), channel_id=1, source_target_pairs={{0,32},{1,33},{2,34},{3,35},{4,36},{5,37},{6,38},{7,39},{8,40},{9,... | collective-permute-start | bytes 221192 | tf_op jit(solution)/shard_map/ppermute | solution.py:26
  29.7 56.9 %collective-permute-start.3 = (bf16[528,128]{1,0:T(8,128)(2,1)S(1)}, bf16[528,128]{1,0:T(8,128)(2,1)S(1)}, u32[]{:S(2)}, u32[]{:S(2)}) collective-permute-start(bf16[528,128]{1,0:T(8,128)(2,1)S(1)} %collective-permute-done), channel_id=1, source_target_pairs={{0,24},{1,25},{4,28},{5,29},{10,2},{11,3},{14,6},{15,7},{16,8},{17... | collective-permute-start | bytes 405512 | tf_op jit(solution)/shard_map/ppermute | solution.py:26
  32.3 54.4 %collective-permute-start.2 = (bf16[528,128]{1,0:T(8,128)(2,1)S(1)}, bf16[528,128]{1,0:T(8,128)(2,1)S(1)}, u32[]{:S(2)}, u32[]{:S(2)}) collective-permute-start(bf16[528,128]{1,0:T(8,128)(2,1)S(1)} %collective-permute-done), channel_id=1, source_target_pairs={{0,16},{1,17},{4,20},{5,21},{10,26},{11,27},{14,30},{15,31},{16,0}... | collective-permute-start | bytes 405512 | tf_op jit(solution)/shard_map/ppermute | solution.py:26
  35.4 51.3 %collective-permute-start.1 = (bf16[528,128]{1,0:T(8,128)(2,1)S(1)}, bf16[528,128]{1,0:T(8,128)(2,1)S(1)}, u32[]{:S(2)}, u32[]{:S(2)}) collective-permute-start(bf16[528,128]{1,0:T(8,128)(2,1)S(1)} %collective-permute-done), channel_id=1, source_target_pairs={{0,8},{1,9},{4,12},{5,13},{10,18},{11,19},{14,22},{15,23},{16,24},... | collective-permute-start | bytes 405512 | tf_op jit(solution)/shard_map/ppermute | solution.py:26
  36.7 1.5 %collective-permute-start.23 = (bf16[288,128]{0,1:T(8,128)(2,1)S(1)}, bf16[288,128]{0,1:T(8,128)(2,1)S(1)}, u32[]{:S(2)}, u32[]{:S(2)}) collective-permute-start(bf16[288,128]{0,1:T(8,128)(2,1)S(1)} %select_select_fusion.2), channel_id=1, source_target_pairs={{0,4},{1,5},{2,6},{3,7},{4,0},{5,1},{6,2},{7,3},{8,12},{9,13},{10,... | collective-permute-start | bytes 221192 | tf_op jit(solution)/shard_map/ppermute | solution.py:26
  86.8 9.3 %collective-permute-start.6 = (bf16[1056,128]{1,0:T(8,128)(2,1)S(1)}, bf16[1056,128]{1,0:T(8,128)(2,1)S(1)}, u32[]{:S(2)}, u32[]{:S(2)}) collective-permute-start(bf16[1056,128]{1,0:T(8,128)(2,1)S(1)} %pad_maximum_fusion.m0), channel_id=1, source_target_pairs={{0,64},{1,65},{2,66},{3,67},{4,68},{5,69},{6,70},{7,71},{8,72},{9,... | collective-permute-start | bytes 811016 | tf_op jit(solution)/shard_map/ppermute | solution.py:26
  87.6 10.7 %collective-permute-start.5 = (bf16[1056,128]{1,0:T(8,128)(2,1)S(1)}, bf16[1056,128]{1,0:T(8,128)(2,1)S(1)}, u32[]{:S(2)}, u32[]{:S(2)}) collective-permute-start(bf16[1056,128]{1,0:T(8,128)(2,1)S(1)} %pad_maximum_fusion.m0), channel_id=1, source_target_pairs={{0,96},{1,97},{2,98},{3,99},{4,100},{5,101},{6,102},{7,103},{8,104... | collective-permute-start | bytes 811016 | tf_op jit(solution)/shard_map/ppermute | solution.py:26
  87.6 14.9 %collective-permute-start.4 = (bf16[1056,128]{1,0:T(8,128)(2,1)S(1)}, bf16[1056,128]{1,0:T(8,128)(2,1)S(1)}, u32[]{:S(2)}, u32[]{:S(2)}) collective-permute-start(bf16[1056,128]{1,0:T(8,128)(2,1)S(1)} %pad_maximum_fusion.m0), channel_id=1, source_target_pairs={{0,32},{1,33},{2,34},{3,35},{4,36},{5,37},{6,38},{7,39},{8,40},{9,... | collective-permute-start | bytes 811016 | tf_op jit(solution)/shard_map/ppermute | solution.py:26
  89.7 13.7 %collective-permute-start.7 = (bf16[1056,128]{1,0:T(8,128)(2,1)S(1)}, bf16[1056,128]{1,0:T(8,128)(2,1)S(1)}, u32[]{:S(2)}, u32[]{:S(2)}) collective-permute-start(bf16[1056,128]{1,0:T(8,128)(2,1)S(1)} %pad_maximum_fusion.m0), channel_id=1, source_target_pairs={{0,4},{1,5},{2,6},{3,7},{4,0},{5,1},{6,2},{7,3},{8,12},{9,13},{10,... | collective-permute-start | bytes 811016 | tf_op jit(solution)/shard_map/ppermute | solution.py:26
  96.1 7.3 %collective-permute-start.10 = (bf16[1056,128]{1,0:T(8,128)(2,1)S(1)}, bf16[1056,128]{1,0:T(8,128)(2,1)S(1)}, u32[]{:S(2)}, u32[]{:S(2)}) collective-permute-start(bf16[1056,128]{1,0:T(8,128)(2,1)S(1)} %collective-permute-done.6.m3), channel_id=1, source_target_pairs={{0,4},{1,5},{2,6},{3,7},{4,0},{5,1},{6,2},{7,3},{8,12},{9,13},{10,... | collective-permute-start | bytes 811016 | tf_op jit(solution)/shard_map/ppermute | solution.py:26
  98.4 5.0 %collective-permute-start.9 = (bf16[1056,128]{1,0:T(8,128)(2,1)S(1)}, bf16[1056,128]{1,0:T(8,128)(2,1)S(1)}, u32[]{:S(2)}, u32[]{:S(2)}) collective-permute-start(bf16[1056,128]{1,0:T(8,128)(2,1)S(1)} %collective-permute-done.5.m2), channel_id=1, source_target_pairs={{0,4},{1,5},{2,6},{3,7},{4,0},{5,1},{6,2},{7,3},{8,12},{9,13},{10,... | collective-permute-start | bytes 811016 | tf_op jit(solution)/shard_map/ppermute | solution.py:26
  102.6 1.7 %collective-permute-start.8 = (bf16[1056,128]{1,0:T(8,128)(2,1)S(1)}, bf16[1056,128]{1,0:T(8,128)(2,1)S(1)}, u32[]{:S(2)}, u32[]{:S(2)}) collective-permute-start(bf16[1056,128]{1,0:T(8,128)(2,1)S(1)} %collective-permute-done.4.m1), channel_id=1, source_target_pairs={{0,4},{1,5},{2,6},{3,7},{4,0},{5,1},{6,2},{7,3},{8,12},{9,13},{10,... | collective-permute-start | bytes 811016 | tf_op jit(solution)/shard_map/ppermute | solution.py:26
  104.3 2.2 %copy-start = (bf16[4,1,128,32,1,128]{5,3,4,2,1,0:T(8,128)(2,1)S(1)}, bf16[4,1,128,32,1,128]{5,3,4,2,1,0:T(8,128)(2,1)}, u32[]{:S(2)}) copy-start(bf16[4,1,128,32,1,128]{5,3,4,2,1,0:T(8,128)(2,1)} %param.5) | copy-start | bytes 12582916

commit v2 on v1

v2 whole, which is shorter than its diff:
```python
import jax
import jax.numpy as jnp
from jax import lax
from jax.experimental import pallas as pl
from jax.experimental.pallas import tpu as pltpu
from jax.sharding import PartitionSpec as P

AXES = ("row", "col")
NX, NY, NZ, NK = 4, 4, 4, 2
BS = 128
PIECE = 4 * BS + 16


def dev(z, y, k, x):
    return (((z % NZ) * NY + (y % NY)) * NK + (k % NK)) * NX + (x % NX)


PLACES = [(z, y, k, x) for z in range(NZ) for y in range(NY) for k in range(NK) for x in range(NX)]


def shift(array, dz=0, dy=0, dk=0, dx=0, where=lambda z, y, k, x: True):
    pairs = [
        (dev(z, y, k, x), dev(z + dz, y + dy, k + dk, x + dx)) for z, y, k, x in PLACES if where(z, y, k, x)
    ]
    return lax.ppermute(array, AXES, pairs)


def scale_rows(scale):
    high = lax.reduce_precision(scale, 8, 7)
    rest = scale - high
    mid = lax.reduce_precision(rest, 8, 7)
    low = lax.reduce_precision(rest - mid, 8, 7)
    rows = jnp.stack([high, mid, low], axis=1).reshape(12, 1)
    rows = jnp.concatenate([rows, jnp.zeros((4, 1), jnp.float32)], axis=0)
    return jnp.broadcast_to(rows, (16, BS)).astype(jnp.bfloat16)


def along_x(array, x):
    got = []
    for hop in ({0: 1, 1: 0}, {0: 3, 1: 2}, {0: 2, 1: 3}):
        table = [(dev(z, y, k, s), dev(z, y, k, hop[s])) for z, y, k, s in PLACES if s in hop]
        got.append(lax.ppermute(array, AXES, table))
    u = jnp.where(x <= 1, array, got[1])
    v = jnp.where(x <= 1, got[0], got[2])
    return u, v


def leading_pair(u, v, first, z, y):
    head = lambda w: jnp.concatenate([w[:BS], w[4 * BS :]], axis=0)
    pair = jnp.concatenate([jnp.where(first == 0, head(u), head(v)), jnp.where(first == 0, head(v), head(u))], axis=0)
    root = lambda z, y, k, x: z == 0 and y == 0
    up, down, over = (shift(pair, dy=d, where=root) for d in (1, -1, 2))
    pair = jnp.where(y == 0, pair, jnp.where(y == 1, up, jnp.where(y == 3, down, over)))
    root = lambda z, y, k, x: z == 0
    up, down, over = (shift(pair, dz=d, where=root) for d in (1, -1, 2))
    return jnp.where(z == 0, pair, jnp.where(z == 1, up, jnp.where(z == 3, down, over)))


def column_strips(u, v, first, y, k, x):
    source = lambda z, y, k, x: y % 2 == x // 2
    giver = lambda z, y, k, x: source(z, y, k, x) and k == x % 2
    ours = jnp.where(first == k, u, v)
    mine = jnp.where(k == x % 2, ours, shift(jnp.where(first == k, v, u), dk=1, where=giver))
    up, down, over = (shift(mine, dy=d, where=source) for d in (1, -1, 2))
    turn = (y - x // 2) % 4
    slot0 = jnp.where(turn == 0, mine, jnp.where(turn == 1, up, jnp.where(turn == 2, over, down)))
    slot1 = jnp.where(turn == 0, over, jnp.where(turn == 1, down, jnp.where(turn == 2, mine, up)))
    return jnp.concatenate([slot0, slot1], axis=0)


def split3(x):
    h = x.astype(jnp.bfloat16).astype(jnp.float32)
    m = (x - h).astype(jnp.bfloat16).astype(jnp.float32)
    return h, m, x - h - m


def splat(x, shape):
    return jnp.broadcast_to(x, shape)


def eliminate(ref):
    width = ref.shape[1]
    lanes = width // BS
    wide = lambda w: jnp.concatenate([w] * lanes, axis=1)
    for base in range(0, BS, 8):
        tile = ref[base : base + 8, :]
        rows = [splat(tile[i : i + 1, :], (8, width)) for i in range(8)]
        cols = [splat(tile[:, base + j : base + j + 1], (8, BS)) for j in range(8)]
        e = [[splat(cols[j][i : i + 1, :], (8, BS)) for j in range(i + 1)] for i in range(8)]
        for j in range(8):
            r = lax.rsqrt(e[j][j])
            rows[j] = rows[j] * wide(r)
            l = [None] * 8
            for i in range(j + 1, 8):
                l[i] = e[i][j] * r
            for i in range(j + 1, 8):
                for m in range(j + 1, i + 1):
                    e[i][m] = e[i][m] - l[i] * l[m]
                rows[i] = rows[i] - wide(l[i]) * rows[j]
        sub = lax.broadcasted_iota(jnp.int32, (8, width), 0)
        out = rows[0]
        for i in range(1, 8):
            out = jnp.where(sub == i, rows[i], out)
        below = lax.broadcasted_iota(jnp.int32, (8, BS), 0) + base
        upper = jnp.where(lax.broadcasted_iota(jnp.int32, (8, BS), 1) >= below, out[:, :BS], 0.0)
        out = jnp.concatenate([upper, out[:, BS:]], axis=1)
        ref[base : base + 8, :] = out
        if base + 8 < BS:
            h, m, l = split3(out)
            left = jnp.concatenate([w[:, :BS] for w in (h, h, m, m, h, l)], axis=0).astype(jnp.bfloat16)
            right = jnp.concatenate([h, m, h, m, l, h], axis=0).astype(jnp.bfloat16)
            d = lax.dot_general(left, right, (((0,), (0,)), ((), ())), preferred_element_type=jnp.float32)
            ref[base + 8 :, :] = ref[base + 8 :, :] - d[base + 8 :, :]


def factor_kernel(place, pair_ref, other_ref, wk_ref, corner_ref, one_ref, two_ref):
    row, col, k = place[0], place[1], place[2]
    rows = BS + 16

    def value(ref, base):
        s = ref[base + BS : base + rows, :].astype(jnp.float32)
        s = s[0:1] + s[1:2] + s[2:3]
        return ref[base : base + BS, :].astype(jnp.float32) * s

    def fill(core0, core1):
        one_ref[:, :BS] = value(core0, 0)
        one_ref[:, BS : 2 * BS] = value(core1, 0).T
        two_ref[:, :BS] = value(core1, rows)

    @pl.when(k == 0)
    def _():
        fill(pair_ref, other_ref)

    @pl.when(k == 1)
    def _():
        fill(other_ref, pair_ref)

    e = lax.broadcasted_iota(jnp.int32, (BS, BS), 0)
    f = lax.broadcasted_iota(jnp.int32, (BS, BS), 1)
    eye = jnp.where(e == f, 1.0, 0.0)
    one_ref[:, 2 * BS :] = eye
    eliminate(one_ref)
    l10t = one_ref[:, BS : 2 * BS].astype(jnp.bfloat16)
    w00 = one_ref[:, 2 * BS :]
    inner = (((0,), (0,)), ((), ()))
    two_ref[:, :BS] = two_ref[:, :BS] - lax.dot_general(l10t, l10t, inner, preferred_element_type=jnp.float32)
    two_ref[:, BS : 2 * BS] = eye
    parts = jnp.concatenate(split3(w00), axis=0).astype(jnp.bfloat16)
    two_ref[:, 2 * BS :] = -lax.dot_general(
        jnp.concatenate([l10t] * 3, axis=0), parts, inner, preferred_element_type=jnp.float32
    )
    eliminate(two_ref)

    def put(h, r, w):
        hi = w.astype(jnp.bfloat16)
        wk_ref[h, r * BS : (r + 1) * BS, :BS] = hi
        wk_ref[h, r * BS : (r + 1) * BS, BS:] = (w - hi.astype(jnp.float32)).astype(jnp.bfloat16)

    put(0, 0, w00)
    put(0, 1, two_ref[:, 2 * BS :])
    put(1, 0, jnp.zeros((BS, BS), jnp.float32))
    put(1, 1, two_ref[:, BS : 2 * BS])

    corner_ref[...] = l10t.astype(jnp.float32)

    @pl.when((row == 0) & (col == 0))
    def _():
        corner_ref[...] = one_ref[:, :BS].T

    @pl.when((row == 1) & (col == 0))
    def _():
        corner_ref[...] = l10t.astype(jnp.float32).T

    @pl.when((row == 1) & (col == 1))
    def _():
        corner_ref[...] = two_ref[:, :BS].T


def factor(place, pair, other):
    return pl.pallas_call(
        factor_kernel,
        grid_spec=pltpu.PrefetchScalarGridSpec(
            num_scalar_prefetch=1,
            in_specs=[pl.BlockSpec(memory_space=pltpu.VMEM)] * 2,
            out_specs=[pl.BlockSpec(memory_space=pltpu.VMEM)] * 2,
            scratch_shapes=[pltpu.VMEM((BS, 3 * BS), jnp.float32)] * 2,
        ),
        out_shape=[
            jax.ShapeDtypeStruct((2, 2 * BS, 2 * BS), jnp.bfloat16),
            jax.ShapeDtypeStruct((BS, BS), jnp.float32),
        ],
        compiler_params=pltpu.CompilerParams(vmem_limit_bytes=16 * 1024 * 1024),
        cost_estimate=pl.CostEstimate(flops=2 * 10**10, bytes_accessed=2**20, transcendentals=0),
        name="factor",
    )(place, pair, other)


def finish_kernel(place, a_ref, sc_ref, m0, m1, m2, m3, t0, t1, t2, t3, u_ref, v_ref, wk_ref, corner_ref,
                  out_ref, big_ref, q_ref, p_ref, prod_ref):
    step = pl.program_id(0)
    row, col, k, z, first = place[0], place[1], place[2], place[3], place[4]

    def scale_of(ref, base, a):
        s = ref[base + 4 * BS : base + 4 * BS + 16, :].astype(jnp.float32)
        return s[3 * a : 3 * a + 1] + s[3 * a + 1 : 3 * a + 2] + s[3 * a + 2 : 3 * a + 3]

    def panel_tiles(ref_m, ref_t, base, a0, wm, wt):
        def part(ref, w):
            raw = ref[base + a0 * BS : base + (a0 + 2) * BS, :]
            d = lax.dot_general(
                jnp.concatenate([raw, raw], axis=1), w, (((1,), (1,)), ((), ())), preferred_element_type=jnp.float32
            )
            out = []
            for a in range(2):
                s = scale_of(ref, base, a0 + a)
                out.append(d[a * BS : (a + 1) * BS] * jnp.concatenate([s, s], axis=1))
            return out

        return [(g + h).astype(jnp.bfloat16) for g, h in zip(part(ref_m, wm), part(ref_t, wt))]

    @pl.when(step == 0)
    def _():
        w_mine = wk_ref[k]
        w_other = wk_ref[1 - k]
        for i, (mine, other) in enumerate(((m0, t0), (m1, t1), (m2, t2), (m3, t3))):
            zs = lax.rem(z + (0, 3, 1, 2)[i], 4)
            for ys in range(2):
                for a0 in range(0, 4, 2):
                    tiles = panel_tiles(mine, other, ys * PIECE, a0, w_mine, w_other)
                    for a, tile in enumerate(tiles):
                        b = (a0 + a) * 8 + zs * 2 + ys
                        q_ref[pl.ds(pl.multiple_of(b * BS, BS), BS), :] = tile
        w_u = wk_ref[first]
        w_v = wk_ref[1 - first]
        for a0 in range(0, 4, 2):
            for a, tile in enumerate(panel_tiles(u_ref, v_ref, 0, a0, w_u, w_v)):
                p_ref[(a0 + a) * BS : (a0 + a + 1) * BS, :] = tile
        e = lax.broadcasted_iota(jnp.int32, (BS, 2 * BS), 0)
        f = lax.broadcasted_iota(jnp.int32, (BS, 2 * BS), 1)

        @pl.when(row < 2)
        def _():
            p_ref[0:BS, :] = jnp.where(f == e + row * BS, -1.0, 0.0).astype(jnp.bfloat16)

        @pl.when(col < 2)
        def _():
            q_ref[0:BS, :] = jnp.where(f == e + col * BS, -1.0, 0.0).astype(jnp.bfloat16)

    p = p_ref[pl.ds(pl.multiple_of(step * BS, BS), BS), :]
    for b in range(32):
        d = lax.dot_general(
            p, q_ref[b * BS : (b + 1) * BS, :], (((1,), (1,)), ((), ())), preferred_element_type=jnp.float32
        )
        prod_ref[pl.ds(b, BS, stride=40), :] = d

    @pl.when((step == 0) & (row < 2) & (col < 2))
    def _():
        prod_ref[pl.ds(0, BS, stride=40), :] = -corner_ref[...]

    sc = sc_ref[0]

    def update(e, mx):
        rows = pl.ds(pl.multiple_of(e * 40, 8), 32)
        m = a_ref[0, e].astype(jnp.float32) * sc - prod_ref[rows, :]
        prod_ref[rows, :] = m
        return jnp.maximum(mx, jnp.abs(m))

    mx = lax.fori_loop(0, BS, update, jnp.zeros((32, BS), jnp.float32), unroll=8)
    big = jnp.max(mx, axis=1, keepdims=True) + 1e-06
    big = jnp.broadcast_to(big, (32, BS))
    big_ref[0] = big
    inv = 1.0 / big

    def divide(e, carry):
        rows = pl.ds(pl.multiple_of(e * 40, 8), 32)
        out_ref[0, e] = (prod_ref[rows, :] * inv).astype(jnp.bfloat16)
        return carry

    lax.fori_loop(0, BS, divide, 0, unroll=8)


def finish(place, blocks, sc, held, others, u, v, wk, corner):
    whole = lambda shape: pl.BlockSpec(shape, lambda a, *_: (0,) * len(shape))
    spec = pltpu.PrefetchScalarGridSpec(
        num_scalar_prefetch=1,
        grid=(4,),
        in_specs=[
            pl.BlockSpec((1, BS, 32, BS), lambda a, *_: (a, 0, 0, 0)),
            pl.BlockSpec((1, 32, BS), lambda a, *_: (a, 0, 0)),
        ]
        + [whole((2 * PIECE, BS))] * 8
        + [whole((PIECE, BS))] * 2
        + [whole((2, 2 * BS, 2 * BS)), whole((BS, BS))],
        out_specs=[
            pl.BlockSpec((1, BS, 32, BS), lambda a, *_: (a, 0, 0, 0)),
            pl.BlockSpec((1, 32, BS), lambda a, *_: (a, 0, 0)),
        ],
        scratch_shapes=[
            pltpu.VMEM((32 * BS, 2 * BS), jnp.bfloat16),
            pltpu.VMEM((4 * BS, 2 * BS), jnp.bfloat16),
            pltpu.VMEM((40 * BS, BS), jnp.float32),
        ],
    )
    return pl.pallas_call(
        finish_kernel,
        grid_spec=spec,
        out_shape=[
            jax.ShapeDtypeStruct((4, BS, 32, BS), jnp.bfloat16),
            jax.ShapeDtypeStruct((4, 32, BS), jnp.float32),
        ],
        compiler_params=pltpu.CompilerParams(vmem_limit_bytes=32 * 1024 * 1024),
        cost_estimate=pl.CostEstimate(flops=2 * 512 * 4096 * 512, bytes_accessed=12 * 2**20, transcendentals=0),
        name="finish",
    )(place, blocks, sc, *held, *others, u, v, wk, corner)


def on_device(blocks, scales):
    row = lax.axis_index("row")
    col = lax.axis_index("col")
    x = col
    k = row % 2
    y = (row // 2) % 4
    z = row // 8
    blocks = blocks.reshape(4, BS, 32, BS)
    scales = scales.reshape(4, 32)
    srows = scale_rows(scales[:, 0])
    strip = blocks[:, :, 0, :]
    piece = jnp.concatenate([strip.reshape(4 * BS, BS), srows], axis=0)
    first = jnp.where((x == 0) | (x == 3), 0, 1)
    place = jnp.stack([row, col, k, z, first]).astype(jnp.int32)
    u, v = along_x(piece, x)
    pair = leading_pair(u, v, first, z, y)
    both = column_strips(u, v, first, y, k, x)
    pair, both = lax.optimization_barrier((pair, both))
    held = [both] + [shift(both, dz=d) for d in (1, -1, 2)]
    wk, corner = factor(place, pair, shift(pair, dk=1))
    wk, *held[1:] = lax.optimization_barrier((wk, *held[1:]))
    others = [shift(h, dk=1) for h in held]
    special = ((jnp.arange(4) == 0) & (row < 2))[:, None] | ((jnp.arange(32) == 0) & (col < 2))[None, :]
    sc = jnp.broadcast_to(jnp.where(special, 0.0, scales)[:, :, None], (4, 32, BS))
    factored, largest = finish(place, blocks, sc, held, others, u, v, wk, corner)
    return factored.reshape(4, 1, BS, 32, 1, BS), largest[:, None, :, :1]


def solution(mesh):
    in_specs = (P(None, "row", None, None, "col", None), P(None, "row", None, "col"))
    out_specs = (P(None, "row", None, None, "col", None), P(None, "row", None, "col"))
    return jax.shard_map(
        on_device, mesh=mesh, in_specs=in_specs, out_specs=out_specs, check_vma=False
    )
```

time: 121 us -> 72 us (0.60)
  other arithmetic: 48.6 us -> 1.33 us
  Pallas kernels: 12.9 us -> 21.5 us
  local copies, waits for them, and re-layouts: 6.17 us -> 2.34 us
  starting transfers between devices: 38.7 us -> 34.9 us
  matrix products: 2.17 us -> 0 us
    another operation x10 -> x1, other arithmetic: 46 us -> 0.69 us  [the longest x3 20.4 us: factor(): lax.linalg.triangular_solve(l, eye, left_side=True, lower=True)]
    pallas_call x0 -> x1, Pallas kernels: none -> 12.7 us  [factor(): pl.pallas_call(factor_kernel, grid_spec=pltpu.PrefetchScalarGridSpec(num_...]
    ppermute x6 -> x3, waiting for transfers between devices: 0.02 us -> 5.25 us  [along_x(): got.append(lax.ppermute(array, AXES, table))]
    ppermute x17 -> x18, waiting for transfers between devices: 10.3 us -> 5.21 us  [shift(): return lax.ppermute(array, AXES, pairs)]
    ppermute x6 -> x3, starting transfers between devices: 12.2 us -> 7.45 us  [along_x(): got.append(lax.ppermute(array, AXES, table))]
    ppermute x17 -> x18, starting transfers between devices: 23 us -> 27.4 us  [shift(): return lax.ppermute(array, AXES, pairs)]
    pallas_call x1, Pallas kernels: 12.9 us -> 8.75 us  [finish(): pl.pallas_call(finish_kernel, grid_spec=spec, out_shape=[jax.ShapeDtypeSt...]
    ppermute x1 -> x0, starting transfers between devices: 3.46 us -> none  [column_pieces(): mine = lax.ppermute(piece, AXES, table)]
  transfers between devices with their start and end apart: 24 -> 21, of which waited for: 5 -> 8; matrix products, arithmetic and copies ran while one was open for 43% -> 0% of each run, Pallas kernels for 0% -> 18%
where the time goes in v2:
time: 72 us; the launch traced here: 71.6 us
  starting transfers between devices  34.9 us (48%)
  Pallas kernels  21.5 us (30%)
  waiting for transfers between devices  10.5 us (15%)
  local copies, waits for them, and re-layouts  2.34 us (3%)
  other arithmetic  1.33 us (2%)
  between operations  1.09 us (2%)
    ppermute x18, starting transfers between devices, shift(): return lax.ppermute(array, AXES, pairs)  27.4 us
    pallas_call x1, Pallas kernels, factor(): pl.pallas_call(factor_kernel, grid_spec=pltpu.PrefetchScalarGridSpec(num_...  12.7 us
    pallas_call x1, Pallas kernels, finish(): pl.pallas_call(finish_kernel, grid_spec=spec, out_shape=[jax.ShapeDtypeSt...  8.75 us
    ppermute x3, starting transfers between devices, along_x(): got.append(lax.ppermute(array, AXES, table))  7.45 us
    ppermute x3, waiting for transfers between devices, along_x(): got.append(lax.ppermute(array, AXES, table))  5.25 us
    ppermute x18, waiting for transfers between devices, shift(): return lax.ppermute(array, AXES, pairs)  5.21 us
  transfers between devices with their start and end apart: 21, of which 8 were waited for; matrix products, arithmetic and copies ran while one was open for 0% of the time, Pallas kernels for 18%

profile of v2, /device:TPU:1, one launch (start us, length us, event | category | flops | bytes accessed | tf_op | source)
XLA Modules:
  0.0 71.6 jit_solution(14028608791936892897)
XLA Ops:
  0.6 0.7 reduce-precision_convert_fusion.1
  1.5 1.4 %slice.32 = bf16[4,128,1,128]{3,2,1,0:T(2,128)(2,1)S(1)} slice(bf16[4,128,32,128]{3,2,1,0:T(8,128)(2,1)} %bitcast.16), slice={[0:4], [0:128], [0:1], [0:128]} | slice | bytes 262144 | tf_op jit(solution)/shard_map/slice | solution.py:327
  2.9 0.1 pad_maximum_fusion.1
  3.0 3.9 %collective-permute-start.1 = (bf16[528,128]{1,0:T(8,128)(2,1)S(1)}, bf16[528,128]{1,0:T(8,128)(2,1)S(1)}, u32[]{:S(2)}, u32[]{:S(2)}) collective-permute-start(bf16[528,128]{1,0:T(8,128)(2,1)S(1)} %pad_maximum_fusion.1), channel_id=1, source_target_pairs={{0,1},{1,0},{4,5},{5,4},{8,9},{9,8},{12,13},{13,12},{16,17},{17,16... | collective-permute-start | bytes 405512 | tf_op jit(solution)/shard_map/ppermute | solution.py:42
  7.0 2.2 %collective-permute-start.2 = (bf16[528,128]{1,0:T(8,128)(2,1)S(1)}, bf16[528,128]{1,0:T(8,128)(2,1)S(1)}, u32[]{:S(2)}, u32[]{:S(2)}) collective-permute-start(bf16[528,128]{1,0:T(8,128)(2,1)S(1)} %pad_maximum_fusion.1), channel_id=1, source_target_pairs={{0,2},{1,3},{4,6},{5,7},{8,10},{9,11},{12,14},{13,15},{16,18},{17,... | collective-permute-start | bytes 405512 | tf_op jit(solution)/shard_map/ppermute | solution.py:42
  9.2 1.3 %collective-permute-start = (bf16[528,128]{1,0:T(8,128)(2,1)S(1)}, bf16[528,128]{1,0:T(8,128)(2,1)S(1)}, u32[]{:S(2)}, u32[]{:S(2)}) collective-permute-start(bf16[528,128]{1,0:T(8,128)(2,1)S(1)} %pad_maximum_fusion.1), channel_id=1, source_target_pairs={{0,3},{1,2},{4,7},{5,6},{8,11},{9,10},{12,15},{13,14},{16,19},{17,... | collective-permute-start | bytes 405512 | tf_op jit(solution)/shard_map/ppermute | solution.py:42
  10.6 2.1 %collective-permute-done.2 = bf16[528,128]{1,0:T(8,128)(2,1)S(1)} collective-permute-done((bf16[528,128]{1,0:T(8,128)(2,1)S(1)}, bf16[528,128]{1,0:T(8,128)(2,1)S(1)}, u32[]{:S(2)}, u32[]{:S(2)}) %collective-permute-start.2) | collective-permute-done | bytes 135200 | tf_op jit(solution)/shard_map/ppermute | solution.py:42
  12.6 3.2 %collective-permute-done = bf16[528,128]{1,0:T(8,128)(2,1)S(1)} collective-permute-done((bf16[528,128]{1,0:T(8,128)(2,1)S(1)}, bf16[528,128]{1,0:T(8,128)(2,1)S(1)}, u32[]{:S(2)}, u32[]{:S(2)}) %collective-permute-start) | collective-permute-done | bytes 135200 | tf_op jit(solution)/shard_map/ppermute | solution.py:42
  15.8 0.1 broadcast_select_fusion
  16.0 5.1 %collective-permute-start.5 = (bf16[288,128]{1,0:T(8,128)(2,1)S(1)}, bf16[288,128]{1,0:T(8,128)(2,1)S(1)}, u32[]{:S(2)}, u32[]{:S(2)}) collective-permute-start(bf16[288,128]{1,0:T(8,128)(2,1)S(1)} %pad_maximum_fusion.2), channel_id=1, source_target_pairs={{0,16},{1,17},{2,18},{3,19},{4,20},{5,21},{6,22},{7,23}} | collective-permute-start | bytes 221192 | tf_op jit(solution)/shard_map/ppermute | solution.py:25
  21.1 1.3 %collective-permute-start.4 = (bf16[288,128]{1,0:T(8,128)(2,1)S(1)}, bf16[288,128]{1,0:T(8,128)(2,1)S(1)}, u32[]{:S(2)}, u32[]{:S(2)}) collective-permute-start(bf16[288,128]{1,0:T(8,128)(2,1)S(1)} %pad_maximum_fusion.2), channel_id=1, source_target_pairs={{0,24},{1,25},{2,26},{3,27},{4,28},{5,29},{6,30},{7,31}} | collective-permute-start | bytes 221192 | tf_op jit(solution)/shard_map/ppermute | solution.py:25
  22.4 1.3 %collective-permute-start.3 = (bf16[288,128]{1,0:T(8,128)(2,1)S(1)}, bf16[288,128]{1,0:T(8,128)(2,1)S(1)}, u32[]{:S(2)}, u32[]{:S(2)}) collective-permute-start(bf16[288,128]{1,0:T(8,128)(2,1)S(1)} %pad_maximum_fusion.2), channel_id=1, source_target_pairs={{0,8},{1,9},{2,10},{3,11},{4,12},{5,13},{6,14},{7,15}} | collective-permute-start | bytes 221192 | tf_op jit(solution)/shard_map/ppermute | solution.py:25
  23.9 1.3 %collective-permute-start.9 = (bf16[528,128]{1,0:T(8,128)(2,1)S(1)}, bf16[528,128]{1,0:T(8,128)(2,1)S(1)}, u32[]{:S(2)}, u32[]{:S(2)}) collective-permute-start(bf16[528,128]{1,0:T(8,128)(2,1)S(1)} %get-tuple-element.26), channel_id=1, source_target_pairs={{0,4},{5,1},{10,14},{15,11},{16,20},{21,17},{26,30},{31,27},{32,36... | collective-permute-start | bytes 405512 | tf_op jit(solution)/shard_map/ppermute | solution.py:25
  25.3 1.3 %collective-permute-start.8 = (bf16[288,128]{1,0:T(8,128)(2,1)S(1)}, bf16[288,128]{1,0:T(8,128)(2,1)S(1)}, u32[]{:S(2)}, u32[]{:S(2)}) collective-permute-start(bf16[288,128]{1,0:T(8,128)(2,1)S(1)} %select_select_fusion.4), channel_id=1, source_target_pairs={{0,64},{1,65},{2,66},{3,67},{4,68},{5,69},{6,70},{7,71},{8,72},{9,... | collective-permute-start | bytes 221192 | tf_op jit(solution)/shard_map/ppermute | solution.py:25
  26.6 1.3 %collective-permute-start.7 = (bf16[288,128]{1,0:T(8,128)(2,1)S(1)}, bf16[288,128]{1,0:T(8,128)(2,1)S(1)}, u32[]{:S(2)}, u32[]{:S(2)}) collective-permute-start(bf16[288,128]{1,0:T(8,128)(2,1)S(1)} %select_select_fusion.4), channel_id=1, source_target_pairs={{0,96},{1,97},{2,98},{3,99},{4,100},{5,101},{6,102},{7,103},{8,104... | collective-permute-start | bytes 221192 | tf_op jit(solution)/shard_map/ppermute | solution.py:25
  27.9 1.3 %collective-permute-start.6 = (bf16[288,128]{1,0:T(8,128)(2,1)S(1)}, bf16[288,128]{1,0:T(8,128)(2,1)S(1)}, u32[]{:S(2)}, u32[]{:S(2)}) collective-permute-start(bf16[288,128]{1,0:T(8,128)(2,1)S(1)} %select_select_fusion.4), channel_id=1, source_target_pairs={{0,32},{1,33},{2,34},{3,35},{4,36},{5,37},{6,38},{7,39},{8,40},{9,... | collective-permute-start | bytes 221192 | tf_op jit(solution)/shard_map/ppermute | solution.py:25
  29.2 3.5 %collective-permute-start.12 = (bf16[528,128]{1,0:T(8,128)(2,1)S(1)}, bf16[528,128]{1,0:T(8,128)(2,1)S(1)}, u32[]{:S(2)}, u32[]{:S(2)}) collective-permute-start(bf16[528,128]{1,0:T(8,128)(2,1)S(1)} %select_select_fusion.2), channel_id=1, source_target_pairs={{0,24},{1,25},{4,28},{5,29},{10,2},{11,3},{14,6},{15,7},{16,8},{17... | collective-permute-start | bytes 405512 | tf_op jit(solution)/shard_map/ppermute | solution.py:25
  32.7 3.8 %collective-permute-start.11 = (bf16[528,128]{1,0:T(8,128)(2,1)S(1)}, bf16[528,128]{1,0:T(8,128)(2,1)S(1)}, u32[]{:S(2)}, u32[]{:S(2)}) collective-permute-start(bf16[528,128]{1,0:T(8,128)(2,1)S(1)} %select_select_fusion.2), channel_id=1, source_target_pairs={{0,16},{1,17},{4,20},{5,21},{10,26},{11,27},{14,30},{15,31},{16,0}... | collective-permute-start | bytes 405512 | tf_op jit(solution)/shard_map/ppermute | solution.py:25
  36.5 1.3 %collective-permute-start.10 = (bf16[528,128]{1,0:T(8,128)(2,1)S(1)}, bf16[528,128]{1,0:T(8,128)(2,1)S(1)}, u32[]{:S(2)}, u32[]{:S(2)}) collective-permute-start(bf16[528,128]{1,0:T(8,128)(2,1)S(1)} %select_select_fusion.2), channel_id=1, source_target_pairs={{0,8},{1,9},{4,12},{5,13},{10,18},{11,19},{14,22},{15,23},{16,24},... | collective-permute-start | bytes 405512 | tf_op jit(solution)/shard_map/ppermute | solution.py:25
  37.9 2.1 %collective-permute-done.11 = bf16[528,128]{1,0:T(8,128)(2,1)S(1)} collective-permute-done((bf16[528,128]{1,0:T(8,128)(2,1)S(1)}, bf16[528,128]{1,0:T(8,128)(2,1)S(1)}, u32[]{:S(2)}, u32[]{:S(2)}) %collective-permute-start.11) | collective-permute-done | bytes 135200 | tf_op jit(solution)/shard_map/ppermute | solution.py:25
  40.0 0.4 collective-permute-done.10
  40.4 3.3 %collective-permute-start.13 = (bf16[288,128]{1,0:T(8,128)(2,1)S(1)}, bf16[288,128]{1,0:T(8,128)(2,1)S(1)}, u32[]{:S(2)}, u32[]{:S(2)}) collective-permute-start(bf16[288,128]{1,0:T(8,128)(2,1)S(1)} %select_select_fusion.3.pair_ref), channel_id=1, source_target_pairs={{0,4},{1,5},{2,6},{3,7},{4,0},{5,1},{6,2},{7,3},{8,12},{9,13},{10,... | collective-permute-start | bytes 221192 | tf_op jit(solution)/shard_map/ppermute | solution.py:25
  44.0 1.5 %collective-permute-start.14 = (bf16[1056,128]{1,0:T(8,128)(2,1)S(1)}, bf16[1056,128]{1,0:T(8,128)(2,1)S(1)}, u32[]{:S(2)}, u32[]{:S(2)}) collective-permute-start(bf16[1056,128]{1,0:T(8,128)(2,1)S(1)} %pad_maximum_fusion.m0), channel_id=1, source_target_pairs={{0,32},{1,33},{2,34},{3,35},{4,36},{5,37},{6,38},{7,39},{8,40},{9,... | collective-permute-start | bytes 811016 | tf_op jit(solution)/shard_map/ppermute | solution.py:25
  45.5 12.7 %factor.1 = (bf16[2,256,256]{2,1,0:T(8,128)(2,1)S(1)}, f32[128,128]{1,0:T(8,128)S(1)}) custom-call(s32[5]{0:T(128)S(1)} %stack.30.place, bf16[288,128]{1,0:T(8,128)(2,1)S(1)} %select_select_fusion.3.pair_ref, bf16[288,128]{1,0:T(8,128)(2,1)S(1)} %collective-permute-done.13.other_ref), custom_call_target="tpu_custom_call" | custom-call | flops 20000000000 | bytes 1048576 | tf_op jit(solution)/shard_map/factor/pallas_call | solution.py:180
  58.2 1.4 %collective-permute-done.14.m1 = bf16[1056,128]{1,0:T(8,128)(2,1)S(1)} collective-permute-done((bf16[1056,128]{1,0:T(8,128)(2,1)S(1)}, bf16[1056,128]{1,0:T(8,128)(2,1)S(1)}, u32[]{:S(2)}, u32[]{:S(2)}) %collective-permute-start.14) | collective-permute-done | bytes 270368 | tf_op jit(solution)/shard_map/ppermute | solution.py:25
  59.6 0.5 collective-permute-start.18
  60.1 0.5 collective-permute-start.20
  60.7 0.6 collective-permute-done.18.t1
  61.3 0.4 collective-permute-done.19.t2
  61.7 0.4 collective-permute-done.20.t3
  62.2 8.7 %finish.1 = (bf16[4,128,32,128]{3,2,1,0:T(8,128)(2,1)}, f32[4,32,128]{2,1,0:T(8,128)S(1)}) custom-call(s32[5]{0:T(128)S(1)} %stack.30.place, bf16[4,128,32,128]{3,2,1,0:T(8,128)(2,1)S(1)} %bitcast.17, f32[4,32,128]{2,1,0:T(8,128)S(1)} %broadcast_in_dim.11.sc_ref, bf16[1056,128]{1,0:T(8,128)(2,1)S(1)} %pad_maximum_fusion.m0, ...), custom_call_target="tpu_custom_call" | custom-call | flops 2147483648 | bytes 12582912 | tf_op jit(solution)/shard_map/finish/pallas_call | solution.py:304
  70.9 0.7 slice_reduce_fusion
  (42 shorter events, 1.0 us)
Async XLA Ops:
  3.0 7.5 %collective-permute-start.1 = (bf16[528,128]{1,0:T(8,128)(2,1)S(1)}, bf16[528,128]{1,0:T(8,128)(2,1)S(1)}, u32[]{:S(2)}, u32[]{:S(2)}) collective-permute-start(bf16[528,128]{1,0:T(8,128)(2,1)S(1)} %pad_maximum_fusion.1), channel_id=1, source_target_pairs={{0,1},{1,0},{4,5},{5,4},{8,9},{9,8},{12,13},{13,12},{16,17},{17,16... | collective-permute-start | bytes 405512 | tf_op jit(solution)/shard_map/ppermute | solution.py:42
  7.0 5.6 %collective-permute-start.2 = (bf16[528,128]{1,0:T(8,128)(2,1)S(1)}, bf16[528,128]{1,0:T(8,128)(2,1)S(1)}, u32[]{:S(2)}, u32[]{:S(2)}) collective-permute-start(bf16[528,128]{1,0:T(8,128)(2,1)S(1)} %pad_maximum_fusion.1), channel_id=1, source_target_pairs={{0,2},{1,3},{4,6},{5,7},{8,10},{9,11},{12,14},{13,15},{16,18},{17,... | collective-permute-start | bytes 405512 | tf_op jit(solution)/shard_map/ppermute | solution.py:42
  9.2 6.6 %collective-permute-start = (bf16[528,128]{1,0:T(8,128)(2,1)S(1)}, bf16[528,128]{1,0:T(8,128)(2,1)S(1)}, u32[]{:S(2)}, u32[]{:S(2)}) collective-permute-start(bf16[528,128]{1,0:T(8,128)(2,1)S(1)} %pad_maximum_fusion.1), channel_id=1, source_target_pairs={{0,3},{1,2},{4,7},{5,6},{8,11},{9,10},{12,15},{13,14},{16,19},{17,... | collective-permute-start | bytes 405512 | tf_op jit(solution)/shard_map/ppermute | solution.py:42
  16.0 9.2 %collective-permute-start.5 = (bf16[288,128]{1,0:T(8,128)(2,1)S(1)}, bf16[288,128]{1,0:T(8,128)(2,1)S(1)}, u32[]{:S(2)}, u32[]{:S(2)}) collective-permute-start(bf16[288,128]{1,0:T(8,128)(2,1)S(1)} %pad_maximum_fusion.2), channel_id=1, source_target_pairs={{0,16},{1,17},{2,18},{3,19},{4,20},{5,21},{6,22},{7,23}} | collective-permute-start | bytes 221192 | tf_op jit(solution)/shard_map/ppermute | solution.py:25
  21.1 4.1 %collective-permute-start.4 = (bf16[288,128]{1,0:T(8,128)(2,1)S(1)}, bf16[288,128]{1,0:T(8,128)(2,1)S(1)}, u32[]{:S(2)}, u32[]{:S(2)}) collective-permute-start(bf16[288,128]{1,0:T(8,128)(2,1)S(1)} %pad_maximum_fusion.2), channel_id=1, source_target_pairs={{0,24},{1,25},{2,26},{3,27},{4,28},{5,29},{6,30},{7,31}} | collective-permute-start | bytes 221192 | tf_op jit(solution)/shard_map/ppermute | solution.py:25
  22.4 2.8 %collective-permute-start.3 = (bf16[288,128]{1,0:T(8,128)(2,1)S(1)}, bf16[288,128]{1,0:T(8,128)(2,1)S(1)}, u32[]{:S(2)}, u32[]{:S(2)}) collective-permute-start(bf16[288,128]{1,0:T(8,128)(2,1)S(1)} %pad_maximum_fusion.2), channel_id=1, source_target_pairs={{0,8},{1,9},{2,10},{3,11},{4,12},{5,13},{6,14},{7,15}} | collective-permute-start | bytes 221192 | tf_op jit(solution)/shard_map/ppermute | solution.py:25
  23.9 5.3 %collective-permute-start.9 = (bf16[528,128]{1,0:T(8,128)(2,1)S(1)}, bf16[528,128]{1,0:T(8,128)(2,1)S(1)}, u32[]{:S(2)}, u32[]{:S(2)}) collective-permute-start(bf16[528,128]{1,0:T(8,128)(2,1)S(1)} %get-tuple-element.26), channel_id=1, source_target_pairs={{0,4},{5,1},{10,14},{15,11},{16,20},{21,17},{26,30},{31,27},{32,36... | collective-permute-start | bytes 405512 | tf_op jit(solution)/shard_map/ppermute | solution.py:25
  25.3 11.2 %collective-permute-start.8 = (bf16[288,128]{1,0:T(8,128)(2,1)S(1)}, bf16[288,128]{1,0:T(8,128)(2,1)S(1)}, u32[]{:S(2)}, u32[]{:S(2)}) collective-permute-start(bf16[288,128]{1,0:T(8,128)(2,1)S(1)} %select_select_fusion.4), channel_id=1, source_target_pairs={{0,64},{1,65},{2,66},{3,67},{4,68},{5,69},{6,70},{7,71},{8,72},{9,... | collective-permute-start | bytes 221192 | tf_op jit(solution)/shard_map/ppermute | solution.py:25
  26.6 11.3 %collective-permute-start.7 = (bf16[288,128]{1,0:T(8,128)(2,1)S(1)}, bf16[288,128]{1,0:T(8,128)(2,1)S(1)}, u32[]{:S(2)}, u32[]{:S(2)}) collective-permute-start(bf16[288,128]{1,0:T(8,128)(2,1)S(1)} %select_select_fusion.4), channel_id=1, source_target_pairs={{0,96},{1,97},{2,98},{3,99},{4,100},{5,101},{6,102},{7,103},{8,104... | collective-permute-start | bytes 221192 | tf_op jit(solution)/shard_map/ppermute | solution.py:25
  27.9 10.0 %collective-permute-start.6 = (bf16[288,128]{1,0:T(8,128)(2,1)S(1)}, bf16[288,128]{1,0:T(8,128)(2,1)S(1)}, u32[]{:S(2)}, u32[]{:S(2)}) collective-permute-start(bf16[288,128]{1,0:T(8,128)(2,1)S(1)} %select_select_fusion.4), channel_id=1, source_target_pairs={{0,32},{1,33},{2,34},{3,35},{4,36},{5,37},{6,38},{7,39},{8,40},{9,... | collective-permute-start | bytes 221192 | tf_op jit(solution)/shard_map/ppermute | solution.py:25
  29.2 8.7 %collective-permute-start.12 = (bf16[528,128]{1,0:T(8,128)(2,1)S(1)}, bf16[528,128]{1,0:T(8,128)(2,1)S(1)}, u32[]{:S(2)}, u32[]{:S(2)}) collective-permute-start(bf16[528,128]{1,0:T(8,128)(2,1)S(1)} %select_select_fusion.2), channel_id=1, source_target_pairs={{0,24},{1,25},{4,28},{5,29},{10,2},{11,3},{14,6},{15,7},{16,8},{17... | collective-permute-start | bytes 405512 | tf_op jit(solution)/shard_map/ppermute | solution.py:25
  32.7 7.3 %collective-permute-start.11 = (bf16[528,128]{1,0:T(8,128)(2,1)S(1)}, bf16[528,128]{1,0:T(8,128)(2,1)S(1)}, u32[]{:S(2)}, u32[]{:S(2)}) collective-permute-start(bf16[528,128]{1,0:T(8,128)(2,1)S(1)} %select_select_fusion.2), channel_id=1, source_target_pairs={{0,16},{1,17},{4,20},{5,21},{10,26},{11,27},{14,30},{15,31},{16,0}... | collective-permute-start | bytes 405512 | tf_op jit(solution)/shard_map/ppermute | solution.py:25
  36.5 3.8 %collective-permute-start.10 = (bf16[528,128]{1,0:T(8,128)(2,1)S(1)}, bf16[528,128]{1,0:T(8,128)(2,1)S(1)}, u32[]{:S(2)}, u32[]{:S(2)}) collective-permute-start(bf16[528,128]{1,0:T(8,128)(2,1)S(1)} %select_select_fusion.2), channel_id=1, source_target_pairs={{0,8},{1,9},{4,12},{5,13},{10,18},{11,19},{14,22},{15,23},{16,24},... | collective-permute-start | bytes 405512 | tf_op jit(solution)/shard_map/ppermute | solution.py:25
  40.4 5.1 %collective-permute-start.13 = (bf16[288,128]{1,0:T(8,128)(2,1)S(1)}, bf16[288,128]{1,0:T(8,128)(2,1)S(1)}, u32[]{:S(2)}, u32[]{:S(2)}) collective-permute-start(bf16[288,128]{1,0:T(8,128)(2,1)S(1)} %select_select_fusion.3.pair_ref), channel_id=1, source_target_pairs={{0,4},{1,5},{2,6},{3,7},{4,0},{5,1},{6,2},{7,3},{8,12},{9,13},{10,... | collective-permute-start | bytes 221192 | tf_op jit(solution)/shard_map/ppermute | solution.py:25
  43.7 16.9 %copy-start.1 = (f32[4,1,32,1]{2,3,1,0:T(1,128)S(1)}, f32[4,1,32,1]{2,3,1,0:T(1,128)}, u32[]{:S(2)}) copy-start(f32[4,1,32,1]{2,3,1,0:T(1,128)} %param.3) | copy-start | bytes 1540
  43.7 18.4 %copy-start = (bf16[4,1,128,32,1,128]{5,3,4,2,1,0:T(8,128)(2,1)S(1)}, bf16[4,1,128,32,1,128]{5,3,4,2,1,0:T(8,128)(2,1)}, u32[]{:S(2)}) copy-start(bf16[4,1,128,32,1,128]{5,3,4,2,1,0:T(8,128)(2,1)} %param.2) | copy-start | bytes 12582916
  43.8 17.0 %collective-permute-start.17 = (bf16[1056,128]{1,0:T(8,128)(2,1)S(1)}, bf16[1056,128]{1,0:T(8,128)(2,1)S(1)}, u32[]{:S(2)}, u32[]{:S(2)}) collective-permute-start(bf16[1056,128]{1,0:T(8,128)(2,1)S(1)} %pad_maximum_fusion.m0), channel_id=1, source_target_pairs={{0,4},{1,5},{2,6},{3,7},{4,0},{5,1},{6,2},{7,3},{8,12},{9,13},{10,... | collective-permute-start | bytes 811016 | tf_op jit(solution)/shard_map/ppermute | solution.py:25
  43.9 14.4 %collective-permute-start.16 = (bf16[1056,128]{1,0:T(8,128)(2,1)S(1)}, bf16[1056,128]{1,0:T(8,128)(2,1)S(1)}, u32[]{:S(2)}, u32[]{:S(2)}) collective-permute-start(bf16[1056,128]{1,0:T(8,128)(2,1)S(1)} %pad_maximum_fusion.m0), channel_id=1, source_target_pairs={{0,64},{1,65},{2,66},{3,67},{4,68},{5,69},{6,70},{7,71},{8,72},{9,... | collective-permute-start | bytes 811016 | tf_op jit(solution)/shard_map/ppermute | solution.py:25
  43.9 14.3 %collective-permute-start.15 = (bf16[1056,128]{1,0:T(8,128)(2,1)S(1)}, bf16[1056,128]{1,0:T(8,128)(2,1)S(1)}, u32[]{:S(2)}, u32[]{:S(2)}) collective-permute-start(bf16[1056,128]{1,0:T(8,128)(2,1)S(1)} %pad_maximum_fusion.m0), channel_id=1, source_target_pairs={{0,96},{1,97},{2,98},{3,99},{4,100},{5,101},{6,102},{7,103},{8,104... | collective-permute-start | bytes 811016 | tf_op jit(solution)/shard_map/ppermute | solution.py:25
  44.0 15.6 %collective-permute-start.14 = (bf16[1056,128]{1,0:T(8,128)(2,1)S(1)}, bf16[1056,128]{1,0:T(8,128)(2,1)S(1)}, u32[]{:S(2)}, u32[]{:S(2)}) collective-permute-start(bf16[1056,128]{1,0:T(8,128)(2,1)S(1)} %pad_maximum_fusion.m0), channel_id=1, source_target_pairs={{0,32},{1,33},{2,34},{3,35},{4,36},{5,37},{6,38},{7,39},{8,40},{9,... | collective-permute-start | bytes 811016 | tf_op jit(solution)/shard_map/ppermute | solution.py:25
  59.6 1.7 %collective-permute-start.18 = (bf16[1056,128]{1,0:T(8,128)(2,1)S(1)}, bf16[1056,128]{1,0:T(8,128)(2,1)S(1)}, u32[]{:S(2)}, u32[]{:S(2)}) collective-permute-start(bf16[1056,128]{1,0:T(8,128)(2,1)S(1)} %collective-permute-done.14.m1), channel_id=1, source_target_pairs={{0,4},{1,5},{2,6},{3,7},{4,0},{5,1},{6,2},{7,3},{8,12},{9,13},{10,... | collective-permute-start | bytes 811016 | tf_op jit(solution)/shard_map/ppermute | solution.py:25
  60.1 1.6 %collective-permute-start.19 = (bf16[1056,128]{1,0:T(8,128)(2,1)S(1)}, bf16[1056,128]{1,0:T(8,128)(2,1)S(1)}, u32[]{:S(2)}, u32[]{:S(2)}) collective-permute-start(bf16[1056,128]{1,0:T(8,128)(2,1)S(1)} %collective-permute-done.15.m2), channel_id=1, source_target_pairs={{0,4},{1,5},{2,6},{3,7},{4,0},{5,1},{6,2},{7,3},{8,12},{9,13},{10,... | collective-permute-start | bytes 811016 | tf_op jit(solution)/shard_map/ppermute | solution.py:25
  60.1 1.9 %collective-permute-start.20 = (bf16[1056,128]{1,0:T(8,128)(2,1)S(1)}, bf16[1056,128]{1,0:T(8,128)(2,1)S(1)}, u32[]{:S(2)}, u32[]{:S(2)}) collective-permute-start(bf16[1056,128]{1,0:T(8,128)(2,1)S(1)} %collective-permute-done.16.m3), channel_id=1, source_target_pairs={{0,4},{1,5},{2,6},{3,7},{4,0},{5,1},{6,2},{7,3},{8,12},{9,13},{10,... | collective-permute-start | bytes 811016 | tf_op jit(solution)/shard_map/ppermute | solution.py:25

commit v3 on v2

--- a/solution.py
+++ b/solution.py
@@ -18,54 +18,83 @@
 PLACES = [(z, y, k, x) for z in range(NZ) for y in range(NY) for k in range(NK) for x in range(NX)]
 
 
-def shift(array, dz=0, dy=0, dk=0, dx=0, where=lambda z, y, k, x: True):
-    pairs = [
-        (dev(z, y, k, x), dev(z + dz, y + dy, k + dk, x + dx)) for z, y, k, x in PLACES if where(z, y, k, x)
+def permute(array, to):
+    return lax.ppermute(array, AXES, [(dev(*place), dev(*to(*place))) for place in PLACES])
+
+
+def sibling(z, y, k, x):
+    return z, y, 1 - k, x
+
+
+def strip_kernel(blocks_ref, scales_ref, piece_ref):
+    sub = lax.broadcasted_iota(jnp.int32, (16, BS), 0)
+    rows = jnp.zeros((16, BS), jnp.float32)
+    for a in range(4):
+        for t, part in enumerate(split3(jnp.broadcast_to(scales_ref[a, 0:1, 0:1], (16, BS)))):
+            rows = jnp.where(sub == 3 * a + t, part, rows)
+    rows = rows.astype(jnp.bfloat16)
+    for a in range(4):
+        piece_ref[a * BS : (a + 1) * BS, :] = blocks_ref[a, :, 0, :]
+    piece_ref[4 * BS :, :] = rows
+
+
+def strip(blocks, scales):
+    return pl.pallas_call(
+        strip_kernel,
+        grid=(1,),
+        in_specs=[
+            pl.BlockSpec((4, BS, 16, BS), lambda i: (0, 0, 0, 0)),
+            pl.BlockSpec((4, 1, 32), lambda i: (0, 0, 0)),
+        ],
+        out_specs=pl.BlockSpec((PIECE, BS), lambda i: (0, 0)),
+        out_shape=jax.ShapeDtypeStruct((PIECE, BS), jnp.bfloat16),
+        compiler_params=pltpu.CompilerParams(vmem_limit_bytes=60 * 1024 * 1024),
+        cost_estimate=pl.CostEstimate(flops=0, bytes_accessed=2 * 2**20, transcendentals=0),
+        name="strip",
+    )(blocks, scales)
+
+
+def along_x(array, x):
+    got = [
+        permute(array, lambda z, y, k, x: (z, y, k, hop[x])) for hop in ((1, 0, 3, 2), (3, 2, 1, 0), (2, 3, 0, 1))
     ]
-    return lax.ppermute(array, AXES, pairs)
-
-
-def scale_rows(scale):
-    high = lax.reduce_precision(scale, 8, 7)
-    rest = scale - high
-    mid = lax.reduce_precision(rest, 8, 7)
-    low = lax.reduce_precision(rest - mid, 8, 7)
-    rows = jnp.stack([high, mid, low], axis=1).reshape(12, 1)
-    rows = jnp.concatenate([rows, jnp.zeros((4, 1), jnp.float32)], axis=0)
-    return jnp.broadcast_to(rows, (16, BS)).astype(jnp.bfloat16)
-
-
-def along_x(array, x):
-    got = []
-    for hop in ({0: 1, 1: 0}, {0: 3, 1: 2}, {0: 2, 1: 3}):
-        table = [(dev(z, y, k, s), dev(z, y, k, hop[s])) for z, y, k, s in PLACES if s in hop]
-        got.append(lax.ppermute(array, AXES, table))
     u = jnp.where(x <= 1, array, got[1])
     v = jnp.where(x <= 1, got[0], got[2])
     return u, v
 
 
-def leading_pair(u, v, first, z, y):
-    head = lambda w: jnp.concatenate([w[:BS], w[4 * BS :]], axis=0)
-    pair = jnp.concatenate([jnp.where(first == 0, head(u), head(v)), jnp.where(first == 0, head(v), head(u))], axis=0)
-    root = lambda z, y, k, x: z == 0 and y == 0
-    up, down, over = (shift(pair, dy=d, where=root) for d in (1, -1, 2))
-    pair = jnp.where(y == 0, pair, jnp.where(y == 1, up, jnp.where(y == 3, down, over)))
-    root = lambda z, y, k, x: z == 0
-    up, down, over = (shift(pair, dz=d, where=root) for d in (1, -1, 2))
-    return jnp.where(z == 0, pair, jnp.where(z == 1, up, jnp.where(z == 3, down, over)))
-
-
-def column_strips(u, v, first, y, k, x):
-    source = lambda z, y, k, x: y % 2 == x // 2
-    giver = lambda z, y, k, x: source(z, y, k, x) and k == x % 2
-    ours = jnp.where(first == k, u, v)
-    mine = jnp.where(k == x % 2, ours, shift(jnp.where(first == k, v, u), dk=1, where=giver))
-    up, down, over = (shift(mine, dy=d, where=source) for d in (1, -1, 2))
+def trade(p, q):
+    return (q if p == 0 else 0), p in (0, q)
+
+
+def pick(at, zero, one, two, three):
+    return jnp.where(at == 0, zero, jnp.where(at == 1, one, jnp.where(at == 2, two, three)))
+
+
+def along_y(mine, y, x):
+    def across(z, y, k, x):
+        return (z, y + 2, k, x) if y % 2 == x // 2 else (z, y, 1 - k, x)
+
+    up = permute(mine, lambda z, y, k, x: (z, y + 1, k, x))
+    down = permute(mine, lambda z, y, k, x: (z, y - 1, k, x))
+    over = permute(mine, across)
     turn = (y - x // 2) % 4
-    slot0 = jnp.where(turn == 0, mine, jnp.where(turn == 1, up, jnp.where(turn == 2, over, down)))
-    slot1 = jnp.where(turn == 0, over, jnp.where(turn == 1, down, jnp.where(turn == 2, mine, up)))
-    return jnp.concatenate([slot0, slot1], axis=0)
+    slots = [pick(turn, mine, up, over, down), pick(turn, over, down, mine, up)]
+    return jnp.concatenate(slots, axis=0)
+
+
+def lead_along(pair, at, axis):
+    got = []
+    for q in (1, 2, 3):
+
+        def place(*here):
+            there = list(here)
+            other, moves = trade(here[axis], q)
+            there[axis if moves else 2] = other if moves else 1 - here[2]
+            return there
+
+        got.append(permute(pair, place))
+    return pick(at, pair, *got)
 
 
 def split3(x):
@@ -268,7 +297,7 @@
     mx = lax.fori_loop(0, BS, update, jnp.zeros((32, BS), jnp.float32), unroll=8)
     big = jnp.max(mx, axis=1, keepdims=True) + 1e-06
     big = jnp.broadcast_to(big, (32, BS))
-    big_ref[0] = big
+    big_ref[0] = big.T[0:1]
     inv = 1.0 / big
 
     def divide(e, carry):
@@ -280,7 +309,7 @@
 
 
 def finish(place, blocks, sc, held, others, u, v, wk, corner):
-    whole = lambda shape: pl.BlockSpec(shape, lambda a, *_: (0,) * len(shape))
+    whole = lambda shape: pl.BlockSpec(memory_space=pltpu.VMEM)
     spec = pltpu.PrefetchScalarGridSpec(
         num_scalar_prefetch=1,
         grid=(4,),
@@ -293,7 +322,7 @@
         + [whole((2, 2 * BS, 2 * BS)), whole((BS, BS))],
         out_specs=[
             pl.BlockSpec((1, BS, 32, BS), lambda a, *_: (a, 0, 0, 0)),
-            pl.BlockSpec((1, 32, BS), lambda a, *_: (a, 0, 0)),
+            pl.BlockSpec((1, 1, 32), lambda a, *_: (a, 0, 0)),
         ],
         scratch_shapes=[
             pltpu.VMEM((32 * BS, 2 * BS), jnp.bfloat16),
@@ -306,7 +335,7 @@
         grid_spec=spec,
         out_shape=[
             jax.ShapeDtypeStruct((4, BS, 32, BS), jnp.bfloat16),
-            jax.ShapeDtypeStruct((4, 32, BS), jnp.float32),
+            jax.ShapeDtypeStruct((4, 1, 32), jnp.float32),
         ],
         compiler_params=pltpu.CompilerParams(vmem_limit_bytes=32 * 1024 * 1024),
         cost_estimate=pl.CostEstimate(flops=2 * 512 * 4096 * 512, bytes_accessed=12 * 2**20, transcendentals=0),
@@ -323,23 +352,27 @@
     z = row // 8
     blocks = blocks.reshape(4, BS, 32, BS)
     scales = scales.reshape(4, 32)
-    srows = scale_rows(scales[:, 0])
-    strip = blocks[:, :, 0, :]
-    piece = jnp.concatenate([strip.reshape(4 * BS, BS), srows], axis=0)
+    piece = strip(blocks, scales.reshape(4, 1, 32))
     first = jnp.where((x == 0) | (x == 3), 0, 1)
     place = jnp.stack([row, col, k, z, first]).astype(jnp.int32)
     u, v = along_x(piece, x)
-    pair = leading_pair(u, v, first, z, y)
-    both = column_strips(u, v, first, y, k, x)
+    ours = jnp.where(first == k, u, v)
+    mine = jnp.where(k == x % 2, ours, permute(jnp.where(first == k, v, u), sibling))
+    head = lambda w: jnp.concatenate([w[:BS], w[4 * BS :]], axis=0)
+    pair = jnp.concatenate([jnp.where(first == 0, head(u), head(v)), jnp.where(first == 0, head(v), head(u))], axis=0)
+    pair, mine = lax.optimization_barrier((pair, mine))
+    pair = lead_along(pair, y, 1)
+    both = along_y(mine, y, x)
+    pair = lead_along(pair, z, 0)
     pair, both = lax.optimization_barrier((pair, both))
-    held = [both] + [shift(both, dz=d) for d in (1, -1, 2)]
-    wk, corner = factor(place, pair, shift(pair, dk=1))
+    held = [both] + [permute(both, lambda z, y, k, x: (z + d, y, k, x)) for d in (1, -1, 2)]
+    wk, corner = factor(place, pair, permute(pair, sibling))
     wk, *held[1:] = lax.optimization_barrier((wk, *held[1:]))
-    others = [shift(h, dk=1) for h in held]
+    others = [permute(h, sibling) for h in held]
     special = ((jnp.arange(4) == 0) & (row < 2))[:, None] | ((jnp.arange(32) == 0) & (col < 2))[None, :]
     sc = jnp.broadcast_to(jnp.where(special, 0.0, scales)[:, :, None], (4, 32, BS))
     factored, largest = finish(place, blocks, sc, held, others, u, v, wk, corner)
-    return factored.reshape(4, 1, BS, 32, 1, BS), largest[:, None, :, :1]
+    return factored.reshape(4, 1, BS, 32, 1, BS), largest.reshape(4, 1, 32, 1)
 
 
 def solution(mesh):

time: 72 us -> 65.2 us (0.906)
  starting transfers between devices: 34.9 us -> 26.4 us
  Pallas kernels: 21.5 us -> 24.3 us
  local copies, waits for them, and re-layouts: 2.34 us -> 0.18 us
  waiting for transfers between devices: 10.5 us -> 12.2 us
    ppermute x21, starting transfers between devices: 34.9 us -> 26.4 us  [permute(): lax.ppermute(array, AXES, [(dev(*place), dev(*to(*place))) for place in P...]
    pallas_call x0 -> x1, Pallas kernels: none -> 2.56 us  [strip(): pl.pallas_call(strip_kernel, grid=(1,), in_specs=[pl.BlockSpec((4, BS, 16...]
    slice x6 -> x4, local copies, waits for them, and re-layouts: 2.06 us -> 0.02 us  [on_device(): head = lambda w: jnp.concatenate([w[:BS], w[4 * BS:]], axis=0)]
    ppermute x21, waiting for transfers between devices: 10.5 us -> 12.2 us  [permute(): lax.ppermute(array, AXES, [(dev(*place), dev(*to(*place))) for place in P...]
    select_n x6, other arithmetic: 0.31 us -> 1.11 us  [the longest x1 0.97 us: on_device(): jnp.where(first == k, v, u)]
    another operation x2 -> x0, other arithmetic: 0.77 us -> none
  transfers between devices with their start and end apart: 21 -> 21, of which waited for: 8 -> 11; matrix products, arithmetic and copies ran while one was open for 0% -> 0% of each run, Pallas kernels for 18% -> 20%
where the time goes in v3:
time: 65.2 us; the launch traced here: 65 us
  starting transfers between devices  26.4 us (40%)
  Pallas kernels  24.3 us (37%)
  waiting for transfers between devices  12.2 us (19%)
  other arithmetic  1.22 us (2%)
  between operations  0.75 us (1%)
    ppermute x21, starting transfers between devices, permute(): lax.ppermute(array, AXES, [(dev(*place), dev(*to(*place))) for place in P...  26.4 us
    pallas_call x1, Pallas kernels, factor(): pl.pallas_call(factor_kernel, grid_spec=pltpu.PrefetchScalarGridSpec(num_...  12.7 us
    ppermute x21, waiting for transfers between devices, permute(): lax.ppermute(array, AXES, [(dev(*place), dev(*to(*place))) for place in P...  12.2 us
    pallas_call x1, Pallas kernels, finish(): pl.pallas_call(finish_kernel, grid_spec=spec, out_shape=[jax.ShapeDtypeSt...  9 us
    pallas_call x1, Pallas kernels, strip(): pl.pallas_call(strip_kernel, grid=(1,), in_specs=[pl.BlockSpec((4, BS, 16...  2.56 us
  transfers between devices with their start and end apart: 21, of which 11 were waited for; matrix products, arithmetic and copies ran while one was open for 0% of the time, Pallas kernels for 20%

profile of v3, /device:TPU:1, one launch (start us, length us, event | category | flops | bytes accessed | tf_op | source)
XLA Modules:
  0.0 65.0 jit_solution(3297641255921514106)
XLA Ops:
  0.6 2.6 %strip.1 = bf16[528,128]{1,0:T(8,128)(2,1)} custom-call(bf16[4,128,32,128]{3,2,1,0:T(8,128)(2,1)} %bitcast.16, f32[4,1,32]{2,1,0:T(1,128)} %bitcast.18), custom_call_target="tpu_custom_call" | custom-call | bytes 2097152 | tf_op jit(solution)/shard_map/strip/pallas_call | solution.py:42
  3.2 3.6 %collective-permute-start.2 = (bf16[528,128]{1,0:T(8,128)(2,1)}, bf16[528,128]{1,0:T(8,128)(2,1)S(1)}, u32[]{:S(2)}, u32[]{:S(2)}) collective-permute-start(bf16[528,128]{1,0:T(8,128)(2,1)} %strip.1), channel_id=1, source_target_pairs={{0,2},{1,3},{2,0},{3,1},{4,6},{5,7},{6,4},{7,5},{8,10},{9,11},{10,... | collective-permute-start | bytes 405512 | tf_op jit(solution)/shard_map/ppermute | solution.py:22
  6.8 0.3 collective-permute-start.1
  7.1 0.6 collective-permute-start
  7.6 2.2 %collective-permute-done.2 = bf16[528,128]{1,0:T(8,128)(2,1)S(1)} collective-permute-done((bf16[528,128]{1,0:T(8,128)(2,1)}, bf16[528,128]{1,0:T(8,128)(2,1)S(1)}, u32[]{:S(2)}, u32[]{:S(2)}) %collective-permute-start.2) | collective-permute-done | bytes 135200 | tf_op jit(solution)/shard_map/ppermute | solution.py:22
  9.8 3.4 %collective-permute-done.1 = bf16[528,128]{1,0:T(8,128)(2,1)S(1)} collective-permute-done((bf16[528,128]{1,0:T(8,128)(2,1)}, bf16[528,128]{1,0:T(8,128)(2,1)S(1)}, u32[]{:S(2)}, u32[]{:S(2)}) %collective-permute-start.1) | collective-permute-done | bytes 135200 | tf_op jit(solution)/shard_map/ppermute | solution.py:22
  13.2 1.0 %broadcast_select_fusion = (bf16[528,128]{1,0:T(8,128)(2,1)S(1)}, bf16[528,128]{1,0:T(8,128)(2,1)S(1)}, bf16[528,128]{1,0:T(8,128)(2,1)S(1)}) fusion(pred[]{:T(512)S(6)} %eq.78, bf16[528,128]{1,0:T(8,128)(2,1)} %strip.1, bf16[528,128]{1,0:T(8,128)(2,1)S(1)} %collective-permute-done, pred[]{:T(512)S(6)} %le.4, bf16[528,128]{1,0:T(8,128)(2,1)S(1)} %collective-permute-done.1, ...), kind=kLoop, calls=%fused_computation.4 | loop fusion | flops 202752 | bytes 946178 | tf_op jit(solution)/shard_map/jit(_where)/select_n | solution.py:360
  14.2 1.8 %collective-permute-start.3 = (bf16[528,128]{1,0:T(8,128)(2,1)S(1)}, bf16[528,128]{1,0:T(8,128)(2,1)S(1)}, u32[]{:S(2)}, u32[]{:S(2)}) collective-permute-start(bf16[528,128]{1,0:T(8,128)(2,1)S(1)} %get-tuple-element.28), channel_id=1, source_target_pairs={{0,4},{1,5},{2,6},{3,7},{4,0},{5,1},{6,2},{7,3},{8,12},{9,13},{10,... | collective-permute-start | bytes 405512 | tf_op jit(solution)/shard_map/ppermute | solution.py:22
  16.0 1.0 %collective-permute-done.3 = bf16[528,128]{1,0:T(8,128)(2,1)S(1)} collective-permute-done((bf16[528,128]{1,0:T(8,128)(2,1)S(1)}, bf16[528,128]{1,0:T(8,128)(2,1)S(1)}, u32[]{:S(2)}, u32[]{:S(2)}) %collective-permute-start.3) | collective-permute-done | bytes 135200 | tf_op jit(solution)/shard_map/ppermute | solution.py:22
  17.0 3.0 %collective-permute-start.6 = (bf16[288,128]{1,0:T(8,128)(2,1)S(1)}, bf16[288,128]{1,0:T(8,128)(2,1)S(1)}, u32[]{:S(2)}, u32[]{:S(2)}) collective-permute-start(bf16[288,128]{1,0:T(8,128)(2,1)S(1)} %pad_maximum_fusion.1), channel_id=1, source_target_pairs={{0,24},{1,25},{2,26},{3,27},{4,28},{5,29},{6,30},{7,31},{8,12},{9,... | collective-permute-start | bytes 221192 | tf_op jit(solution)/shard_map/ppermute | solution.py:22
  20.1 0.5 collective-permute-start.5
  20.6 0.1 stack.23.place
  20.7 3.4 %collective-permute-start.11 = (bf16[528,128]{1,0:T(8,128)(2,1)S(1)}, bf16[528,128]{1,0:T(8,128)(2,1)S(1)}, u32[]{:S(2)}, u32[]{:S(2)}) collective-permute-start(bf16[528,128]{1,0:T(8,128)(2,1)S(1)} %select_select_fusion.2), channel_id=1, source_target_pairs={{0,16},{1,17},{2,6},{3,7},{4,20},{5,21},{6,2},{7,3},{8,12},{9,13},... | collective-permute-start | bytes 405512 | tf_op jit(solution)/shard_map/ppermute | solution.py:22
  24.1 0.6 collective-permute-done.5
  24.8 3.8 %collective-permute-start.9 = (bf16[288,128]{1,0:T(8,128)(2,1)S(1)}, bf16[288,128]{1,0:T(8,128)(2,1)S(1)}, u32[]{:S(2)}, u32[]{:S(2)}) collective-permute-start(bf16[288,128]{1,0:T(8,128)(2,1)S(1)} %select_select_fusion.4), channel_id=1, source_target_pairs={{0,96},{1,97},{2,98},{3,99},{4,100},{5,101},{6,102},{7,103},{8,104... | collective-permute-start | bytes 221192 | tf_op jit(solution)/shard_map/ppermute | solution.py:22
  28.6 2.4 %collective-permute-start.8 = (bf16[288,128]{1,0:T(8,128)(2,1)S(1)}, bf16[288,128]{1,0:T(8,128)(2,1)S(1)}, u32[]{:S(2)}, u32[]{:S(2)}) collective-permute-start(bf16[288,128]{1,0:T(8,128)(2,1)S(1)} %select_select_fusion.4), channel_id=1, source_target_pairs={{0,64},{1,65},{2,66},{3,67},{4,68},{5,69},{6,70},{7,71},{8,72},{9,... | collective-permute-start | bytes 221192 | tf_op jit(solution)/shard_map/ppermute | solution.py:22
  31.1 0.1 collective-permute-done.10
  31.3 2.1 %collective-permute-done.8 = bf16[288,128]{1,0:T(8,128)(2,1)S(1)} collective-permute-done((bf16[288,128]{1,0:T(8,128)(2,1)S(1)}, bf16[288,128]{1,0:T(8,128)(2,1)S(1)}, u32[]{:S(2)}, u32[]{:S(2)}) %collective-permute-start.8) | collective-permute-done | bytes 73760 | tf_op jit(solution)/shard_map/ppermute | solution.py:22
  33.4 0.8 %collective-permute-done.7 = bf16[288,128]{1,0:T(8,128)(2,1)S(1)} collective-permute-done((bf16[288,128]{1,0:T(8,128)(2,1)S(1)}, bf16[288,128]{1,0:T(8,128)(2,1)S(1)}, u32[]{:S(2)}, u32[]{:S(2)}) %collective-permute-start.7) | collective-permute-done | bytes 73760 | tf_op jit(solution)/shard_map/ppermute | solution.py:22
  34.3 3.2 %collective-permute-start.13 = (bf16[288,128]{1,0:T(8,128)(2,1)S(1)}, bf16[288,128]{1,0:T(8,128)(2,1)S(1)}, u32[]{:S(2)}, u32[]{:S(2)}) collective-permute-start(bf16[288,128]{1,0:T(8,128)(2,1)S(1)} %select_select_fusion.3.pair_ref), channel_id=1, source_target_pairs={{0,4},{1,5},{2,6},{3,7},{4,0},{5,1},{6,2},{7,3},{8,12},{9,13},{10,... | collective-permute-start | bytes 221192 | tf_op jit(solution)/shard_map/ppermute | solution.py:22
  37.5 0.1 collective-permute-start.17
  37.6 0.5 collective-permute-start.16
  38.1 1.9 %collective-permute-start.15 = (bf16[1056,128]{1,0:T(8,128)(2,1)S(1)}, bf16[1056,128]{1,0:T(8,128)(2,1)S(1)}, u32[]{:S(2)}, u32[]{:S(2)}) collective-permute-start(bf16[1056,128]{1,0:T(8,128)(2,1)S(1)} %pad_maximum_fusion.m0), channel_id=1, source_target_pairs={{0,96},{1,97},{2,98},{3,99},{4,100},{5,101},{6,102},{7,103},{8,104... | collective-permute-start | bytes 811016 | tf_op jit(solution)/shard_map/ppermute | solution.py:22
  40.0 12.7 %factor.1 = (bf16[2,256,256]{2,1,0:T(8,128)(2,1)S(1)}, f32[128,128]{1,0:T(8,128)S(1)}) custom-call(s32[5]{0:T(128)S(1)} %stack.23.place, bf16[288,128]{1,0:T(8,128)(2,1)S(1)} %select_select_fusion.3.pair_ref, bf16[288,128]{1,0:T(8,128)(2,1)S(1)} %collective-permute-done.13.other_ref), custom_call_target="tpu_custom_call" | custom-call | flops 20000000000 | bytes 1048576 | tf_op jit(solution)/shard_map/factor/pallas_call | solution.py:209
  52.8 0.6 collective-permute-done.14.m1
  53.3 0.7 %collective-permute-start.18 = (bf16[1056,128]{1,0:T(8,128)(2,1)S(1)}, bf16[1056,128]{1,0:T(8,128)(2,1)S(1)}, u32[]{:S(2)}, u32[]{:S(2)}) collective-permute-start(bf16[1056,128]{1,0:T(8,128)(2,1)S(1)} %collective-permute-done.14.m1), channel_id=1, source_target_pairs={{0,4},{1,5},{2,6},{3,7},{4,0},{5,1},{6,2},{7,3},{8,12},{9,13},{10,... | collective-permute-start | bytes 811016 | tf_op jit(solution)/shard_map/ppermute | solution.py:22
  54.0 0.1 collective-permute-start.19
  54.1 0.4 collective-permute-start.20
  54.6 0.6 collective-permute-done.18.t1
  55.2 0.4 collective-permute-done.19.t2
  55.6 0.4 collective-permute-done.20.t3
  56.0 9.0 %finish.1 = (bf16[4,128,32,128]{3,2,1,0:T(8,128)(2,1)}, f32[4,1,32]{2,1,0:T(1,128)}) custom-call(s32[5]{0:T(128)S(1)} %stack.23.place, bf16[4,128,32,128]{3,2,1,0:T(8,128)(2,1)S(1)} %bitcast.17, f32[4,32,128]{2,1,0:T(8,128)S(1)} %broadcast_in_dim.7.sc_ref, bf16[1056,128]{1,0:T(8,128)(2,1)S(1)} %pad_maximum_fusion.m0, ...), custom_call_target="tpu_custom_call" | custom-call | flops 2147483648 | bytes 12582912 | tf_op jit(solution)/shard_map/finish/pallas_call | solution.py:333
  (34 shorter events, 0.4 us)
Async XLA Ops:
  3.2 6.6 %collective-permute-start.2 = (bf16[528,128]{1,0:T(8,128)(2,1)}, bf16[528,128]{1,0:T(8,128)(2,1)S(1)}, u32[]{:S(2)}, u32[]{:S(2)}) collective-permute-start(bf16[528,128]{1,0:T(8,128)(2,1)} %strip.1), channel_id=1, source_target_pairs={{0,2},{1,3},{2,0},{3,1},{4,6},{5,7},{6,4},{7,5},{8,10},{9,11},{10,... | collective-permute-start | bytes 405512 | tf_op jit(solution)/shard_map/ppermute | solution.py:22
  6.8 6.4 %collective-permute-start.1 = (bf16[528,128]{1,0:T(8,128)(2,1)}, bf16[528,128]{1,0:T(8,128)(2,1)S(1)}, u32[]{:S(2)}, u32[]{:S(2)}) collective-permute-start(bf16[528,128]{1,0:T(8,128)(2,1)} %strip.1), channel_id=1, source_target_pairs={{0,1},{1,0},{2,3},{3,2},{4,5},{5,4},{6,7},{7,6},{8,9},{9,8},{10,11... | collective-permute-start | bytes 405512 | tf_op jit(solution)/shard_map/ppermute | solution.py:22
  7.1 6.1 %collective-permute-start = (bf16[528,128]{1,0:T(8,128)(2,1)}, bf16[528,128]{1,0:T(8,128)(2,1)S(1)}, u32[]{:S(2)}, u32[]{:S(2)}) collective-permute-start(bf16[528,128]{1,0:T(8,128)(2,1)} %strip.1), channel_id=1, source_target_pairs={{0,3},{1,2},{2,1},{3,0},{4,7},{5,6},{6,5},{7,4},{8,11},{9,10},{10,... | collective-permute-start | bytes 405512 | tf_op jit(solution)/shard_map/ppermute | solution.py:22
  14.2 2.8 %collective-permute-start.3 = (bf16[528,128]{1,0:T(8,128)(2,1)S(1)}, bf16[528,128]{1,0:T(8,128)(2,1)S(1)}, u32[]{:S(2)}, u32[]{:S(2)}) collective-permute-start(bf16[528,128]{1,0:T(8,128)(2,1)S(1)} %get-tuple-element.28), channel_id=1, source_target_pairs={{0,4},{1,5},{2,6},{3,7},{4,0},{5,1},{6,2},{7,3},{8,12},{9,13},{10,... | collective-permute-start | bytes 405512 | tf_op jit(solution)/shard_map/ppermute | solution.py:22
  17.0 7.1 %collective-permute-start.6 = (bf16[288,128]{1,0:T(8,128)(2,1)S(1)}, bf16[288,128]{1,0:T(8,128)(2,1)S(1)}, u32[]{:S(2)}, u32[]{:S(2)}) collective-permute-start(bf16[288,128]{1,0:T(8,128)(2,1)S(1)} %pad_maximum_fusion.1), channel_id=1, source_target_pairs={{0,24},{1,25},{2,26},{3,27},{4,28},{5,29},{6,30},{7,31},{8,12},{9,... | collective-permute-start | bytes 221192 | tf_op jit(solution)/shard_map/ppermute | solution.py:22
  20.1 4.7 %collective-permute-start.5 = (bf16[288,128]{1,0:T(8,128)(2,1)S(1)}, bf16[288,128]{1,0:T(8,128)(2,1)S(1)}, u32[]{:S(2)}, u32[]{:S(2)}) collective-permute-start(bf16[288,128]{1,0:T(8,128)(2,1)S(1)} %pad_maximum_fusion.1), channel_id=1, source_target_pairs={{0,16},{1,17},{2,18},{3,19},{4,20},{5,21},{6,22},{7,23},{8,12},{9,... | collective-permute-start | bytes 221192 | tf_op jit(solution)/shard_map/ppermute | solution.py:22
  20.6 4.2 %collective-permute-start.4 = (bf16[288,128]{1,0:T(8,128)(2,1)S(1)}, bf16[288,128]{1,0:T(8,128)(2,1)S(1)}, u32[]{:S(2)}, u32[]{:S(2)}) collective-permute-start(bf16[288,128]{1,0:T(8,128)(2,1)S(1)} %pad_maximum_fusion.1), channel_id=1, source_target_pairs={{0,8},{1,9},{2,10},{3,11},{4,12},{5,13},{6,14},{7,15},{8,0},{9,1},... | collective-permute-start | bytes 221192 | tf_op jit(solution)/shard_map/ppermute | solution.py:22
  20.7 10.4 %collective-permute-start.12 = (bf16[528,128]{1,0:T(8,128)(2,1)S(1)}, bf16[528,128]{1,0:T(8,128)(2,1)S(1)}, u32[]{:S(2)}, u32[]{:S(2)}) collective-permute-start(bf16[528,128]{1,0:T(8,128)(2,1)S(1)} %select_select_fusion.2), channel_id=1, source_target_pairs={{0,24},{1,25},{2,26},{3,27},{4,28},{5,29},{6,30},{7,31},{8,0},{9,1... | collective-permute-start | bytes 405512 | tf_op jit(solution)/shard_map/ppermute | solution.py:22
  20.7 10.3 %collective-permute-start.11 = (bf16[528,128]{1,0:T(8,128)(2,1)S(1)}, bf16[528,128]{1,0:T(8,128)(2,1)S(1)}, u32[]{:S(2)}, u32[]{:S(2)}) collective-permute-start(bf16[528,128]{1,0:T(8,128)(2,1)S(1)} %select_select_fusion.2), channel_id=1, source_target_pairs={{0,16},{1,17},{2,6},{3,7},{4,20},{5,21},{6,2},{7,3},{8,12},{9,13},... | collective-permute-start | bytes 405512 | tf_op jit(solution)/shard_map/ppermute | solution.py:22
  24.1 7.1 %collective-permute-start.10 = (bf16[528,128]{1,0:T(8,128)(2,1)S(1)}, bf16[528,128]{1,0:T(8,128)(2,1)S(1)}, u32[]{:S(2)}, u32[]{:S(2)}) collective-permute-start(bf16[528,128]{1,0:T(8,128)(2,1)S(1)} %select_select_fusion.2), channel_id=1, source_target_pairs={{0,8},{1,9},{2,10},{3,11},{4,12},{5,13},{6,14},{7,15},{8,16},{9,17... | collective-permute-start | bytes 405512 | tf_op jit(solution)/shard_map/ppermute | solution.py:22
  24.8 6.5 %collective-permute-start.9 = (bf16[288,128]{1,0:T(8,128)(2,1)S(1)}, bf16[288,128]{1,0:T(8,128)(2,1)S(1)}, u32[]{:S(2)}, u32[]{:S(2)}) collective-permute-start(bf16[288,128]{1,0:T(8,128)(2,1)S(1)} %select_select_fusion.4), channel_id=1, source_target_pairs={{0,96},{1,97},{2,98},{3,99},{4,100},{5,101},{6,102},{7,103},{8,104... | collective-permute-start | bytes 221192 | tf_op jit(solution)/shard_map/ppermute | solution.py:22
  28.6 4.8 %collective-permute-start.8 = (bf16[288,128]{1,0:T(8,128)(2,1)S(1)}, bf16[288,128]{1,0:T(8,128)(2,1)S(1)}, u32[]{:S(2)}, u32[]{:S(2)}) collective-permute-start(bf16[288,128]{1,0:T(8,128)(2,1)S(1)} %select_select_fusion.4), channel_id=1, source_target_pairs={{0,64},{1,65},{2,66},{3,67},{4,68},{5,69},{6,70},{7,71},{8,72},{9,... | collective-permute-start | bytes 221192 | tf_op jit(solution)/shard_map/ppermute | solution.py:22
  31.1 3.2 %collective-permute-start.7 = (bf16[288,128]{1,0:T(8,128)(2,1)S(1)}, bf16[288,128]{1,0:T(8,128)(2,1)S(1)}, u32[]{:S(2)}, u32[]{:S(2)}) collective-permute-start(bf16[288,128]{1,0:T(8,128)(2,1)S(1)} %select_select_fusion.4), channel_id=1, source_target_pairs={{0,32},{1,33},{2,34},{3,35},{4,36},{5,37},{6,38},{7,39},{8,40},{9,... | collective-permute-start | bytes 221192 | tf_op jit(solution)/shard_map/ppermute | solution.py:22
  34.3 5.7 %collective-permute-start.13 = (bf16[288,128]{1,0:T(8,128)(2,1)S(1)}, bf16[288,128]{1,0:T(8,128)(2,1)S(1)}, u32[]{:S(2)}, u32[]{:S(2)}) collective-permute-start(bf16[288,128]{1,0:T(8,128)(2,1)S(1)} %select_select_fusion.3.pair_ref), channel_id=1, source_target_pairs={{0,4},{1,5},{2,6},{3,7},{4,0},{5,1},{6,2},{7,3},{8,12},{9,13},{10,... | collective-permute-start | bytes 221192 | tf_op jit(solution)/shard_map/ppermute | solution.py:22
  37.5 17.1 %copy-start.1 = (f32[4,1,32,1]{2,3,1,0:T(1,128)S(1)}, f32[4,1,32,1]{2,3,1,0:T(1,128)}, u32[]{:S(2)}) copy-start(f32[4,1,32,1]{2,3,1,0:T(1,128)} %param.3) | copy-start | bytes 1540
  37.5 18.6 %copy-start = (bf16[4,1,128,32,1,128]{5,3,4,2,1,0:T(8,128)(2,1)S(1)}, bf16[4,1,128,32,1,128]{5,3,4,2,1,0:T(8,128)(2,1)}, u32[]{:S(2)}) copy-start(bf16[4,1,128,32,1,128]{5,3,4,2,1,0:T(8,128)(2,1)} %param.2) | copy-start | bytes 12582916
  37.5 17.1 %collective-permute-start.17 = (bf16[1056,128]{1,0:T(8,128)(2,1)S(1)}, bf16[1056,128]{1,0:T(8,128)(2,1)S(1)}, u32[]{:S(2)}, u32[]{:S(2)}) collective-permute-start(bf16[1056,128]{1,0:T(8,128)(2,1)S(1)} %pad_maximum_fusion.m0), channel_id=1, source_target_pairs={{0,4},{1,5},{2,6},{3,7},{4,0},{5,1},{6,2},{7,3},{8,12},{9,13},{10,... | collective-permute-start | bytes 811016 | tf_op jit(solution)/shard_map/ppermute | solution.py:22
  37.6 15.2 %collective-permute-start.16 = (bf16[1056,128]{1,0:T(8,128)(2,1)S(1)}, bf16[1056,128]{1,0:T(8,128)(2,1)S(1)}, u32[]{:S(2)}, u32[]{:S(2)}) collective-permute-start(bf16[1056,128]{1,0:T(8,128)(2,1)S(1)} %pad_maximum_fusion.m0), channel_id=1, source_target_pairs={{0,64},{1,65},{2,66},{3,67},{4,68},{5,69},{6,70},{7,71},{8,72},{9,... | collective-permute-start | bytes 811016 | tf_op jit(solution)/shard_map/ppermute | solution.py:22
  38.1 14.7 %collective-permute-start.15 = (bf16[1056,128]{1,0:T(8,128)(2,1)S(1)}, bf16[1056,128]{1,0:T(8,128)(2,1)S(1)}, u32[]{:S(2)}, u32[]{:S(2)}) collective-permute-start(bf16[1056,128]{1,0:T(8,128)(2,1)S(1)} %pad_maximum_fusion.m0), channel_id=1, source_target_pairs={{0,96},{1,97},{2,98},{3,99},{4,100},{5,101},{6,102},{7,103},{8,104... | collective-permute-start | bytes 811016 | tf_op jit(solution)/shard_map/ppermute | solution.py:22
  40.0 13.3 %collective-permute-start.14 = (bf16[1056,128]{1,0:T(8,128)(2,1)S(1)}, bf16[1056,128]{1,0:T(8,128)(2,1)S(1)}, u32[]{:S(2)}, u32[]{:S(2)}) collective-permute-start(bf16[1056,128]{1,0:T(8,128)(2,1)S(1)} %pad_maximum_fusion.m0), channel_id=1, source_target_pairs={{0,32},{1,33},{2,34},{3,35},{4,36},{5,37},{6,38},{7,39},{8,40},{9,... | collective-permute-start | bytes 811016 | tf_op jit(solution)/shard_map/ppermute | solution.py:22
  53.3 1.8 %collective-permute-start.18 = (bf16[1056,128]{1,0:T(8,128)(2,1)S(1)}, bf16[1056,128]{1,0:T(8,128)(2,1)S(1)}, u32[]{:S(2)}, u32[]{:S(2)}) collective-permute-start(bf16[1056,128]{1,0:T(8,128)(2,1)S(1)} %collective-permute-done.14.m1), channel_id=1, source_target_pairs={{0,4},{1,5},{2,6},{3,7},{4,0},{5,1},{6,2},{7,3},{8,12},{9,13},{10,... | collective-permute-start | bytes 811016 | tf_op jit(solution)/shard_map/ppermute | solution.py:22
  54.0 1.6 %collective-permute-start.19 = (bf16[1056,128]{1,0:T(8,128)(2,1)S(1)}, bf16[1056,128]{1,0:T(8,128)(2,1)S(1)}, u32[]{:S(2)}, u32[]{:S(2)}) collective-permute-start(bf16[1056,128]{1,0:T(8,128)(2,1)S(1)} %collective-permute-done.15.m2), channel_id=1, source_target_pairs={{0,4},{1,5},{2,6},{3,7},{4,0},{5,1},{6,2},{7,3},{8,12},{9,13},{10,... | collective-permute-start | bytes 811016 | tf_op jit(solution)/shard_map/ppermute | solution.py:22
  54.1 1.9 %collective-permute-start.20 = (bf16[1056,128]{1,0:T(8,128)(2,1)S(1)}, bf16[1056,128]{1,0:T(8,128)(2,1)S(1)}, u32[]{:S(2)}, u32[]{:S(2)}) collective-permute-start(bf16[1056,128]{1,0:T(8,128)(2,1)S(1)} %collective-permute-done.16.m3), channel_id=1, source_target_pairs={{0,4},{1,5},{2,6},{3,7},{4,0},{5,1},{6,2},{7,3},{8,12},{9,13},{10,... | collective-permute-start | bytes 811016 | tf_op jit(solution)/shard_map/ppermute | solution.py:22

commit v4 on v3

--- a/solution.py
+++ b/solution.py
@@ -58,6 +58,10 @@
     got = [
         permute(array, lambda z, y, k, x: (z, y, k, hop[x])) for hop in ((1, 0, 3, 2), (3, 2, 1, 0), (2, 3, 0, 1))
     ]
+    return got
+
+
+def by_column(array, got, x):
     u = jnp.where(x <= 1, array, got[1])
     v = jnp.where(x <= 1, got[0], got[2])
     return u, v
@@ -111,35 +115,39 @@
     width = ref.shape[1]
     lanes = width // BS
     wide = lambda w: jnp.concatenate([w] * lanes, axis=1)
-    for base in range(0, BS, 8):
-        tile = ref[base : base + 8, :]
-        rows = [splat(tile[i : i + 1, :], (8, width)) for i in range(8)]
-        cols = [splat(tile[:, base + j : base + j + 1], (8, BS)) for j in range(8)]
-        e = [[splat(cols[j][i : i + 1, :], (8, BS)) for j in range(i + 1)] for i in range(8)]
-        for j in range(8):
+    for base in range(0, BS, 16):
+        tile = ref[base : base + 16, :]
+        rows = [splat(tile[i : i + 1, :], (8, width)) for i in range(16)]
+        cols = [splat(tile[:, base + j : base + j + 1], (16, BS)) for j in range(16)]
+        e = [[splat(cols[j][i : i + 1, :], (8, BS)) for j in range(i + 1)] for i in range(16)]
+        for j in range(16):
             r = lax.rsqrt(e[j][j])
             rows[j] = rows[j] * wide(r)
-            l = [None] * 8
-            for i in range(j + 1, 8):
+            l = [None] * 16
+            for i in range(j + 1, 16):
                 l[i] = e[i][j] * r
-            for i in range(j + 1, 8):
+            for i in range(j + 1, 16):
                 for m in range(j + 1, i + 1):
                     e[i][m] = e[i][m] - l[i] * l[m]
                 rows[i] = rows[i] - wide(l[i]) * rows[j]
         sub = lax.broadcasted_iota(jnp.int32, (8, width), 0)
-        out = rows[0]
-        for i in range(1, 8):
-            out = jnp.where(sub == i, rows[i], out)
-        below = lax.broadcasted_iota(jnp.int32, (8, BS), 0) + base
-        upper = jnp.where(lax.broadcasted_iota(jnp.int32, (8, BS), 1) >= below, out[:, :BS], 0.0)
+        out = []
+        for g in range(0, 16, 8):
+            acc = rows[g]
+            for i in range(1, 8):
+                acc = jnp.where(sub == i, rows[g + i], acc)
+            out.append(acc)
+        out = jnp.concatenate(out, axis=0)
+        below = lax.broadcasted_iota(jnp.int32, (16, BS), 0) + base
+        upper = jnp.where(lax.broadcasted_iota(jnp.int32, (16, BS), 1) >= below, out[:, :BS], 0.0)
         out = jnp.concatenate([upper, out[:, BS:]], axis=1)
-        ref[base : base + 8, :] = out
-        if base + 8 < BS:
+        ref[base : base + 16, :] = out
+        if base + 16 < BS:
             h, m, l = split3(out)
             left = jnp.concatenate([w[:, :BS] for w in (h, h, m, m, h, l)], axis=0).astype(jnp.bfloat16)
             right = jnp.concatenate([h, m, h, m, l, h], axis=0).astype(jnp.bfloat16)
             d = lax.dot_general(left, right, (((0,), (0,)), ((), ())), preferred_element_type=jnp.float32)
-            ref[base + 8 :, :] = ref[base + 8 :, :] - d[base + 8 :, :]
+            ref[base + 16 :, :] = ref[base + 16 :, :] - d[base + 16 :, :]
 
 
 def factor_kernel(place, pair_ref, other_ref, wk_ref, corner_ref, one_ref, two_ref):
@@ -219,7 +227,7 @@
             jax.ShapeDtypeStruct((BS, BS), jnp.float32),
         ],
         compiler_params=pltpu.CompilerParams(vmem_limit_bytes=16 * 1024 * 1024),
-        cost_estimate=pl.CostEstimate(flops=2 * 10**10, bytes_accessed=2**20, transcendentals=0),
+        cost_estimate=pl.CostEstimate(flops=10**6, bytes_accessed=2**16, transcendentals=0),
         name="factor",
     )(place, pair, other)
 
@@ -355,7 +363,8 @@
     piece = strip(blocks, scales.reshape(4, 1, 32))
     first = jnp.where((x == 0) | (x == 3), 0, 1)
     place = jnp.stack([row, col, k, z, first]).astype(jnp.int32)
-    u, v = along_x(piece, x)
+    got = along_x(piece, x)
+    u, v = by_column(piece, got, x)
     ours = jnp.where(first == k, u, v)
     mine = jnp.where(k == x % 2, ours, permute(jnp.where(first == k, v, u), sibling))
     head = lambda w: jnp.concatenate([w[:BS], w[4 * BS :]], axis=0)
@@ -364,7 +373,8 @@
     pair = lead_along(pair, y, 1)
     both = along_y(mine, y, x)
     pair = lead_along(pair, z, 0)
-    pair, both = lax.optimization_barrier((pair, both))
+    pair, piece, got = lax.optimization_barrier((pair, piece, got))
+    u, v = by_column(piece, got, x)
     held = [both] + [permute(both, lambda z, y, k, x: (z + d, y, k, x)) for d in (1, -1, 2)]
     wk, corner = factor(place, pair, permute(pair, sibling))
     wk, *held[1:] = lax.optimization_barrier((wk, *held[1:]))

time: 65.2 us -> 62.4 us (0.957)
  waiting for transfers between devices: 12.2 us -> 9.44 us
  Pallas kernels: 24.3 us -> 23 us
  starting transfers between devices: 26.4 us -> 27.7 us
    ppermute x21, waiting for transfers between devices: 12.2 us -> 9.44 us  [permute(): lax.ppermute(array, AXES, [(dev(*place), dev(*to(*place))) for place in P...]
    ppermute x21, starting transfers between devices: 26.4 us -> 27.7 us  [permute(): lax.ppermute(array, AXES, [(dev(*place), dev(*to(*place))) for place in P...]
    pallas_call x1, Pallas kernels: 12.7 us -> 11.6 us  [factor(): pl.pallas_call(factor_kernel, grid_spec=pltpu.PrefetchScalarGridSpec(num_...]
  transfers between devices with their start and end apart: 21 -> 21, of which waited for: 11 -> 9; matrix products, arithmetic and copies ran while one was open for 0% -> 1% of each run, Pallas kernels for 20% -> 19%
where the time goes in v4:
time: 62.4 us; the launch traced here: 62.3 us
  starting transfers between devices  27.7 us (44%)
  Pallas kernels  23 us (37%)
  waiting for transfers between devices  9.44 us (15%)
  other arithmetic  1.23 us (2%)
  between operations  0.78 us (1%)
    ppermute x21, starting transfers between devices, permute(): lax.ppermute(array, AXES, [(dev(*place), dev(*to(*place))) for place in P...  27.7 us
    pallas_call x1, Pallas kernels, factor(): pl.pallas_call(factor_kernel, grid_spec=pltpu.PrefetchScalarGridSpec(num_...  11.6 us
    ppermute x21, waiting for transfers between devices, permute(): lax.ppermute(array, AXES, [(dev(*place), dev(*to(*place))) for place in P...  9.44 us
    pallas_call x1, Pallas kernels, finish(): pl.pallas_call(finish_kernel, grid_spec=spec, out_shape=[jax.ShapeDtypeSt...  8.85 us
    pallas_call x1, Pallas kernels, strip(): pl.pallas_call(strip_kernel, grid=(1,), in_specs=[pl.BlockSpec((4, BS, 16...  2.56 us
  transfers between devices with their start and end apart: 21, of which 9 were waited for; matrix products, arithmetic and copies ran while one was open for 1% of the time, Pallas kernels for 19%

profile of v4, /device:TPU:1, one launch (start us, length us, event | category | flops | bytes accessed | tf_op | source)
XLA Modules:
  0.0 62.3 jit_solution(6545745388623745897)
XLA Ops:
  0.6 2.6 %strip.1 = bf16[528,128]{1,0:T(8,128)(2,1)} custom-call(bf16[4,128,32,128]{3,2,1,0:T(8,128)(2,1)} %bitcast.16, f32[4,1,32]{2,1,0:T(1,128)} %bitcast.18), custom_call_target="tpu_custom_call" | custom-call | bytes 2097152 | tf_op jit(solution)/shard_map/strip/pallas_call | solution.py:42
  3.2 3.6 %collective-permute-start.2 = (bf16[528,128]{1,0:T(8,128)(2,1)}, bf16[528,128]{1,0:T(8,128)(2,1)S(1)}, u32[]{:S(2)}, u32[]{:S(2)}) collective-permute-start(bf16[528,128]{1,0:T(8,128)(2,1)} %strip.1), channel_id=1, source_target_pairs={{0,2},{1,3},{2,0},{3,1},{4,6},{5,7},{6,4},{7,5},{8,10},{9,11},{10,... | collective-permute-start | bytes 405512 | tf_op jit(solution)/shard_map/ppermute | solution.py:22
  6.8 0.3 collective-permute-start.1
  7.1 0.6 collective-permute-start
  7.6 0.1 stack.23.place
  7.7 2.2 %collective-permute-done.2 = bf16[528,128]{1,0:T(8,128)(2,1)S(1)} collective-permute-done((bf16[528,128]{1,0:T(8,128)(2,1)}, bf16[528,128]{1,0:T(8,128)(2,1)S(1)}, u32[]{:S(2)}, u32[]{:S(2)}) %collective-permute-start.2) | collective-permute-done | bytes 135200 | tf_op jit(solution)/shard_map/ppermute | solution.py:22
  10.0 3.2 %collective-permute-done.1 = bf16[528,128]{1,0:T(8,128)(2,1)S(1)} collective-permute-done((bf16[528,128]{1,0:T(8,128)(2,1)}, bf16[528,128]{1,0:T(8,128)(2,1)S(1)}, u32[]{:S(2)}, u32[]{:S(2)}) %collective-permute-start.1) | collective-permute-done | bytes 135200 | tf_op jit(solution)/shard_map/ppermute | solution.py:22
  13.2 0.1 collective-permute-done
  13.3 0.9 %broadcast_select_fusion = (bf16[528,128]{1,0:T(8,128)(2,1)S(1)}, bf16[528,128]{1,0:T(8,128)(2,1)S(1)}, bf16[528,128]{1,0:T(8,128)(2,1)S(1)}) fusion(pred[]{:T(512)S(6)} %eq.77, bf16[528,128]{1,0:T(8,128)(2,1)} %strip.1, bf16[528,128]{1,0:T(8,128)(2,1)S(1)} %collective-permute-done, pred[]{:T(512)S(6)} %le.2, bf16[528,128]{1,0:T(8,128)(2,1)S(1)} %collective-permute-done.1, ...), kind=kLoop, calls=%fused_computation.4 | loop fusion | flops 202752 | bytes 946178 | tf_op jit(solution)/shard_map/jit(_where)/select_n | solution.py:369
  14.3 1.8 %collective-permute-start.3 = (bf16[528,128]{1,0:T(8,128)(2,1)S(1)}, bf16[528,128]{1,0:T(8,128)(2,1)S(1)}, u32[]{:S(2)}, u32[]{:S(2)}) collective-permute-start(bf16[528,128]{1,0:T(8,128)(2,1)S(1)} %get-tuple-element.34), channel_id=1, source_target_pairs={{0,4},{1,5},{2,6},{3,7},{4,0},{5,1},{6,2},{7,3},{8,12},{9,13},{10,... | collective-permute-start | bytes 405512 | tf_op jit(solution)/shard_map/ppermute | solution.py:22
  16.1 1.0 %collective-permute-done.3 = bf16[528,128]{1,0:T(8,128)(2,1)S(1)} collective-permute-done((bf16[528,128]{1,0:T(8,128)(2,1)S(1)}, bf16[528,128]{1,0:T(8,128)(2,1)S(1)}, u32[]{:S(2)}, u32[]{:S(2)}) %collective-permute-start.3) | collective-permute-done | bytes 135200 | tf_op jit(solution)/shard_map/ppermute | solution.py:22
  17.1 3.0 %collective-permute-start.9 = (bf16[288,128]{1,0:T(8,128)(2,1)S(1)}, bf16[288,128]{1,0:T(8,128)(2,1)S(1)}, u32[]{:S(2)}, u32[]{:S(2)}) collective-permute-start(bf16[288,128]{1,0:T(8,128)(2,1)S(1)} %pad_maximum_fusion.1), channel_id=1, source_target_pairs={{0,24},{1,25},{2,26},{3,27},{4,28},{5,29},{6,30},{7,31},{8,12},{9,... | collective-permute-start | bytes 221192 | tf_op jit(solution)/shard_map/ppermute | solution.py:22
  20.0 0.5 collective-permute-start.8
  20.6 0.1 collective-permute-start.6
  20.7 3.3 %collective-permute-start.5 = (bf16[528,128]{1,0:T(8,128)(2,1)S(1)}, bf16[528,128]{1,0:T(8,128)(2,1)S(1)}, u32[]{:S(2)}, u32[]{:S(2)}) collective-permute-start(bf16[528,128]{1,0:T(8,128)(2,1)S(1)} %select_select_fusion.2), channel_id=1, source_target_pairs={{0,16},{1,17},{2,6},{3,7},{4,20},{5,21},{6,2},{7,3},{8,12},{9,13},... | collective-permute-start | bytes 405512 | tf_op jit(solution)/shard_map/ppermute | solution.py:22
  24.0 0.7 %collective-permute-done.8 = bf16[288,128]{1,0:T(8,128)(2,1)S(1)} collective-permute-done((bf16[288,128]{1,0:T(8,128)(2,1)S(1)}, bf16[288,128]{1,0:T(8,128)(2,1)S(1)}, u32[]{:S(2)}, u32[]{:S(2)}) %collective-permute-start.8) | collective-permute-done | bytes 73760 | tf_op jit(solution)/shard_map/ppermute | solution.py:22
  24.8 3.8 %collective-permute-start.12 = (bf16[288,128]{1,0:T(8,128)(2,1)S(1)}, bf16[288,128]{1,0:T(8,128)(2,1)S(1)}, u32[]{:S(2)}, u32[]{:S(2)}) collective-permute-start(bf16[288,128]{1,0:T(8,128)(2,1)S(1)} %select_select_fusion.4), channel_id=1, source_target_pairs={{0,96},{1,97},{2,98},{3,99},{4,100},{5,101},{6,102},{7,103},{8,104... | collective-permute-start | bytes 221192 | tf_op jit(solution)/shard_map/ppermute | solution.py:22
  28.6 2.4 %collective-permute-start.11 = (bf16[288,128]{1,0:T(8,128)(2,1)S(1)}, bf16[288,128]{1,0:T(8,128)(2,1)S(1)}, u32[]{:S(2)}, u32[]{:S(2)}) collective-permute-start(bf16[288,128]{1,0:T(8,128)(2,1)S(1)} %select_select_fusion.4), channel_id=1, source_target_pairs={{0,64},{1,65},{2,66},{3,67},{4,68},{5,69},{6,70},{7,71},{8,72},{9,... | collective-permute-start | bytes 221192 | tf_op jit(solution)/shard_map/ppermute | solution.py:22
  31.2 3.7 %collective-permute-start.16 = (bf16[1056,128]{1,0:T(8,128)(2,1)S(1)}, bf16[1056,128]{1,0:T(8,128)(2,1)S(1)}, u32[]{:S(2)}, u32[]{:S(2)}) collective-permute-start(bf16[1056,128]{1,0:T(8,128)(2,1)S(1)} %pad_maximum_fusion.m0), channel_id=1, source_target_pairs={{0,64},{1,65},{2,66},{3,67},{4,68},{5,69},{6,70},{7,71},{8,72},{9,... | collective-permute-start | bytes 811016 | tf_op jit(solution)/shard_map/ppermute | solution.py:22
  34.9 0.4 collective-permute-start.15
  35.3 1.1 %collective-permute-start.14 = (bf16[1056,128]{1,0:T(8,128)(2,1)S(1)}, bf16[1056,128]{1,0:T(8,128)(2,1)S(1)}, u32[]{:S(2)}, u32[]{:S(2)}) collective-permute-start(bf16[1056,128]{1,0:T(8,128)(2,1)S(1)} %pad_maximum_fusion.m0), channel_id=1, source_target_pairs={{0,32},{1,33},{2,34},{3,35},{4,36},{5,37},{6,38},{7,39},{8,40},{9,... | collective-permute-start | bytes 811016 | tf_op jit(solution)/shard_map/ppermute | solution.py:22
  36.4 2.0 %collective-permute-start.13 = (bf16[288,128]{1,0:T(8,128)(2,1)S(1)}, bf16[288,128]{1,0:T(8,128)(2,1)S(1)}, u32[]{:S(2)}, u32[]{:S(2)}) collective-permute-start(bf16[288,128]{1,0:T(8,128)(2,1)S(1)} %select_select_fusion.3.pair_ref), channel_id=1, source_target_pairs={{0,4},{1,5},{2,6},{3,7},{4,0},{5,1},{6,2},{7,3},{8,12},{9,13},{10,... | collective-permute-start | bytes 221192 | tf_op jit(solution)/shard_map/ppermute | solution.py:22
  38.4 0.1 collective-permute-start.17
  38.5 0.8 %collective-permute-done.13.other_ref = bf16[288,128]{1,0:T(8,128)(2,1)S(1)} collective-permute-done((bf16[288,128]{1,0:T(8,128)(2,1)S(1)}, bf16[288,128]{1,0:T(8,128)(2,1)S(1)}, u32[]{:S(2)}, u32[]{:S(2)}) %collective-permute-start.13) | collective-permute-done | bytes 73760 | tf_op jit(solution)/shard_map/ppermute | solution.py:22
  39.3 11.6 %factor.1 = (bf16[2,256,256]{2,1,0:T(8,128)(2,1)S(1)}, f32[128,128]{1,0:T(8,128)S(1)}) custom-call(s32[5]{0:T(128)S(1)} %stack.23.place, bf16[288,128]{1,0:T(8,128)(2,1)S(1)} %select_select_fusion.3.pair_ref, bf16[288,128]{1,0:T(8,128)(2,1)S(1)} %collective-permute-done.13.other_ref), custom_call_target="tpu_custom_call" | custom-call | flops 1000000 | bytes 65536 | tf_op jit(solution)/shard_map/factor/pallas_call | solution.py:217
  50.9 0.4 collective-permute-start.18
  51.4 0.2 collective-permute-start.19
  51.5 0.3 collective-permute-start.20
  52.0 0.6 collective-permute-done.18.t1
  52.6 0.4 collective-permute-done.19.t2
  53.0 0.4 collective-permute-done.20.t3
  53.4 8.9 %finish.1 = (bf16[4,128,32,128]{3,2,1,0:T(8,128)(2,1)}, f32[4,1,32]{2,1,0:T(1,128)}) custom-call(s32[5]{0:T(128)S(1)} %stack.23.place, bf16[4,128,32,128]{3,2,1,0:T(8,128)(2,1)S(1)} %bitcast.17, f32[4,32,128]{2,1,0:T(8,128)S(1)} %broadcast_in_dim.7.sc_ref, bf16[1056,128]{1,0:T(8,128)(2,1)S(1)} %pad_maximum_fusion.m0, ...), custom_call_target="tpu_custom_call" | custom-call | flops 2147483648 | bytes 12582912 | tf_op jit(solution)/shard_map/finish/pallas_call | solution.py:341
  (37 shorter events, 0.4 us)
Async XLA Ops:
  0.6 51.2 %copy-start.2 = (f32[4,1,32,1]{2,3,1,0:T(1,128)S(1)}, f32[4,1,32,1]{2,3,1,0:T(1,128)}, u32[]{:S(2)}) copy-start(f32[4,1,32,1]{2,3,1,0:T(1,128)} %param.3) | copy-start | bytes 1540
  3.2 48.7 %copy-start.1 = (bf16[528,128]{1,0:T(8,128)(2,1)S(1)}, bf16[528,128]{1,0:T(8,128)(2,1)}, u32[]{:S(2)}) copy-start(bf16[528,128]{1,0:T(8,128)(2,1)} %strip.1) | copy-start | bytes 405508
  3.2 6.8 %collective-permute-start.2 = (bf16[528,128]{1,0:T(8,128)(2,1)}, bf16[528,128]{1,0:T(8,128)(2,1)S(1)}, u32[]{:S(2)}, u32[]{:S(2)}) collective-permute-start(bf16[528,128]{1,0:T(8,128)(2,1)} %strip.1), channel_id=1, source_target_pairs={{0,2},{1,3},{2,0},{3,1},{4,6},{5,7},{6,4},{7,5},{8,10},{9,11},{10,... | collective-permute-start | bytes 405512 | tf_op jit(solution)/shard_map/ppermute | solution.py:22
  6.8 6.4 %collective-permute-start.1 = (bf16[528,128]{1,0:T(8,128)(2,1)}, bf16[528,128]{1,0:T(8,128)(2,1)S(1)}, u32[]{:S(2)}, u32[]{:S(2)}) collective-permute-start(bf16[528,128]{1,0:T(8,128)(2,1)} %strip.1), channel_id=1, source_target_pairs={{0,1},{1,0},{2,3},{3,2},{4,5},{5,4},{6,7},{7,6},{8,9},{9,8},{10,11... | collective-permute-start | bytes 405512 | tf_op jit(solution)/shard_map/ppermute | solution.py:22
  7.1 6.2 %collective-permute-start = (bf16[528,128]{1,0:T(8,128)(2,1)}, bf16[528,128]{1,0:T(8,128)(2,1)S(1)}, u32[]{:S(2)}, u32[]{:S(2)}) collective-permute-start(bf16[528,128]{1,0:T(8,128)(2,1)} %strip.1), channel_id=1, source_target_pairs={{0,3},{1,2},{2,1},{3,0},{4,7},{5,6},{6,5},{7,4},{8,11},{9,10},{10,... | collective-permute-start | bytes 405512 | tf_op jit(solution)/shard_map/ppermute | solution.py:22
  7.7 45.7 %copy-start = (bf16[4,1,128,32,1,128]{5,3,4,2,1,0:T(8,128)(2,1)S(1)}, bf16[4,1,128,32,1,128]{5,3,4,2,1,0:T(8,128)(2,1)}, u32[]{:S(2)}) copy-start(bf16[4,1,128,32,1,128]{5,3,4,2,1,0:T(8,128)(2,1)} %param.2) | copy-start | bytes 12582916
  14.3 2.8 %collective-permute-start.3 = (bf16[528,128]{1,0:T(8,128)(2,1)S(1)}, bf16[528,128]{1,0:T(8,128)(2,1)S(1)}, u32[]{:S(2)}, u32[]{:S(2)}) collective-permute-start(bf16[528,128]{1,0:T(8,128)(2,1)S(1)} %get-tuple-element.34), channel_id=1, source_target_pairs={{0,4},{1,5},{2,6},{3,7},{4,0},{5,1},{6,2},{7,3},{8,12},{9,13},{10,... | collective-permute-start | bytes 405512 | tf_op jit(solution)/shard_map/ppermute | solution.py:22
  17.1 7.0 %collective-permute-start.9 = (bf16[288,128]{1,0:T(8,128)(2,1)S(1)}, bf16[288,128]{1,0:T(8,128)(2,1)S(1)}, u32[]{:S(2)}, u32[]{:S(2)}) collective-permute-start(bf16[288,128]{1,0:T(8,128)(2,1)S(1)} %pad_maximum_fusion.1), channel_id=1, source_target_pairs={{0,24},{1,25},{2,26},{3,27},{4,28},{5,29},{6,30},{7,31},{8,12},{9,... | collective-permute-start | bytes 221192 | tf_op jit(solution)/shard_map/ppermute | solution.py:22
  20.0 4.7 %collective-permute-start.8 = (bf16[288,128]{1,0:T(8,128)(2,1)S(1)}, bf16[288,128]{1,0:T(8,128)(2,1)S(1)}, u32[]{:S(2)}, u32[]{:S(2)}) collective-permute-start(bf16[288,128]{1,0:T(8,128)(2,1)S(1)} %pad_maximum_fusion.1), channel_id=1, source_target_pairs={{0,16},{1,17},{2,18},{3,19},{4,20},{5,21},{6,22},{7,23},{8,12},{9,... | collective-permute-start | bytes 221192 | tf_op jit(solution)/shard_map/ppermute | solution.py:22
  20.6 4.2 %collective-permute-start.7 = (bf16[288,128]{1,0:T(8,128)(2,1)S(1)}, bf16[288,128]{1,0:T(8,128)(2,1)S(1)}, u32[]{:S(2)}, u32[]{:S(2)}) collective-permute-start(bf16[288,128]{1,0:T(8,128)(2,1)S(1)} %pad_maximum_fusion.1), channel_id=1, source_target_pairs={{0,8},{1,9},{2,10},{3,11},{4,12},{5,13},{6,14},{7,15},{8,0},{9,1},... | collective-permute-start | bytes 221192 | tf_op jit(solution)/shard_map/ppermute | solution.py:22
  20.6 10.5 %collective-permute-start.6 = (bf16[528,128]{1,0:T(8,128)(2,1)S(1)}, bf16[528,128]{1,0:T(8,128)(2,1)S(1)}, u32[]{:S(2)}, u32[]{:S(2)}) collective-permute-start(bf16[528,128]{1,0:T(8,128)(2,1)S(1)} %select_select_fusion.2), channel_id=1, source_target_pairs={{0,24},{1,25},{2,26},{3,27},{4,28},{5,29},{6,30},{7,31},{8,0},{9,1... | collective-permute-start | bytes 405512 | tf_op jit(solution)/shard_map/ppermute | solution.py:22
  20.7 10.4 %collective-permute-start.5 = (bf16[528,128]{1,0:T(8,128)(2,1)S(1)}, bf16[528,128]{1,0:T(8,128)(2,1)S(1)}, u32[]{:S(2)}, u32[]{:S(2)}) collective-permute-start(bf16[528,128]{1,0:T(8,128)(2,1)S(1)} %select_select_fusion.2), channel_id=1, source_target_pairs={{0,16},{1,17},{2,6},{3,7},{4,20},{5,21},{6,2},{7,3},{8,12},{9,13},... | collective-permute-start | bytes 405512 | tf_op jit(solution)/shard_map/ppermute | solution.py:22
  24.0 7.0 %collective-permute-start.4 = (bf16[528,128]{1,0:T(8,128)(2,1)S(1)}, bf16[528,128]{1,0:T(8,128)(2,1)S(1)}, u32[]{:S(2)}, u32[]{:S(2)}) collective-permute-start(bf16[528,128]{1,0:T(8,128)(2,1)S(1)} %select_select_fusion.2), channel_id=1, source_target_pairs={{0,8},{1,9},{2,10},{3,11},{4,12},{5,13},{6,14},{7,15},{8,16},{9,17... | collective-permute-start | bytes 405512 | tf_op jit(solution)/shard_map/ppermute | solution.py:22
  24.8 10.5 %collective-permute-start.12 = (bf16[288,128]{1,0:T(8,128)(2,1)S(1)}, bf16[288,128]{1,0:T(8,128)(2,1)S(1)}, u32[]{:S(2)}, u32[]{:S(2)}) collective-permute-start(bf16[288,128]{1,0:T(8,128)(2,1)S(1)} %select_select_fusion.4), channel_id=1, source_target_pairs={{0,96},{1,97},{2,98},{3,99},{4,100},{5,101},{6,102},{7,103},{8,104... | collective-permute-start | bytes 221192 | tf_op jit(solution)/shard_map/ppermute | solution.py:22
  28.6 7.8 %collective-permute-start.11 = (bf16[288,128]{1,0:T(8,128)(2,1)S(1)}, bf16[288,128]{1,0:T(8,128)(2,1)S(1)}, u32[]{:S(2)}, u32[]{:S(2)}) collective-permute-start(bf16[288,128]{1,0:T(8,128)(2,1)S(1)} %select_select_fusion.4), channel_id=1, source_target_pairs={{0,64},{1,65},{2,66},{3,67},{4,68},{5,69},{6,70},{7,71},{8,72},{9,... | collective-permute-start | bytes 221192 | tf_op jit(solution)/shard_map/ppermute | solution.py:22
  31.1 5.3 %collective-permute-start.10 = (bf16[288,128]{1,0:T(8,128)(2,1)S(1)}, bf16[288,128]{1,0:T(8,128)(2,1)S(1)}, u32[]{:S(2)}, u32[]{:S(2)}) collective-permute-start(bf16[288,128]{1,0:T(8,128)(2,1)S(1)} %select_select_fusion.4), channel_id=1, source_target_pairs={{0,32},{1,33},{2,34},{3,35},{4,36},{5,37},{6,38},{7,39},{8,40},{9,... | collective-permute-start | bytes 221192 | tf_op jit(solution)/shard_map/ppermute | solution.py:22
  31.2 19.8 %collective-permute-start.16 = (bf16[1056,128]{1,0:T(8,128)(2,1)S(1)}, bf16[1056,128]{1,0:T(8,128)(2,1)S(1)}, u32[]{:S(2)}, u32[]{:S(2)}) collective-permute-start(bf16[1056,128]{1,0:T(8,128)(2,1)S(1)} %pad_maximum_fusion.m0), channel_id=1, source_target_pairs={{0,64},{1,65},{2,66},{3,67},{4,68},{5,69},{6,70},{7,71},{8,72},{9,... | collective-permute-start | bytes 811016 | tf_op jit(solution)/shard_map/ppermute | solution.py:22
  34.9 16.0 %collective-permute-start.15 = (bf16[1056,128]{1,0:T(8,128)(2,1)S(1)}, bf16[1056,128]{1,0:T(8,128)(2,1)S(1)}, u32[]{:S(2)}, u32[]{:S(2)}) collective-permute-start(bf16[1056,128]{1,0:T(8,128)(2,1)S(1)} %pad_maximum_fusion.m0), channel_id=1, source_target_pairs={{0,96},{1,97},{2,98},{3,99},{4,100},{5,101},{6,102},{7,103},{8,104... | collective-permute-start | bytes 811016 | tf_op jit(solution)/shard_map/ppermute | solution.py:22
  35.3 15.7 %collective-permute-start.14 = (bf16[1056,128]{1,0:T(8,128)(2,1)S(1)}, bf16[1056,128]{1,0:T(8,128)(2,1)S(1)}, u32[]{:S(2)}, u32[]{:S(2)}) collective-permute-start(bf16[1056,128]{1,0:T(8,128)(2,1)S(1)} %pad_maximum_fusion.m0), channel_id=1, source_target_pairs={{0,32},{1,33},{2,34},{3,35},{4,36},{5,37},{6,38},{7,39},{8,40},{9,... | collective-permute-start | bytes 811016 | tf_op jit(solution)/shard_map/ppermute | solution.py:22
  36.4 2.9 %collective-permute-start.13 = (bf16[288,128]{1,0:T(8,128)(2,1)S(1)}, bf16[288,128]{1,0:T(8,128)(2,1)S(1)}, u32[]{:S(2)}, u32[]{:S(2)}) collective-permute-start(bf16[288,128]{1,0:T(8,128)(2,1)S(1)} %select_select_fusion.3.pair_ref), channel_id=1, source_target_pairs={{0,4},{1,5},{2,6},{3,7},{4,0},{5,1},{6,2},{7,3},{8,12},{9,13},{10,... | collective-permute-start | bytes 221192 | tf_op jit(solution)/shard_map/ppermute | solution.py:22
  38.4 13.5 %collective-permute-start.17 = (bf16[1056,128]{1,0:T(8,128)(2,1)S(1)}, bf16[1056,128]{1,0:T(8,128)(2,1)S(1)}, u32[]{:S(2)}, u32[]{:S(2)}) collective-permute-start(bf16[1056,128]{1,0:T(8,128)(2,1)S(1)} %pad_maximum_fusion.m0), channel_id=1, source_target_pairs={{0,4},{1,5},{2,6},{3,7},{4,0},{5,1},{6,2},{7,3},{8,12},{9,13},{10,... | collective-permute-start | bytes 811016 | tf_op jit(solution)/shard_map/ppermute | solution.py:22
  50.9 1.6 %collective-permute-start.18 = (bf16[1056,128]{1,0:T(8,128)(2,1)S(1)}, bf16[1056,128]{1,0:T(8,128)(2,1)S(1)}, u32[]{:S(2)}, u32[]{:S(2)}) collective-permute-start(bf16[1056,128]{1,0:T(8,128)(2,1)S(1)} %collective-permute-done.14.m1), channel_id=1, source_target_pairs={{0,4},{1,5},{2,6},{3,7},{4,0},{5,1},{6,2},{7,3},{8,12},{9,13},{10,... | collective-permute-start | bytes 811016 | tf_op jit(solution)/shard_map/ppermute | solution.py:22
  51.4 1.6 %collective-permute-start.19 = (bf16[1056,128]{1,0:T(8,128)(2,1)S(1)}, bf16[1056,128]{1,0:T(8,128)(2,1)S(1)}, u32[]{:S(2)}, u32[]{:S(2)}) collective-permute-start(bf16[1056,128]{1,0:T(8,128)(2,1)S(1)} %collective-permute-done.15.m2), channel_id=1, source_target_pairs={{0,4},{1,5},{2,6},{3,7},{4,0},{5,1},{6,2},{7,3},{8,12},{9,13},{10,... | collective-permute-start | bytes 811016 | tf_op jit(solution)/shard_map/ppermute | solution.py:22
  51.5 1.8 %collective-permute-start.20 = (bf16[1056,128]{1,0:T(8,128)(2,1)S(1)}, bf16[1056,128]{1,0:T(8,128)(2,1)S(1)}, u32[]{:S(2)}, u32[]{:S(2)}) collective-permute-start(bf16[1056,128]{1,0:T(8,128)(2,1)S(1)} %collective-permute-done.16.m3), channel_id=1, source_target_pairs={{0,4},{1,5},{2,6},{3,7},{4,0},{5,1},{6,2},{7,3},{8,12},{9,13},{10,... | collective-permute-start | bytes 811016 | tf_op jit(solution)/shard_map/ppermute | solution.py:22

commit v5 on v4

--- a/solution.py
+++ b/solution.py
@@ -369,7 +369,6 @@
     mine = jnp.where(k == x % 2, ours, permute(jnp.where(first == k, v, u), sibling))
     head = lambda w: jnp.concatenate([w[:BS], w[4 * BS :]], axis=0)
     pair = jnp.concatenate([jnp.where(first == 0, head(u), head(v)), jnp.where(first == 0, head(v), head(u))], axis=0)
-    pair, mine = lax.optimization_barrier((pair, mine))
     pair = lead_along(pair, y, 1)
     both = along_y(mine, y, x)
     pair = lead_along(pair, z, 0)

time: 62.4 us -> 61.6 us (0.987)
  starting transfers between devices: 27.7 us -> 26.9 us
    ppermute x21, starting transfers between devices: 27.7 us -> 26.9 us  [permute(): lax.ppermute(array, AXES, [(dev(*place), dev(*to(*place))) for place in P...]
  transfers between devices with their start and end apart: 21 -> 21, of which waited for: 9 -> 10; matrix products, arithmetic and copies ran while one was open for 1% -> 1% of each run, Pallas kernels for 19% -> 19%
where the time goes in v5:
time: 61.6 us; the launch traced here: 61.5 us
  starting transfers between devices  26.9 us (44%)
  Pallas kernels  23 us (37%)
  waiting for transfers between devices  9.43 us (15%)
  other arithmetic  1.26 us (2%)
  between operations  0.75 us (1%)
    ppermute x21, starting transfers between devices, permute(): lax.ppermute(array, AXES, [(dev(*place), dev(*to(*place))) for place in P...  26.9 us
    pallas_call x1, Pallas kernels, factor(): pl.pallas_call(factor_kernel, grid_spec=pltpu.PrefetchScalarGridSpec(num_...  11.6 us
    ppermute x21, waiting for transfers between devices, permute(): lax.ppermute(array, AXES, [(dev(*place), dev(*to(*place))) for place in P...  9.43 us
    pallas_call x1, Pallas kernels, finish(): pl.pallas_call(finish_kernel, grid_spec=spec, out_shape=[jax.ShapeDtypeSt...  8.85 us
    pallas_call x1, Pallas kernels, strip(): pl.pallas_call(strip_kernel, grid=(1,), in_specs=[pl.BlockSpec((4, BS, 16...  2.56 us
  transfers between devices with their start and end apart: 21, of which 10 were waited for; matrix products, arithmetic and copies ran while one was open for 1% of the time, Pallas kernels for 19%

profile of v5, /device:TPU:1, one launch (start us, length us, event | category | flops | bytes accessed | tf_op | source)
XLA Modules:
  0.0 61.5 jit_solution(3693388047727982595)
XLA Ops:
  0.6 2.6 %strip.1 = bf16[528,128]{1,0:T(8,128)(2,1)} custom-call(bf16[4,128,32,128]{3,2,1,0:T(8,128)(2,1)} %bitcast.16, f32[4,1,32]{2,1,0:T(1,128)} %bitcast.18), custom_call_target="tpu_custom_call" | custom-call | bytes 2097152 | tf_op jit(solution)/shard_map/strip/pallas_call | solution.py:42
  3.2 3.6 %collective-permute-start.2 = (bf16[528,128]{1,0:T(8,128)(2,1)}, bf16[528,128]{1,0:T(8,128)(2,1)S(1)}, u32[]{:S(2)}, u32[]{:S(2)}) collective-permute-start(bf16[528,128]{1,0:T(8,128)(2,1)} %strip.1), channel_id=1, source_target_pairs={{0,2},{1,3},{2,0},{3,1},{4,6},{5,7},{6,4},{7,5},{8,10},{9,11},{10,... | collective-permute-start | bytes 405512 | tf_op jit(solution)/shard_map/ppermute | solution.py:22
  6.8 0.3 collective-permute-start.1
  7.1 0.6 collective-permute-start
  7.7 2.2 %collective-permute-done.2 = bf16[528,128]{1,0:T(8,128)(2,1)S(1)} collective-permute-done((bf16[528,128]{1,0:T(8,128)(2,1)}, bf16[528,128]{1,0:T(8,128)(2,1)S(1)}, u32[]{:S(2)}, u32[]{:S(2)}) %collective-permute-start.2) | collective-permute-done | bytes 135200 | tf_op jit(solution)/shard_map/ppermute | solution.py:22
  10.0 3.2 %collective-permute-done.1 = bf16[528,128]{1,0:T(8,128)(2,1)S(1)} collective-permute-done((bf16[528,128]{1,0:T(8,128)(2,1)}, bf16[528,128]{1,0:T(8,128)(2,1)S(1)}, u32[]{:S(2)}, u32[]{:S(2)}) %collective-permute-start.1) | collective-permute-done | bytes 135200 | tf_op jit(solution)/shard_map/ppermute | solution.py:22
  13.2 0.1 collective-permute-done
  13.3 0.9 %broadcast_select_fusion.4 = (bf16[528,128]{1,0:T(8,128)(2,1)S(1)}, bf16[528,128]{1,0:T(8,128)(2,1)S(1)}, bf16[528,128]{1,0:T(8,128)(2,1)S(1)}) fusion(pred[]{:T(512)S(6)} %eq.76, bf16[528,128]{1,0:T(8,128)(2,1)} %strip.1, bf16[528,128]{1,0:T(8,128)(2,1)S(1)} %collective-permute-done, pred[]{:T(512)S(6)} %le.2, ...), kind=kLoop, calls=%fused_computation.8 | loop fusion | flops 202752 | bytes 946178 | tf_op jit(solution)/shard_map/jit(_where)/select_n | solution.py:369
  14.3 1.8 %collective-permute-start.3 = (bf16[528,128]{1,0:T(8,128)(2,1)S(1)}, bf16[528,128]{1,0:T(8,128)(2,1)S(1)}, u32[]{:S(2)}, u32[]{:S(2)}) collective-permute-start(bf16[528,128]{1,0:T(8,128)(2,1)S(1)} %get-tuple-element.30), channel_id=1, source_target_pairs={{0,4},{1,5},{2,6},{3,7},{4,0},{5,1},{6,2},{7,3},{8,12},{9,13},{10,... | collective-permute-start | bytes 405512 | tf_op jit(solution)/shard_map/ppermute | solution.py:22
  16.1 3.0 %collective-permute-start.9 = (bf16[288,128]{1,0:T(8,128)(2,1)S(1)}, bf16[288,128]{1,0:T(8,128)(2,1)S(1)}, u32[]{:S(2)}, u32[]{:S(2)}) collective-permute-start(bf16[288,128]{1,0:T(8,128)(2,1)S(1)} %pad_maximum_fusion.1), channel_id=1, source_target_pairs={{0,24},{1,25},{2,26},{3,27},{4,28},{5,29},{6,30},{7,31},{8,12},{9,... | collective-permute-start | bytes 221192 | tf_op jit(solution)/shard_map/ppermute | solution.py:22
  19.1 0.3 collective-permute-start.8
  19.4 0.7 %collective-permute-start.6 = (bf16[528,128]{1,0:T(8,128)(2,1)S(1)}, bf16[528,128]{1,0:T(8,128)(2,1)S(1)}, u32[]{:S(2)}, u32[]{:S(2)}) collective-permute-start(bf16[528,128]{1,0:T(8,128)(2,1)S(1)} %select_select_fusion.2), channel_id=1, source_target_pairs={{0,24},{1,25},{2,26},{3,27},{4,28},{5,29},{6,30},{7,31},{8,0},{9,1... | collective-permute-start | bytes 405512 | tf_op jit(solution)/shard_map/ppermute | solution.py:22
  20.0 2.8 %collective-permute-start.5 = (bf16[528,128]{1,0:T(8,128)(2,1)S(1)}, bf16[528,128]{1,0:T(8,128)(2,1)S(1)}, u32[]{:S(2)}, u32[]{:S(2)}) collective-permute-start(bf16[528,128]{1,0:T(8,128)(2,1)S(1)} %select_select_fusion.2), channel_id=1, source_target_pairs={{0,16},{1,17},{2,6},{3,7},{4,20},{5,21},{6,2},{7,3},{8,12},{9,13},... | collective-permute-start | bytes 405512 | tf_op jit(solution)/shard_map/ppermute | solution.py:22
  22.8 1.3 %collective-permute-done.8 = bf16[288,128]{1,0:T(8,128)(2,1)S(1)} collective-permute-done((bf16[288,128]{1,0:T(8,128)(2,1)S(1)}, bf16[288,128]{1,0:T(8,128)(2,1)S(1)}, u32[]{:S(2)}, u32[]{:S(2)}) %collective-permute-start.8) | collective-permute-done | bytes 73760 | tf_op jit(solution)/shard_map/ppermute | solution.py:22
  24.2 3.8 %collective-permute-start.12 = (bf16[288,128]{1,0:T(8,128)(2,1)S(1)}, bf16[288,128]{1,0:T(8,128)(2,1)S(1)}, u32[]{:S(2)}, u32[]{:S(2)}) collective-permute-start(bf16[288,128]{1,0:T(8,128)(2,1)S(1)} %select_select_fusion.4), channel_id=1, source_target_pairs={{0,96},{1,97},{2,98},{3,99},{4,100},{5,101},{6,102},{7,103},{8,104... | collective-permute-start | bytes 221192 | tf_op jit(solution)/shard_map/ppermute | solution.py:22
  28.0 1.6 %collective-permute-start.11 = (bf16[288,128]{1,0:T(8,128)(2,1)S(1)}, bf16[288,128]{1,0:T(8,128)(2,1)S(1)}, u32[]{:S(2)}, u32[]{:S(2)}) collective-permute-start(bf16[288,128]{1,0:T(8,128)(2,1)S(1)} %select_select_fusion.4), channel_id=1, source_target_pairs={{0,64},{1,65},{2,66},{3,67},{4,68},{5,69},{6,70},{7,71},{8,72},{9,... | collective-permute-start | bytes 221192 | tf_op jit(solution)/shard_map/ppermute | solution.py:22
  29.6 0.1 collective-permute-done.4
  29.8 3.7 %collective-permute-start.16 = (bf16[1056,128]{1,0:T(8,128)(2,1)S(1)}, bf16[1056,128]{1,0:T(8,128)(2,1)S(1)}, u32[]{:S(2)}, u32[]{:S(2)}) collective-permute-start(bf16[1056,128]{1,0:T(8,128)(2,1)S(1)} %pad_maximum_fusion.m0), channel_id=1, source_target_pairs={{0,64},{1,65},{2,66},{3,67},{4,68},{5,69},{6,70},{7,71},{8,72},{9,... | collective-permute-start | bytes 811016 | tf_op jit(solution)/shard_map/ppermute | solution.py:22
  33.5 0.4 collective-permute-start.15
  33.9 1.0 %collective-permute-start.14 = (bf16[1056,128]{1,0:T(8,128)(2,1)S(1)}, bf16[1056,128]{1,0:T(8,128)(2,1)S(1)}, u32[]{:S(2)}, u32[]{:S(2)}) collective-permute-start(bf16[1056,128]{1,0:T(8,128)(2,1)S(1)} %pad_maximum_fusion.m0), channel_id=1, source_target_pairs={{0,32},{1,33},{2,34},{3,35},{4,36},{5,37},{6,38},{7,39},{8,40},{9,... | collective-permute-start | bytes 811016 | tf_op jit(solution)/shard_map/ppermute | solution.py:22
  35.0 2.2 %collective-permute-start.13 = (bf16[288,128]{1,0:T(8,128)(2,1)S(1)}, bf16[288,128]{1,0:T(8,128)(2,1)S(1)}, u32[]{:S(2)}, u32[]{:S(2)}) collective-permute-start(bf16[288,128]{1,0:T(8,128)(2,1)S(1)} %select_select_fusion.3.pair_ref), channel_id=1, source_target_pairs={{0,4},{1,5},{2,6},{3,7},{4,0},{5,1},{6,2},{7,3},{8,12},{9,13},{10,... | collective-permute-start | bytes 221192 | tf_op jit(solution)/shard_map/ppermute | solution.py:22
  37.2 0.9 %collective-permute-done.13.other_ref = bf16[288,128]{1,0:T(8,128)(2,1)S(1)} collective-permute-done((bf16[288,128]{1,0:T(8,128)(2,1)S(1)}, bf16[288,128]{1,0:T(8,128)(2,1)S(1)}, u32[]{:S(2)}, u32[]{:S(2)}) %collective-permute-start.13) | collective-permute-done | bytes 73760 | tf_op jit(solution)/shard_map/ppermute | solution.py:22
  38.1 11.6 %factor.1 = (bf16[2,256,256]{2,1,0:T(8,128)(2,1)S(1)}, f32[128,128]{1,0:T(8,128)S(1)}) custom-call(s32[5]{0:T(128)S(1)} %stack.23.place, bf16[288,128]{1,0:T(8,128)(2,1)S(1)} %select_select_fusion.3.pair_ref, bf16[288,128]{1,0:T(8,128)(2,1)S(1)} %collective-permute-done.13.other_ref), custom_call_target="tpu_custom_call" | custom-call | flops 1000000 | bytes 65536 | tf_op jit(solution)/shard_map/factor/pallas_call | solution.py:217
  49.7 0.4 collective-permute-start.17
  50.1 0.3 collective-permute-start.18
  50.4 0.3 collective-permute-start.19
  50.7 0.2 collective-permute-start.20
  51.0 0.3 collective-permute-done.17.t0
  51.3 0.4 collective-permute-done.18.t1
  51.7 0.4 collective-permute-done.19.t2
  52.1 0.4 collective-permute-done.20.t3
  52.6 8.9 %finish.1 = (bf16[4,128,32,128]{3,2,1,0:T(8,128)(2,1)}, f32[4,1,32]{2,1,0:T(1,128)}) custom-call(s32[5]{0:T(128)S(1)} %stack.23.place, bf16[4,128,32,128]{3,2,1,0:T(8,128)(2,1)S(1)} %bitcast.17, f32[4,32,128]{2,1,0:T(8,128)S(1)} %broadcast_in_dim.7.sc_ref, bf16[1056,128]{1,0:T(8,128)(2,1)S(1)} %pad_maximum_fusion.m0, ...), custom_call_target="tpu_custom_call" | custom-call | flops 2147483648 | bytes 12582912 | tf_op jit(solution)/shard_map/finish/pallas_call | solution.py:341
  (37 shorter events, 0.5 us)
Async XLA Ops:
  0.6 50.3 %copy-start.2 = (f32[4,1,32,1]{2,3,1,0:T(1,128)S(1)}, f32[4,1,32,1]{2,3,1,0:T(1,128)}, u32[]{:S(2)}) copy-start(f32[4,1,32,1]{2,3,1,0:T(1,128)} %param.3) | copy-start | bytes 1540
  3.2 47.8 %copy-start.1 = (bf16[528,128]{1,0:T(8,128)(2,1)S(1)}, bf16[528,128]{1,0:T(8,128)(2,1)}, u32[]{:S(2)}) copy-start(bf16[528,128]{1,0:T(8,128)(2,1)} %strip.1) | copy-start | bytes 405508
  3.2 6.8 %collective-permute-start.2 = (bf16[528,128]{1,0:T(8,128)(2,1)}, bf16[528,128]{1,0:T(8,128)(2,1)S(1)}, u32[]{:S(2)}, u32[]{:S(2)}) collective-permute-start(bf16[528,128]{1,0:T(8,128)(2,1)} %strip.1), channel_id=1, source_target_pairs={{0,2},{1,3},{2,0},{3,1},{4,6},{5,7},{6,4},{7,5},{8,10},{9,11},{10,... | collective-permute-start | bytes 405512 | tf_op jit(solution)/shard_map/ppermute | solution.py:22
  6.8 6.4 %collective-permute-start.1 = (bf16[528,128]{1,0:T(8,128)(2,1)}, bf16[528,128]{1,0:T(8,128)(2,1)S(1)}, u32[]{:S(2)}, u32[]{:S(2)}) collective-permute-start(bf16[528,128]{1,0:T(8,128)(2,1)} %strip.1), channel_id=1, source_target_pairs={{0,1},{1,0},{2,3},{3,2},{4,5},{5,4},{6,7},{7,6},{8,9},{9,8},{10,11... | collective-permute-start | bytes 405512 | tf_op jit(solution)/shard_map/ppermute | solution.py:22
  7.1 6.2 %collective-permute-start = (bf16[528,128]{1,0:T(8,128)(2,1)}, bf16[528,128]{1,0:T(8,128)(2,1)S(1)}, u32[]{:S(2)}, u32[]{:S(2)}) collective-permute-start(bf16[528,128]{1,0:T(8,128)(2,1)} %strip.1), channel_id=1, source_target_pairs={{0,3},{1,2},{2,1},{3,0},{4,7},{5,6},{6,5},{7,4},{8,11},{9,10},{10,... | collective-permute-start | bytes 405512 | tf_op jit(solution)/shard_map/ppermute | solution.py:22
  7.7 44.9 %copy-start = (bf16[4,1,128,32,1,128]{5,3,4,2,1,0:T(8,128)(2,1)S(1)}, bf16[4,1,128,32,1,128]{5,3,4,2,1,0:T(8,128)(2,1)}, u32[]{:S(2)}) copy-start(bf16[4,1,128,32,1,128]{5,3,4,2,1,0:T(8,128)(2,1)} %param.2) | copy-start | bytes 12582916
  14.3 5.1 %collective-permute-start.3 = (bf16[528,128]{1,0:T(8,128)(2,1)S(1)}, bf16[528,128]{1,0:T(8,128)(2,1)S(1)}, u32[]{:S(2)}, u32[]{:S(2)}) collective-permute-start(bf16[528,128]{1,0:T(8,128)(2,1)S(1)} %get-tuple-element.30), channel_id=1, source_target_pairs={{0,4},{1,5},{2,6},{3,7},{4,0},{5,1},{6,2},{7,3},{8,12},{9,13},{10,... | collective-permute-start | bytes 405512 | tf_op jit(solution)/shard_map/ppermute | solution.py:22
  16.1 6.7 %collective-permute-start.9 = (bf16[288,128]{1,0:T(8,128)(2,1)S(1)}, bf16[288,128]{1,0:T(8,128)(2,1)S(1)}, u32[]{:S(2)}, u32[]{:S(2)}) collective-permute-start(bf16[288,128]{1,0:T(8,128)(2,1)S(1)} %pad_maximum_fusion.1), channel_id=1, source_target_pairs={{0,24},{1,25},{2,26},{3,27},{4,28},{5,29},{6,30},{7,31},{8,12},{9,... | collective-permute-start | bytes 221192 | tf_op jit(solution)/shard_map/ppermute | solution.py:22
  19.1 5.1 %collective-permute-start.8 = (bf16[288,128]{1,0:T(8,128)(2,1)S(1)}, bf16[288,128]{1,0:T(8,128)(2,1)S(1)}, u32[]{:S(2)}, u32[]{:S(2)}) collective-permute-start(bf16[288,128]{1,0:T(8,128)(2,1)S(1)} %pad_maximum_fusion.1), channel_id=1, source_target_pairs={{0,16},{1,17},{2,18},{3,19},{4,20},{5,21},{6,22},{7,23},{8,12},{9,... | collective-permute-start | bytes 221192 | tf_op jit(solution)/shard_map/ppermute | solution.py:22
  19.3 4.8 %collective-permute-start.7 = (bf16[288,128]{1,0:T(8,128)(2,1)S(1)}, bf16[288,128]{1,0:T(8,128)(2,1)S(1)}, u32[]{:S(2)}, u32[]{:S(2)}) collective-permute-start(bf16[288,128]{1,0:T(8,128)(2,1)S(1)} %pad_maximum_fusion.1), channel_id=1, source_target_pairs={{0,8},{1,9},{2,10},{3,11},{4,12},{5,13},{6,14},{7,15},{8,0},{9,1},... | collective-permute-start | bytes 221192 | tf_op jit(solution)/shard_map/ppermute | solution.py:22
  19.4 10.2 %collective-permute-start.6 = (bf16[528,128]{1,0:T(8,128)(2,1)S(1)}, bf16[528,128]{1,0:T(8,128)(2,1)S(1)}, u32[]{:S(2)}, u32[]{:S(2)}) collective-permute-start(bf16[528,128]{1,0:T(8,128)(2,1)S(1)} %select_select_fusion.2), channel_id=1, source_target_pairs={{0,24},{1,25},{2,26},{3,27},{4,28},{5,29},{6,30},{7,31},{8,0},{9,1... | collective-permute-start | bytes 405512 | tf_op jit(solution)/shard_map/ppermute | solution.py:22
  20.0 9.6 %collective-permute-start.5 = (bf16[528,128]{1,0:T(8,128)(2,1)S(1)}, bf16[528,128]{1,0:T(8,128)(2,1)S(1)}, u32[]{:S(2)}, u32[]{:S(2)}) collective-permute-start(bf16[528,128]{1,0:T(8,128)(2,1)S(1)} %select_select_fusion.2), channel_id=1, source_target_pairs={{0,16},{1,17},{2,6},{3,7},{4,20},{5,21},{6,2},{7,3},{8,12},{9,13},... | collective-permute-start | bytes 405512 | tf_op jit(solution)/shard_map/ppermute | solution.py:22
  22.8 6.9 %collective-permute-start.4 = (bf16[528,128]{1,0:T(8,128)(2,1)S(1)}, bf16[528,128]{1,0:T(8,128)(2,1)S(1)}, u32[]{:S(2)}, u32[]{:S(2)}) collective-permute-start(bf16[528,128]{1,0:T(8,128)(2,1)S(1)} %select_select_fusion.2), channel_id=1, source_target_pairs={{0,8},{1,9},{2,10},{3,11},{4,12},{5,13},{6,14},{7,15},{8,16},{9,17... | collective-permute-start | bytes 405512 | tf_op jit(solution)/shard_map/ppermute | solution.py:22
  24.2 9.7 %collective-permute-start.12 = (bf16[288,128]{1,0:T(8,128)(2,1)S(1)}, bf16[288,128]{1,0:T(8,128)(2,1)S(1)}, u32[]{:S(2)}, u32[]{:S(2)}) collective-permute-start(bf16[288,128]{1,0:T(8,128)(2,1)S(1)} %select_select_fusion.4), channel_id=1, source_target_pairs={{0,96},{1,97},{2,98},{3,99},{4,100},{5,101},{6,102},{7,103},{8,104... | collective-permute-start | bytes 221192 | tf_op jit(solution)/shard_map/ppermute | solution.py:22
  28.0 6.9 %collective-permute-start.11 = (bf16[288,128]{1,0:T(8,128)(2,1)S(1)}, bf16[288,128]{1,0:T(8,128)(2,1)S(1)}, u32[]{:S(2)}, u32[]{:S(2)}) collective-permute-start(bf16[288,128]{1,0:T(8,128)(2,1)S(1)} %select_select_fusion.4), channel_id=1, source_target_pairs={{0,64},{1,65},{2,66},{3,67},{4,68},{5,69},{6,70},{7,71},{8,72},{9,... | collective-permute-start | bytes 221192 | tf_op jit(solution)/shard_map/ppermute | solution.py:22
  29.6 5.3 %collective-permute-start.10 = (bf16[288,128]{1,0:T(8,128)(2,1)S(1)}, bf16[288,128]{1,0:T(8,128)(2,1)S(1)}, u32[]{:S(2)}, u32[]{:S(2)}) collective-permute-start(bf16[288,128]{1,0:T(8,128)(2,1)S(1)} %select_select_fusion.4), channel_id=1, source_target_pairs={{0,32},{1,33},{2,34},{3,35},{4,36},{5,37},{6,38},{7,39},{8,40},{9,... | collective-permute-start | bytes 221192 | tf_op jit(solution)/shard_map/ppermute | solution.py:22
  29.8 20.3 %collective-permute-start.16 = (bf16[1056,128]{1,0:T(8,128)(2,1)S(1)}, bf16[1056,128]{1,0:T(8,128)(2,1)S(1)}, u32[]{:S(2)}, u32[]{:S(2)}) collective-permute-start(bf16[1056,128]{1,0:T(8,128)(2,1)S(1)} %pad_maximum_fusion.m0), channel_id=1, source_target_pairs={{0,64},{1,65},{2,66},{3,67},{4,68},{5,69},{6,70},{7,71},{8,72},{9,... | collective-permute-start | bytes 811016 | tf_op jit(solution)/shard_map/ppermute | solution.py:22
  33.5 16.6 %collective-permute-start.15 = (bf16[1056,128]{1,0:T(8,128)(2,1)S(1)}, bf16[1056,128]{1,0:T(8,128)(2,1)S(1)}, u32[]{:S(2)}, u32[]{:S(2)}) collective-permute-start(bf16[1056,128]{1,0:T(8,128)(2,1)S(1)} %pad_maximum_fusion.m0), channel_id=1, source_target_pairs={{0,96},{1,97},{2,98},{3,99},{4,100},{5,101},{6,102},{7,103},{8,104... | collective-permute-start | bytes 811016 | tf_op jit(solution)/shard_map/ppermute | solution.py:22
  33.9 16.2 %collective-permute-start.14 = (bf16[1056,128]{1,0:T(8,128)(2,1)S(1)}, bf16[1056,128]{1,0:T(8,128)(2,1)S(1)}, u32[]{:S(2)}, u32[]{:S(2)}) collective-permute-start(bf16[1056,128]{1,0:T(8,128)(2,1)S(1)} %pad_maximum_fusion.m0), channel_id=1, source_target_pairs={{0,32},{1,33},{2,34},{3,35},{4,36},{5,37},{6,38},{7,39},{8,40},{9,... | collective-permute-start | bytes 811016 | tf_op jit(solution)/shard_map/ppermute | solution.py:22
  35.0 3.2 %collective-permute-start.13 = (bf16[288,128]{1,0:T(8,128)(2,1)S(1)}, bf16[288,128]{1,0:T(8,128)(2,1)S(1)}, u32[]{:S(2)}, u32[]{:S(2)}) collective-permute-start(bf16[288,128]{1,0:T(8,128)(2,1)S(1)} %select_select_fusion.3.pair_ref), channel_id=1, source_target_pairs={{0,4},{1,5},{2,6},{3,7},{4,0},{5,1},{6,2},{7,3},{8,12},{9,13},{10,... | collective-permute-start | bytes 221192 | tf_op jit(solution)/shard_map/ppermute | solution.py:22
  49.7 1.6 %collective-permute-start.17 = (bf16[1056,128]{1,0:T(8,128)(2,1)S(1)}, bf16[1056,128]{1,0:T(8,128)(2,1)S(1)}, u32[]{:S(2)}, u32[]{:S(2)}) collective-permute-start(bf16[1056,128]{1,0:T(8,128)(2,1)S(1)} %pad_maximum_fusion.m0), channel_id=1, source_target_pairs={{0,4},{1,5},{2,6},{3,7},{4,0},{5,1},{6,2},{7,3},{8,12},{9,13},{10,... | collective-permute-start | bytes 811016 | tf_op jit(solution)/shard_map/ppermute | solution.py:22
  50.1 1.6 %collective-permute-start.18 = (bf16[1056,128]{1,0:T(8,128)(2,1)S(1)}, bf16[1056,128]{1,0:T(8,128)(2,1)S(1)}, u32[]{:S(2)}, u32[]{:S(2)}) collective-permute-start(bf16[1056,128]{1,0:T(8,128)(2,1)S(1)} %collective-permute-done.14.m1), channel_id=1, source_target_pairs={{0,4},{1,5},{2,6},{3,7},{4,0},{5,1},{6,2},{7,3},{8,12},{9,13},{10,... | collective-permute-start | bytes 811016 | tf_op jit(solution)/shard_map/ppermute | solution.py:22
  50.4 1.8 %collective-permute-start.19 = (bf16[1056,128]{1,0:T(8,128)(2,1)S(1)}, bf16[1056,128]{1,0:T(8,128)(2,1)S(1)}, u32[]{:S(2)}, u32[]{:S(2)}) collective-permute-start(bf16[1056,128]{1,0:T(8,128)(2,1)S(1)} %collective-permute-done.15.m2), channel_id=1, source_target_pairs={{0,4},{1,5},{2,6},{3,7},{4,0},{5,1},{6,2},{7,3},{8,12},{9,13},{10,... | collective-permute-start | bytes 811016 | tf_op jit(solution)/shard_map/ppermute | solution.py:22
  50.7 1.8 %collective-permute-start.20 = (bf16[1056,128]{1,0:T(8,128)(2,1)S(1)}, bf16[1056,128]{1,0:T(8,128)(2,1)S(1)}, u32[]{:S(2)}, u32[]{:S(2)}) collective-permute-start(bf16[1056,128]{1,0:T(8,128)(2,1)S(1)} %collective-permute-done.16.m3), channel_id=1, source_target_pairs={{0,4},{1,5},{2,6},{3,7},{4,0},{5,1},{6,2},{7,3},{8,12},{9,13},{10,... | collective-permute-start | bytes 811016 | tf_op jit(solution)/shard_map/ppermute | solution.py:22

commit v6 on v5

--- a/solution.py
+++ b/solution.py
@@ -365,8 +365,8 @@
     place = jnp.stack([row, col, k, z, first]).astype(jnp.int32)
     got = along_x(piece, x)
     u, v = by_column(piece, got, x)
-    ours = jnp.where(first == k, u, v)
-    mine = jnp.where(k == x % 2, ours, permute(jnp.where(first == k, v, u), sibling))
+    ours = jnp.where(x <= 1, piece, got[2])
+    mine = jnp.where(k == x % 2, ours, permute(jnp.where(x <= 1, got[0], got[1]), sibling))
     head = lambda w: jnp.concatenate([w[:BS], w[4 * BS :]], axis=0)
     pair = jnp.concatenate([jnp.where(first == 0, head(u), head(v)), jnp.where(first == 0, head(v), head(u))], axis=0)
     pair = lead_along(pair, y, 1)

time: 61.6 us -> 62.7 us (1.018)
  other arithmetic: 1.26 us -> 2.17 us
    select_n x2, other arithmetic: 0.99 us -> 1.89 us  [the longest x1 0.95 us: by_column(): u = jnp.where(x <= 1, array, got[1])]
  transfers between devices with their start and end apart: 21 -> 21, of which waited for: 10 -> 10; matrix products, arithmetic and copies ran while one was open for 1% -> 2% of each run, Pallas kernels for 19% -> 18%
where the time goes in v6:
time: 62.7 us; the launch traced here: 62.5 us
  starting transfers between devices  26.4 us (42%)
  Pallas kernels  23 us (37%)
  waiting for transfers between devices  10 us (16%)
  other arithmetic  2.17 us (3%)
  between operations  0.75 us (1%)
    ppermute x21, starting transfers between devices, permute(): lax.ppermute(array, AXES, [(dev(*place), dev(*to(*place))) for place in P...  26.4 us
    pallas_call x1, Pallas kernels, factor(): pl.pallas_call(factor_kernel, grid_spec=pltpu.PrefetchScalarGridSpec(num_...  11.6 us
    ppermute x21, waiting for transfers between devices, permute(): lax.ppermute(array, AXES, [(dev(*place), dev(*to(*place))) for place in P...  10 us
    pallas_call x1, Pallas kernels, finish(): pl.pallas_call(finish_kernel, grid_spec=spec, out_shape=[jax.ShapeDtypeSt...  8.85 us
    pallas_call x1, Pallas kernels, strip(): pl.pallas_call(strip_kernel, grid=(1,), in_specs=[pl.BlockSpec((4, BS, 16...  2.56 us
  transfers between devices with their start and end apart: 21, of which 10 were waited for; matrix products, arithmetic and copies ran while one was open for 2% of the time, Pallas kernels for 18%

profile of v6, /device:TPU:1, one launch (start us, length us, event | category | flops | bytes accessed | tf_op | source)
XLA Modules:
  0.0 62.5 jit_solution(1588247789017328062)
XLA Ops:
  0.6 2.6 %strip.1 = bf16[528,128]{1,0:T(8,128)(2,1)} custom-call(bf16[4,128,32,128]{3,2,1,0:T(8,128)(2,1)} %bitcast.16, f32[4,1,32]{2,1,0:T(1,128)} %bitcast.18), custom_call_target="tpu_custom_call" | custom-call | bytes 2097152 | tf_op jit(solution)/shard_map/strip/pallas_call | solution.py:42
  3.2 3.3 %collective-permute-start.2 = (bf16[528,128]{1,0:T(8,128)(2,1)}, bf16[528,128]{1,0:T(8,128)(2,1)S(1)}, u32[]{:S(2)}, u32[]{:S(2)}) collective-permute-start(bf16[528,128]{1,0:T(8,128)(2,1)} %strip.1), channel_id=1, source_target_pairs={{0,3},{1,2},{2,1},{3,0},{4,7},{5,6},{6,5},{7,4},{8,11},{9,10},{10,... | collective-permute-start | bytes 405512 | tf_op jit(solution)/shard_map/ppermute | solution.py:22
  6.5 1.2 %collective-permute-start = (bf16[528,128]{1,0:T(8,128)(2,1)}, bf16[528,128]{1,0:T(8,128)(2,1)S(1)}, u32[]{:S(2)}, u32[]{:S(2)}) collective-permute-start(bf16[528,128]{1,0:T(8,128)(2,1)} %strip.1), channel_id=1, source_target_pairs={{0,2},{1,3},{2,0},{3,1},{4,6},{5,7},{6,4},{7,5},{8,10},{9,11},{10,... | collective-permute-start | bytes 405512 | tf_op jit(solution)/shard_map/ppermute | solution.py:22
  7.8 1.9 %collective-permute-done.2 = bf16[528,128]{1,0:T(8,128)(2,1)S(1)} collective-permute-done((bf16[528,128]{1,0:T(8,128)(2,1)}, bf16[528,128]{1,0:T(8,128)(2,1)S(1)}, u32[]{:S(2)}, u32[]{:S(2)}) %collective-permute-start.2) | collective-permute-done | bytes 135200 | tf_op jit(solution)/shard_map/ppermute | solution.py:22
  9.7 1.1 %collective-permute-done.1 = bf16[528,128]{1,0:T(8,128)(2,1)S(1)} collective-permute-done((bf16[528,128]{1,0:T(8,128)(2,1)}, bf16[528,128]{1,0:T(8,128)(2,1)S(1)}, u32[]{:S(2)}, u32[]{:S(2)}) %collective-permute-start.1) | collective-permute-done | bytes 135200 | tf_op jit(solution)/shard_map/ppermute | solution.py:22
  10.9 3.0 %collective-permute-done = bf16[528,128]{1,0:T(8,128)(2,1)S(1)} collective-permute-done((bf16[528,128]{1,0:T(8,128)(2,1)}, bf16[528,128]{1,0:T(8,128)(2,1)S(1)}, u32[]{:S(2)}, u32[]{:S(2)}) %collective-permute-start) | collective-permute-done | bytes 135200 | tf_op jit(solution)/shard_map/ppermute | solution.py:22
  13.8 0.9 %broadcast_select_fusion.3 = (bf16[528,128]{1,0:T(8,128)(2,1)S(1)}, bf16[528,128]{1,0:T(8,128)(2,1)S(1)}, bf16[528,128]{1,0:T(8,128)(2,1)S(1)}) fusion(bf16[528,128]{1,0:T(8,128)(2,1)} %strip.1, bf16[528,128]{1,0:T(8,128)(2,1)S(1)} %collective-permute-done.2, pred[]{:T(512)S(6)} %le.2, bf16[528,128]{1,0:T(8,128)(2,1)S(1)} %collective-permute-done.1, ...), kind=kLoop, calls=%fused_computation.7 | loop fusion | flops 202752 | bytes 946177 | tf_op jit(solution)/shard_map/jit(_where)/select_n | solution.py:65
  14.8 1.7 %collective-permute-start.3 = (bf16[528,128]{1,0:T(8,128)(2,1)S(1)}, bf16[528,128]{1,0:T(8,128)(2,1)S(1)}, u32[]{:S(2)}, u32[]{:S(2)}) collective-permute-start(bf16[528,128]{1,0:T(8,128)(2,1)S(1)} %get-tuple-element.33), channel_id=1, source_target_pairs={{0,4},{1,5},{2,6},{3,7},{4,0},{5,1},{6,2},{7,3},{8,12},{9,13},{10,... | collective-permute-start | bytes 405512 | tf_op jit(solution)/shard_map/ppermute | solution.py:22
  16.5 2.9 %collective-permute-start.9 = (bf16[288,128]{1,0:T(8,128)(2,1)S(1)}, bf16[288,128]{1,0:T(8,128)(2,1)S(1)}, u32[]{:S(2)}, u32[]{:S(2)}) collective-permute-start(bf16[288,128]{1,0:T(8,128)(2,1)S(1)} %pad_maximum_fusion.1), channel_id=1, source_target_pairs={{0,24},{1,25},{2,26},{3,27},{4,28},{5,29},{6,30},{7,31},{8,12},{9,... | collective-permute-start | bytes 221192 | tf_op jit(solution)/shard_map/ppermute | solution.py:22
  19.5 0.3 collective-permute-start.8
  19.7 0.9 %select_select_fusion.2 = bf16[528,128]{1,0:T(8,128)(2,1)S(1)} fusion(bf16[528,128]{1,0:T(8,128)(2,1)S(1)} %collective-permute-done.3, bf16[528,128]{1,0:T(8,128)(2,1)} %strip.1, bf16[528,128]{1,0:T(8,128)(2,1)S(1)} %collective-permute-done, pred[]{:T(512)S(6)} %le.2, pred[]{:T(512)S(6)} %eq.71), kind=kLoop, calls=%fused_computation.3 | loop fusion | flops 135168 | bytes 540674 | tf_op jit(solution)/shard_map/jit(_where)/select_n | solution.py:369
  20.7 0.7 %collective-permute-start.6 = (bf16[528,128]{1,0:T(8,128)(2,1)S(1)}, bf16[528,128]{1,0:T(8,128)(2,1)S(1)}, u32[]{:S(2)}, u32[]{:S(2)}) collective-permute-start(bf16[528,128]{1,0:T(8,128)(2,1)S(1)} %select_select_fusion.2), channel_id=1, source_target_pairs={{0,24},{1,25},{2,26},{3,27},{4,28},{5,29},{6,30},{7,31},{8,0},{9,1... | collective-permute-start | bytes 405512 | tf_op jit(solution)/shard_map/ppermute | solution.py:22
  21.3 2.8 %collective-permute-start.5 = (bf16[528,128]{1,0:T(8,128)(2,1)S(1)}, bf16[528,128]{1,0:T(8,128)(2,1)S(1)}, u32[]{:S(2)}, u32[]{:S(2)}) collective-permute-start(bf16[528,128]{1,0:T(8,128)(2,1)S(1)} %select_select_fusion.2), channel_id=1, source_target_pairs={{0,16},{1,17},{2,6},{3,7},{4,20},{5,21},{6,2},{7,3},{8,12},{9,13},... | collective-permute-start | bytes 405512 | tf_op jit(solution)/shard_map/ppermute | solution.py:22
  24.1 0.4 collective-permute-done.8
  24.6 3.8 %collective-permute-start.12 = (bf16[288,128]{1,0:T(8,128)(2,1)S(1)}, bf16[288,128]{1,0:T(8,128)(2,1)S(1)}, u32[]{:S(2)}, u32[]{:S(2)}) collective-permute-start(bf16[288,128]{1,0:T(8,128)(2,1)S(1)} %select_select_fusion.4), channel_id=1, source_target_pairs={{0,96},{1,97},{2,98},{3,99},{4,100},{5,101},{6,102},{7,103},{8,104... | collective-permute-start | bytes 221192 | tf_op jit(solution)/shard_map/ppermute | solution.py:22
  28.4 1.0 %collective-permute-start.11 = (bf16[288,128]{1,0:T(8,128)(2,1)S(1)}, bf16[288,128]{1,0:T(8,128)(2,1)S(1)}, u32[]{:S(2)}, u32[]{:S(2)}) collective-permute-start(bf16[288,128]{1,0:T(8,128)(2,1)S(1)} %select_select_fusion.4), channel_id=1, source_target_pairs={{0,64},{1,65},{2,66},{3,67},{4,68},{5,69},{6,70},{7,71},{8,72},{9,... | collective-permute-start | bytes 221192 | tf_op jit(solution)/shard_map/ppermute | solution.py:22
  29.4 1.1 %collective-permute-done.4 = bf16[528,128]{1,0:T(8,128)(2,1)S(1)} collective-permute-done((bf16[528,128]{1,0:T(8,128)(2,1)S(1)}, bf16[528,128]{1,0:T(8,128)(2,1)S(1)}, u32[]{:S(2)}, u32[]{:S(2)}) %collective-permute-start.4) | collective-permute-done | bytes 135200 | tf_op jit(solution)/shard_map/ppermute | solution.py:22
  30.6 3.7 %collective-permute-start.16 = (bf16[1056,128]{1,0:T(8,128)(2,1)S(1)}, bf16[1056,128]{1,0:T(8,128)(2,1)S(1)}, u32[]{:S(2)}, u32[]{:S(2)}) collective-permute-start(bf16[1056,128]{1,0:T(8,128)(2,1)S(1)} %pad_maximum_fusion.m0), channel_id=1, source_target_pairs={{0,64},{1,65},{2,66},{3,67},{4,68},{5,69},{6,70},{7,71},{8,72},{9,... | collective-permute-start | bytes 811016 | tf_op jit(solution)/shard_map/ppermute | solution.py:22
  34.3 0.4 collective-permute-start.15
  34.7 1.0 %collective-permute-start.14 = (bf16[1056,128]{1,0:T(8,128)(2,1)S(1)}, bf16[1056,128]{1,0:T(8,128)(2,1)S(1)}, u32[]{:S(2)}, u32[]{:S(2)}) collective-permute-start(bf16[1056,128]{1,0:T(8,128)(2,1)S(1)} %pad_maximum_fusion.m0), channel_id=1, source_target_pairs={{0,32},{1,33},{2,34},{3,35},{4,36},{5,37},{6,38},{7,39},{8,40},{9,... | collective-permute-start | bytes 811016 | tf_op jit(solution)/shard_map/ppermute | solution.py:22
  35.8 2.5 %collective-permute-start.13 = (bf16[288,128]{1,0:T(8,128)(2,1)S(1)}, bf16[288,128]{1,0:T(8,128)(2,1)S(1)}, u32[]{:S(2)}, u32[]{:S(2)}) collective-permute-start(bf16[288,128]{1,0:T(8,128)(2,1)S(1)} %select_select_fusion.3.pair_ref), channel_id=1, source_target_pairs={{0,4},{1,5},{2,6},{3,7},{4,0},{5,1},{6,2},{7,3},{8,12},{9,13},{10,... | collective-permute-start | bytes 221192 | tf_op jit(solution)/shard_map/ppermute | solution.py:22
  38.3 0.9 %collective-permute-done.13.other_ref = bf16[288,128]{1,0:T(8,128)(2,1)S(1)} collective-permute-done((bf16[288,128]{1,0:T(8,128)(2,1)S(1)}, bf16[288,128]{1,0:T(8,128)(2,1)S(1)}, u32[]{:S(2)}, u32[]{:S(2)}) %collective-permute-start.13) | collective-permute-done | bytes 73760 | tf_op jit(solution)/shard_map/ppermute | solution.py:22
  39.2 11.6 %factor.1 = (bf16[2,256,256]{2,1,0:T(8,128)(2,1)S(1)}, f32[128,128]{1,0:T(8,128)S(1)}) custom-call(s32[5]{0:T(128)S(1)} %stack.23.place, bf16[288,128]{1,0:T(8,128)(2,1)S(1)} %select_select_fusion.3.pair_ref, bf16[288,128]{1,0:T(8,128)(2,1)S(1)} %collective-permute-done.13.other_ref), custom_call_target="tpu_custom_call" | custom-call | flops 1000000 | bytes 65536 | tf_op jit(solution)/shard_map/factor/pallas_call | solution.py:217
  50.8 0.4 collective-permute-start.17
  51.2 0.3 collective-permute-start.18
  51.4 0.3 collective-permute-start.19
  51.8 0.2 collective-permute-start.20
  52.1 0.3 collective-permute-done.17.t0
  52.4 0.4 collective-permute-done.18.t1
  52.8 0.4 collective-permute-done.19.t2
  53.2 0.4 collective-permute-done.20.t3
  53.7 8.9 %finish.1 = (bf16[4,128,32,128]{3,2,1,0:T(8,128)(2,1)}, f32[4,1,32]{2,1,0:T(1,128)}) custom-call(s32[5]{0:T(128)S(1)} %stack.23.place, bf16[4,128,32,128]{3,2,1,0:T(8,128)(2,1)S(1)} %bitcast.17, f32[4,32,128]{2,1,0:T(8,128)S(1)} %broadcast_in_dim.7.sc_ref, bf16[1056,128]{1,0:T(8,128)(2,1)S(1)} %pad_maximum_fusion.m0, ...), custom_call_target="tpu_custom_call" | custom-call | flops 2147483648 | bytes 12582912 | tf_op jit(solution)/shard_map/finish/pallas_call | solution.py:341
  (37 shorter events, 0.5 us)
Async XLA Ops:
  0.6 51.3 %copy-start.2 = (f32[4,1,32,1]{2,3,1,0:T(1,128)S(1)}, f32[4,1,32,1]{2,3,1,0:T(1,128)}, u32[]{:S(2)}) copy-start(f32[4,1,32,1]{2,3,1,0:T(1,128)} %param.3) | copy-start | bytes 1540
  3.2 48.8 %copy-start.1 = (bf16[528,128]{1,0:T(8,128)(2,1)S(1)}, bf16[528,128]{1,0:T(8,128)(2,1)}, u32[]{:S(2)}) copy-start(bf16[528,128]{1,0:T(8,128)(2,1)} %strip.1) | copy-start | bytes 405508
  3.2 6.5 %collective-permute-start.2 = (bf16[528,128]{1,0:T(8,128)(2,1)}, bf16[528,128]{1,0:T(8,128)(2,1)S(1)}, u32[]{:S(2)}, u32[]{:S(2)}) collective-permute-start(bf16[528,128]{1,0:T(8,128)(2,1)} %strip.1), channel_id=1, source_target_pairs={{0,3},{1,2},{2,1},{3,0},{4,7},{5,6},{6,5},{7,4},{8,11},{9,10},{10,... | collective-permute-start | bytes 405512 | tf_op jit(solution)/shard_map/ppermute | solution.py:22
  6.5 4.4 %collective-permute-start.1 = (bf16[528,128]{1,0:T(8,128)(2,1)}, bf16[528,128]{1,0:T(8,128)(2,1)S(1)}, u32[]{:S(2)}, u32[]{:S(2)}) collective-permute-start(bf16[528,128]{1,0:T(8,128)(2,1)} %strip.1), channel_id=1, source_target_pairs={{0,1},{1,0},{2,3},{3,2},{4,5},{5,4},{6,7},{7,6},{8,9},{9,8},{10,11... | collective-permute-start | bytes 405512 | tf_op jit(solution)/shard_map/ppermute | solution.py:22
  6.5 7.3 %collective-permute-start = (bf16[528,128]{1,0:T(8,128)(2,1)}, bf16[528,128]{1,0:T(8,128)(2,1)S(1)}, u32[]{:S(2)}, u32[]{:S(2)}) collective-permute-start(bf16[528,128]{1,0:T(8,128)(2,1)} %strip.1), channel_id=1, source_target_pairs={{0,2},{1,3},{2,0},{3,1},{4,6},{5,7},{6,4},{7,5},{8,10},{9,11},{10,... | collective-permute-start | bytes 405512 | tf_op jit(solution)/shard_map/ppermute | solution.py:22
  7.8 45.9 %copy-start = (bf16[4,1,128,32,1,128]{5,3,4,2,1,0:T(8,128)(2,1)S(1)}, bf16[4,1,128,32,1,128]{5,3,4,2,1,0:T(8,128)(2,1)}, u32[]{:S(2)}) copy-start(bf16[4,1,128,32,1,128]{5,3,4,2,1,0:T(8,128)(2,1)} %param.2) | copy-start | bytes 12582916
  14.8 4.9 %collective-permute-start.3 = (bf16[528,128]{1,0:T(8,128)(2,1)S(1)}, bf16[528,128]{1,0:T(8,128)(2,1)S(1)}, u32[]{:S(2)}, u32[]{:S(2)}) collective-permute-start(bf16[528,128]{1,0:T(8,128)(2,1)S(1)} %get-tuple-element.33), channel_id=1, source_target_pairs={{0,4},{1,5},{2,6},{3,7},{4,0},{5,1},{6,2},{7,3},{8,12},{9,13},{10,... | collective-permute-start | bytes 405512 | tf_op jit(solution)/shard_map/ppermute | solution.py:22
  16.5 7.6 %collective-permute-start.9 = (bf16[288,128]{1,0:T(8,128)(2,1)S(1)}, bf16[288,128]{1,0:T(8,128)(2,1)S(1)}, u32[]{:S(2)}, u32[]{:S(2)}) collective-permute-start(bf16[288,128]{1,0:T(8,128)(2,1)S(1)} %pad_maximum_fusion.1), channel_id=1, source_target_pairs={{0,24},{1,25},{2,26},{3,27},{4,28},{5,29},{6,30},{7,31},{8,12},{9,... | collective-permute-start | bytes 221192 | tf_op jit(solution)/shard_map/ppermute | solution.py:22
  19.5 5.1 %collective-permute-start.8 = (bf16[288,128]{1,0:T(8,128)(2,1)S(1)}, bf16[288,128]{1,0:T(8,128)(2,1)S(1)}, u32[]{:S(2)}, u32[]{:S(2)}) collective-permute-start(bf16[288,128]{1,0:T(8,128)(2,1)S(1)} %pad_maximum_fusion.1), channel_id=1, source_target_pairs={{0,16},{1,17},{2,18},{3,19},{4,20},{5,21},{6,22},{7,23},{8,12},{9,... | collective-permute-start | bytes 221192 | tf_op jit(solution)/shard_map/ppermute | solution.py:22
  19.7 4.8 %collective-permute-start.7 = (bf16[288,128]{1,0:T(8,128)(2,1)S(1)}, bf16[288,128]{1,0:T(8,128)(2,1)S(1)}, u32[]{:S(2)}, u32[]{:S(2)}) collective-permute-start(bf16[288,128]{1,0:T(8,128)(2,1)S(1)} %pad_maximum_fusion.1), channel_id=1, source_target_pairs={{0,8},{1,9},{2,10},{3,11},{4,12},{5,13},{6,14},{7,15},{8,0},{9,1},... | collective-permute-start | bytes 221192 | tf_op jit(solution)/shard_map/ppermute | solution.py:22
  20.7 8.7 %collective-permute-start.6 = (bf16[528,128]{1,0:T(8,128)(2,1)S(1)}, bf16[528,128]{1,0:T(8,128)(2,1)S(1)}, u32[]{:S(2)}, u32[]{:S(2)}) collective-permute-start(bf16[528,128]{1,0:T(8,128)(2,1)S(1)} %select_select_fusion.2), channel_id=1, source_target_pairs={{0,24},{1,25},{2,26},{3,27},{4,28},{5,29},{6,30},{7,31},{8,0},{9,1... | collective-permute-start | bytes 405512 | tf_op jit(solution)/shard_map/ppermute | solution.py:22
  21.3 8.1 %collective-permute-start.5 = (bf16[528,128]{1,0:T(8,128)(2,1)S(1)}, bf16[528,128]{1,0:T(8,128)(2,1)S(1)}, u32[]{:S(2)}, u32[]{:S(2)}) collective-permute-start(bf16[528,128]{1,0:T(8,128)(2,1)S(1)} %select_select_fusion.2), channel_id=1, source_target_pairs={{0,16},{1,17},{2,6},{3,7},{4,20},{5,21},{6,2},{7,3},{8,12},{9,13},... | collective-permute-start | bytes 405512 | tf_op jit(solution)/shard_map/ppermute | solution.py:22
  24.1 6.4 %collective-permute-start.4 = (bf16[528,128]{1,0:T(8,128)(2,1)S(1)}, bf16[528,128]{1,0:T(8,128)(2,1)S(1)}, u32[]{:S(2)}, u32[]{:S(2)}) collective-permute-start(bf16[528,128]{1,0:T(8,128)(2,1)S(1)} %select_select_fusion.2), channel_id=1, source_target_pairs={{0,8},{1,9},{2,10},{3,11},{4,12},{5,13},{6,14},{7,15},{8,16},{9,17... | collective-permute-start | bytes 405512 | tf_op jit(solution)/shard_map/ppermute | solution.py:22
  24.6 10.2 %collective-permute-start.12 = (bf16[288,128]{1,0:T(8,128)(2,1)S(1)}, bf16[288,128]{1,0:T(8,128)(2,1)S(1)}, u32[]{:S(2)}, u32[]{:S(2)}) collective-permute-start(bf16[288,128]{1,0:T(8,128)(2,1)S(1)} %select_select_fusion.4), channel_id=1, source_target_pairs={{0,96},{1,97},{2,98},{3,99},{4,100},{5,101},{6,102},{7,103},{8,104... | collective-permute-start | bytes 221192 | tf_op jit(solution)/shard_map/ppermute | solution.py:22
  28.4 7.4 %collective-permute-start.11 = (bf16[288,128]{1,0:T(8,128)(2,1)S(1)}, bf16[288,128]{1,0:T(8,128)(2,1)S(1)}, u32[]{:S(2)}, u32[]{:S(2)}) collective-permute-start(bf16[288,128]{1,0:T(8,128)(2,1)S(1)} %select_select_fusion.4), channel_id=1, source_target_pairs={{0,64},{1,65},{2,66},{3,67},{4,68},{5,69},{6,70},{7,71},{8,72},{9,... | collective-permute-start | bytes 221192 | tf_op jit(solution)/shard_map/ppermute | solution.py:22
  29.4 6.4 %collective-permute-start.10 = (bf16[288,128]{1,0:T(8,128)(2,1)S(1)}, bf16[288,128]{1,0:T(8,128)(2,1)S(1)}, u32[]{:S(2)}, u32[]{:S(2)}) collective-permute-start(bf16[288,128]{1,0:T(8,128)(2,1)S(1)} %select_select_fusion.4), channel_id=1, source_target_pairs={{0,32},{1,33},{2,34},{3,35},{4,36},{5,37},{6,38},{7,39},{8,40},{9,... | collective-permute-start | bytes 221192 | tf_op jit(solution)/shard_map/ppermute | solution.py:22
  30.6 20.6 %collective-permute-start.16 = (bf16[1056,128]{1,0:T(8,128)(2,1)S(1)}, bf16[1056,128]{1,0:T(8,128)(2,1)S(1)}, u32[]{:S(2)}, u32[]{:S(2)}) collective-permute-start(bf16[1056,128]{1,0:T(8,128)(2,1)S(1)} %pad_maximum_fusion.m0), channel_id=1, source_target_pairs={{0,64},{1,65},{2,66},{3,67},{4,68},{5,69},{6,70},{7,71},{8,72},{9,... | collective-permute-start | bytes 811016 | tf_op jit(solution)/shard_map/ppermute | solution.py:22
  34.3 16.9 %collective-permute-start.15 = (bf16[1056,128]{1,0:T(8,128)(2,1)S(1)}, bf16[1056,128]{1,0:T(8,128)(2,1)S(1)}, u32[]{:S(2)}, u32[]{:S(2)}) collective-permute-start(bf16[1056,128]{1,0:T(8,128)(2,1)S(1)} %pad_maximum_fusion.m0), channel_id=1, source_target_pairs={{0,96},{1,97},{2,98},{3,99},{4,100},{5,101},{6,102},{7,103},{8,104... | collective-permute-start | bytes 811016 | tf_op jit(solution)/shard_map/ppermute | solution.py:22
  34.7 16.4 %collective-permute-start.14 = (bf16[1056,128]{1,0:T(8,128)(2,1)S(1)}, bf16[1056,128]{1,0:T(8,128)(2,1)S(1)}, u32[]{:S(2)}, u32[]{:S(2)}) collective-permute-start(bf16[1056,128]{1,0:T(8,128)(2,1)S(1)} %pad_maximum_fusion.m0), channel_id=1, source_target_pairs={{0,32},{1,33},{2,34},{3,35},{4,36},{5,37},{6,38},{7,39},{8,40},{9,... | collective-permute-start | bytes 811016 | tf_op jit(solution)/shard_map/ppermute | solution.py:22
  35.8 3.4 %collective-permute-start.13 = (bf16[288,128]{1,0:T(8,128)(2,1)S(1)}, bf16[288,128]{1,0:T(8,128)(2,1)S(1)}, u32[]{:S(2)}, u32[]{:S(2)}) collective-permute-start(bf16[288,128]{1,0:T(8,128)(2,1)S(1)} %select_select_fusion.3.pair_ref), channel_id=1, source_target_pairs={{0,4},{1,5},{2,6},{3,7},{4,0},{5,1},{6,2},{7,3},{8,12},{9,13},{10,... | collective-permute-start | bytes 221192 | tf_op jit(solution)/shard_map/ppermute | solution.py:22
  50.8 1.6 %collective-permute-start.17 = (bf16[1056,128]{1,0:T(8,128)(2,1)S(1)}, bf16[1056,128]{1,0:T(8,128)(2,1)S(1)}, u32[]{:S(2)}, u32[]{:S(2)}) collective-permute-start(bf16[1056,128]{1,0:T(8,128)(2,1)S(1)} %pad_maximum_fusion.m0), channel_id=1, source_target_pairs={{0,4},{1,5},{2,6},{3,7},{4,0},{5,1},{6,2},{7,3},{8,12},{9,13},{10,... | collective-permute-start | bytes 811016 | tf_op jit(solution)/shard_map/ppermute | solution.py:22
  51.2 1.6 %collective-permute-start.18 = (bf16[1056,128]{1,0:T(8,128)(2,1)S(1)}, bf16[1056,128]{1,0:T(8,128)(2,1)S(1)}, u32[]{:S(2)}, u32[]{:S(2)}) collective-permute-start(bf16[1056,128]{1,0:T(8,128)(2,1)S(1)} %collective-permute-done.14.m1), channel_id=1, source_target_pairs={{0,4},{1,5},{2,6},{3,7},{4,0},{5,1},{6,2},{7,3},{8,12},{9,13},{10,... | collective-permute-start | bytes 811016 | tf_op jit(solution)/shard_map/ppermute | solution.py:22
  51.4 1.8 %collective-permute-start.19 = (bf16[1056,128]{1,0:T(8,128)(2,1)S(1)}, bf16[1056,128]{1,0:T(8,128)(2,1)S(1)}, u32[]{:S(2)}, u32[]{:S(2)}) collective-permute-start(bf16[1056,128]{1,0:T(8,128)(2,1)S(1)} %collective-permute-done.15.m2), channel_id=1, source_target_pairs={{0,4},{1,5},{2,6},{3,7},{4,0},{5,1},{6,2},{7,3},{8,12},{9,13},{10,... | collective-permute-start | bytes 811016 | tf_op jit(solution)/shard_map/ppermute | solution.py:22
  51.8 1.8 %collective-permute-start.20 = (bf16[1056,128]{1,0:T(8,128)(2,1)S(1)}, bf16[1056,128]{1,0:T(8,128)(2,1)S(1)}, u32[]{:S(2)}, u32[]{:S(2)}) collective-permute-start(bf16[1056,128]{1,0:T(8,128)(2,1)S(1)} %collective-permute-done.16.m3), channel_id=1, source_target_pairs={{0,4},{1,5},{2,6},{3,7},{4,0},{5,1},{6,2},{7,3},{8,12},{9,13},{10,... | collective-permute-start | bytes 811016 | tf_op jit(solution)/shard_map/ppermute | solution.py:22
